TPU v7x, 512 devices: a whole 4x8x8 slice. The times are simulated.
512 devices in a mesh: fsdp: 128 (over y, z, core), rep: 4 (over x).
Axes of the slice: x: 4, y: 8, z: 8, core: 2. Of those that a mesh axis runs over, the one named last changes fastest.
Arguments:
- grads: bfloat16 [128, 1024, 1024], P(None, 'fsdp'), may hold values from -96 to 96
- owners: int32 [128], replicated, may hold values from 0 to 127, as said below
- counts: int32 [128], replicated, may hold values from 0 to 2, as said below
Outputs:
- preconditioned: bfloat16 [128, 1024, 1024], P(None, 'fsdp')
Inputs may be any that keep to these rules, and one draw needn't show every extreme that they name: `owners`: no owner is named by more than 2 entries, and some owner by exactly 2. counts[o] is the number of entries of owners equal to o, or one less; some owner named by 2 entries has counts equal to 2.
All inputs are finite; a program needn't handle non-finite values.
Results may differ from a plain program's by a relative error of at most 0.0068.
Values may be sent and summed in bfloat16 or wider, within the bound.
No kernel may reach another device: no remote copies, remote signals or barrier semaphores. Data moves between devices by JAX's collectives and lax.ppermute only.
A program may use at most 64 MiB of HBM per device.

v0:
```python
import jax
import jax.numpy as jnp
from jax import lax
from jax.sharding import PartitionSpec as P

CAP = 2


EPS = 1e-06


def block_places(owners, counts, groups):
    blocks = owners.shape[0]
    index = jnp.arange(blocks, dtype=jnp.int32)
    same = owners[:, None] == owners[None, :]
    earlier = index[None, :] < index[:, None]
    slot = jnp.sum((same & earlier).astype(jnp.int32), axis=1)
    have = jnp.sum(
        jnp.where(
            owners[:, None] == jnp.arange(groups, dtype=jnp.int32)[None, :], counts[None, :], 0
        ),
        axis=1,
    )
    valid = (slot < have).astype(jnp.float32)
    return (slot, valid)


def precondition(full, rank, quarter):
    width = full.shape[1]
    total_sq = jnp.sum(jnp.square(full.astype(jnp.float32)), axis=(1, 2))
    scale_c = total_sq / width + EPS
    root = scale_c ** (-0.25)
    start = rank * quarter
    eye_rows = (
        jnp.arange(quarter, dtype=jnp.int32)[:, None] + start
        == jnp.arange(width, dtype=jnp.int32)[None, :]
    ).astype(jnp.float32)
    own_rows = lax.dynamic_slice_in_dim(full, start, quarter, 1)
    own_cols = lax.dynamic_slice_in_dim(full, start, quarter, 2)
    left = jnp.einsum("kib,kjb->kij", own_rows, full, preferred_element_type=jnp.float32)
    right = jnp.einsum("kai,kaj->kij", full, own_cols, preferred_element_type=jnp.float32)
    factor = root[:, None, None]
    divisor = scale_c[:, None, None]
    x_left = (factor * (5.0 * eye_rows - (left + EPS * eye_rows) / divisor) / 4.0).astype(
        jnp.bfloat16
    )
    eye_cols = eye_rows.T
    x_right = (factor * (5.0 * eye_cols - (right + EPS * eye_cols) / divisor) / 4.0).astype(
        jnp.bfloat16
    )
    part_h = jnp.einsum("kij,kjb->kib", x_left, full, preferred_element_type=jnp.float32).astype(
        jnp.bfloat16
    )
    whole_h = lax.all_gather(part_h, "rep", axis=1, tiled=True)
    product = jnp.einsum("kij,kjq->kiq", whole_h, x_right, preferred_element_type=jnp.float32)
    product_sq = lax.psum(jnp.sum(product * product, axis=(1, 2)), "rep")
    graft = jnp.sqrt((total_sq + EPS) / (product_sq + EPS))
    return (product * graft[:, None, None]).astype(jnp.bfloat16)


def body(grads, owners, counts):
    blocks, rows_dev, width = grads.shape
    groups = lax.axis_size("fsdp")
    replicas = lax.axis_size("rep")
    rank = lax.axis_index("rep")
    quarter = width // replicas
    slots = CAP
    slot, valid = block_places(owners, counts, groups)
    target = slot * groups + owners
    match = target[None, :] == jnp.arange(slots * groups, dtype=jnp.int32)[:, None]
    table = match.astype(jnp.bfloat16)
    picker = (match.astype(jnp.float32).T * valid[:, None]).astype(jnp.bfloat16)
    flat = grads.reshape(blocks, rows_dev * width)
    outgoing = jnp.dot(table, flat, preferred_element_type=jnp.float32).astype(jnp.bfloat16)
    outgoing = outgoing.reshape(slots, groups, rows_dev, width)
    incoming = lax.all_to_all(outgoing, "fsdp", split_axis=1, concat_axis=1, tiled=True)
    items = incoming.shape[0]
    columns = precondition(incoming.reshape(items, width, width), rank, quarter)
    whole = lax.all_gather(columns, "rep", axis=2, tiled=True)
    back = lax.all_to_all(
        whole.reshape(slots, groups, rows_dev, width),
        "fsdp",
        split_axis=1,
        concat_axis=1,
        tiled=True,
    )
    placed = jnp.dot(
        picker, back.reshape(slots * groups, rows_dev * width), preferred_element_type=jnp.float32
    )
    result = placed.astype(jnp.bfloat16).reshape(blocks, rows_dev, width)
    return result


def solution(mesh):
    in_specs = (P(None, "fsdp", None), P(), P())
    out_specs = P(None, "fsdp", None)
    return jax.shard_map(body, mesh=mesh, in_specs=in_specs, out_specs=out_specs, check_vma=False)
```

profile of v0, /device:TPU:97, one launch (start us, length us, event | category | flops | bytes accessed | tf_op | source)
XLA Modules:
  0.0 418.0 jit_solution(11085103575785719748)
XLA Ops:
  6.5 0.9 select_reduce_fusion
  7.4 0.7 multiply_add_fusion.1
  8.1 3.0 copy.17
  11.1 1.2 convolution_convert_fusion
  12.3 4.3 %copy.18 = bf16[32,8,8,1024]{3,2,1,0:T(8,128)(2,1)S(1)} copy(bf16[32,8,8,1024]{3,1,2,0:T(8,128)(2,1)S(1)} %bitcast.21) | data formatting | bytes 8388608
  16.7 2.4 copy.11
  19.1 17.2 %all-to-all-start = ((bf16[2,128,8,1024]{3,2,0,1:T(8,128)(2,1)}), bf16[2,128,8,1024]{3,2,0,1:T(8,128)(2,1)}, u32[]{:S(2)}, u32[]{:S(2)}) async-start(bf16[2,128,8,1024]{3,2,0,1:T(8,128)(2,1)} %copy.11), calls=%async_computation | async-start | bytes 8388608 | tf_op jit(solution)/shard_map/all_to_all | solution.py:76
  36.3 0.2 all-gather.3.cloned.1.call-start
  36.5 0.2 fusion.5
  36.7 102.4 %all-to-all-done = bf16[2,128,8,1024]{3,2,0,1:T(8,128)(2,1)} async-done(((bf16[2,128,8,1024]{3,2,0,1:T(8,128)(2,1)}), bf16[2,128,8,1024]{3,2,0,1:T(8,128)(2,1)}, u32[]{:S(2)}, u32[]{:S(2)}) %all-to-all-start) | async-done | bytes 4194336 | tf_op jit(solution)/shard_map/all_to_all | solution.py:76
  139.1 3.4 multiply_reduce_fusion
  142.5 4.7 %copy.22 = bf16[2,128,8,1024]{3,2,1,0:T(8,128)(2,1)} copy(bf16[2,128,8,1024]{3,2,0,1:T(8,128)(2,1)} %all-to-all-done) | data formatting | bytes 8388608 | tf_op jit(solution)/shard_map/all_to_all | solution.py:76
  147.2 7.3 %convolution_convert_fusion.2 = bf16[2,256,1024]{2,1,0:T(8,128)(2,1)} fusion(bf16[2,1024,1024]{2,1,0:T(8,128)(2,1)} %bitcast.26, f32[2]{0:T(128)S(1)} %get-tuple-element.12, f32[256,1024]{1,0:T(8,128)S(1)} %get-tuple-element.10, s32[]{:T(128)S(6)} %select_n.9, f32[256,1024]{1,0:T(8,128)S(1)} %get-tuple-element.9, f32[2]{0:T(128)S(1)} %get-tuple-element.11), kind=kOutput, calls=%fused_computation.8 | convolution fusion | flops 2151153664 | bytes 12582932 | tf_op jit(solution)/shard_map/kij,kjb->kib/dot_general | solution.py:51
  154.4 0.0 all-gather.3.cloned.1.call-update
  154.5 0.0 all-gather.5.cloned.1.call-start
  154.5 1.2 fusion.2
  155.7 49.2 %all-gather.3.cloned.1.call-done = bf16[2,1024,1024]{2,1,0:T(8,128)(2,1)} async-done(((bf16[2,256,1024]{2,1,0:T(8,128)(2,1)}), bf16[2,1024,1024]{2,1,0:T(8,128)(2,1)}) %all-gather.3.cloned.1.call-update) | async-done | bytes 4194320 | tf_op jit(solution)/shard_map/all_gather | solution.py:54
  205.0 6.6 %multiply_reduce_fusion.1 = (f32[2]{0:T(128)S(1)}, f32[2,1024,256]{2,1,0:T(8,128)S(1)}) fusion(bf16[2,1024,1024]{2,1,0:T(8,128)(2,1)} %all-gather.3.cloned.1.call-done, bf16[2,1024,1024]{2,1,0:T(8,128)(2,1)} %bitcast.27, f32[2]{0:T(128)S(1)} %get-tuple-element.12, f32[1024,256]{1,0:T(8,128)} %get-tuple-element.8, s32[]{:T(128)S(6)} %select_n.9, ...), kind=kOutput, calls=%fused_computation.5 | convolution fusion | flops 2151677952 | bytes 13631516 | tf_op jit(solution)/shard_map/kij,kjq->kiq/dot_general | solution.py:55
  211.6 6.9 %psum.7 = f32[2]{0:T(128)S(1)} all-reduce(f32[2]{0:T(128)S(1)} %get-tuple-element.13), channel_id=1, replica_groups=mesh['fsdp'=128,'rep'=4] {'rep'}, use_global_device_ids=true, to_apply=%region_4.5 | all-reduce | flops 2 | bytes 16 | tf_op jit(solution)/shard_map/psum | solution.py:56
  218.5 1.2 multiply_convert_fusion
  219.7 0.0 all-gather.5.cloned.1.call-update
  219.8 57.8 %all-gather.5.cloned.1.call-done = bf16[2,1024,1024]{2,1,0:T(8,128)(2,1)} async-done(((bf16[2,1024,256]{2,1,0:T(8,128)(2,1)}), bf16[2,1024,1024]{2,1,0:T(8,128)(2,1)}) %all-gather.5.cloned.1.call-update) | async-done | bytes 4194320 | tf_op jit(solution)/shard_map/all_gather | solution.py:79
  277.6 4.8 %copy.14 = bf16[2,128,8,1024]{3,2,0,1:T(8,128)(2,1)} copy(bf16[2,128,8,1024]{3,2,1,0:T(8,128)(2,1)} %bitcast.28) | data formatting | bytes 8388608 | tf_op jit(solution)/shard_map/reshape | solution.py:81
  282.3 15.9 %all-to-all-start.1 = ((bf16[2,128,8,1024]{3,2,0,1:T(8,128)(2,1)}), bf16[2,128,8,1024]{3,2,0,1:T(8,128)(2,1)}, u32[]{:S(2)}, u32[]{:S(2)}) async-start(bf16[2,128,8,1024]{3,2,0,1:T(8,128)(2,1)} %copy.14), calls=%async_computation.1 | async-start | bytes 8388608 | tf_op jit(solution)/shard_map/all_to_all | solution.py:80
  298.3 102.4 %all-to-all-done.1 = bf16[2,128,8,1024]{3,2,0,1:T(8,128)(2,1)} async-done(((bf16[2,128,8,1024]{3,2,0,1:T(8,128)(2,1)}), bf16[2,128,8,1024]{3,2,0,1:T(8,128)(2,1)}, u32[]{:S(2)}, u32[]{:S(2)}) %all-to-all-start.1) | async-done | bytes 4194336 | tf_op jit(solution)/shard_map/all_to_all | solution.py:80
  400.7 2.6 copy.15
  403.3 4.3 %copy.19 = bf16[32,8,8,1024]{3,1,2,0:T(8,128)(2,1)S(1)} copy(bf16[32,8,8,1024]{3,2,1,0:T(8,128)(2,1)S(1)} %bitcast.23) | data formatting | bytes 8388608
  407.7 0.8 convolution_convert_fusion.1
  408.4 2.7 copy.20
  (4 shorter events, 0.0 us)
Async XLA Ops:
  19.1 120.0 %all-to-all-start = ((bf16[2,128,8,1024]{3,2,0,1:T(8,128)(2,1)}), bf16[2,128,8,1024]{3,2,0,1:T(8,128)(2,1)}, u32[]{:S(2)}, u32[]{:S(2)}) async-start(bf16[2,128,8,1024]{3,2,0,1:T(8,128)(2,1)} %copy.11), calls=%async_computation | async-start | bytes 8388608 | tf_op jit(solution)/shard_map/all_to_all | solution.py:76
  36.3 168.7 %all-gather.3.cloned.1.call-start = ((), (), s32[]{:S(2)}) async-start(), calls=%async_computation.2 | async-start | bytes 5242880 | tf_op jit(solution)/shard_map/all_gather | solution.py:54
  154.5 123.1 %all-gather.5.cloned.1.call-start = ((), (), s32[]{:S(2)}) async-start(), calls=%async_computation.3 | async-start | bytes 5242880 | tf_op jit(solution)/shard_map/all_gather | solution.py:79
  282.3 118.4 %all-to-all-start.1 = ((bf16[2,128,8,1024]{3,2,0,1:T(8,128)(2,1)}), bf16[2,128,8,1024]{3,2,0,1:T(8,128)(2,1)}, u32[]{:S(2)}, u32[]{:S(2)}) async-start(bf16[2,128,8,1024]{3,2,0,1:T(8,128)(2,1)} %copy.14), calls=%async_computation.1 | async-start | bytes 8388608 | tf_op jit(solution)/shard_map/all_to_all | solution.py:80
Sparse Core Ops, SparseCore 0:
  154.6 50.3 all-gather.2
  219.9 57.6 all-gather.4
where the time goes:
time: 419 us; the launch traced here: 418 us
  waiting for transfers between devices  312 us (74%)
  starting transfers between devices  33.4 us (8%)
  local copies, waits for them, and re-layouts  28.8 us (7%)
  matrix products  15.9 us (4%)
  between operations  13.5 us (3%)
  other arithmetic  7.61 us (2%)
  blocking collectives  6.88 us (2%)
    all_to_all x1, waiting for transfers between devices, body(): lax.all_to_all(whole.reshape(slots, groups, rows_dev, width), 'fsdp', spl...  102 us
    all_to_all x1, waiting for transfers between devices, body(): lax.all_to_all(outgoing, 'fsdp', split_axis=1, concat_axis=1, tiled=True)  102 us
    all_gather x1, waiting for transfers between devices, body(): whole = lax.all_gather(columns, 'rep', axis=2, tiled=True)  57.8 us
    all_gather x1, waiting for transfers between devices, precondition(): whole_h = lax.all_gather(part_h, 'rep', axis=1, tiled=True)  49.2 us
    all_to_all x1, starting transfers between devices, body(): lax.all_to_all(outgoing, 'fsdp', split_axis=1, concat_axis=1, tiled=True)  17.2 us
    all_to_all x1, starting transfers between devices, body(): lax.all_to_all(whole.reshape(slots, groups, rows_dev, width), 'fsdp', spl...  15.9 us
    unnamed x4, local copies, waits for them, and re-layouts  14.4 us
  transfers between devices with their start and end apart: 4, of which 4 were waited for; matrix products, arithmetic and copies ran while one was open for 0% of the time, Pallas kernels for 0%

commit v1 on v0

v1 whole, which is shorter than its diff:
```python
import jax
import jax.numpy as jnp
from jax import lax
from jax.experimental import pallas as pl
from jax.experimental.pallas import tpu as pltpu
from jax.sharding import Mesh
from jax.sharding import PartitionSpec as P

EPS = 1e-06
TILE = 256


def first_dims(a, b):
    return lax.dot_general(a, b, (((0,), (0,)), ((), ())), preferred_element_type=jnp.float32)


def refresh_kernel(block_ref, owners_ref, counts_ref, mine_ref, theirs_ref, out_ref, right, root_r, product):
    rows, width = mine_ref.shape
    places = lax.broadcasted_iota(jnp.int32, owners_ref.shape, 1)
    block = block_ref[0]
    owners = owners_ref[...]
    owner = jnp.sum(jnp.where(places == block, owners, 0))
    slot = jnp.sum(jnp.where((owners == owner) & (places < block), 1, 0))
    have = jnp.sum(jnp.where(places == owner, counts_ref[...], 0))
    valid = (slot < have).astype(jnp.float32)

    total_sq = jnp.zeros((1, 1), jnp.float32)
    for j in range(0, width, TILE):
        cols = pl.ds(j, TILE)
        tile = first_dims(mine_ref[...], mine_ref[:, cols]) + first_dims(theirs_ref[...], theirs_ref[:, cols])
        right[:, cols] = tile
        diag = right[cols, cols]
        r = lax.broadcasted_iota(jnp.int32, diag.shape, 0)
        c = lax.broadcasted_iota(jnp.int32, diag.shape, 1)
        total_sq += jnp.sum(jnp.where(r == c, diag, 0.0), keepdims=True)

    scale_c = total_sq / width + EPS
    quarter = lax.rsqrt(jnp.sqrt(scale_c)) * 0.25
    slope = quarter / scale_c
    for j in range(0, width, TILE):
        cols = pl.ds(j, TILE)
        tile = right[:, cols]
        r = lax.broadcasted_iota(jnp.int32, tile.shape, 0)
        c = lax.broadcasted_iota(jnp.int32, tile.shape, 1) + j
        diag = 5.0 * quarter - EPS * slope
        root_r[:, cols] = (jnp.where(r == c, diag, 0.0) - slope * tile).astype(jnp.bfloat16)

    product_sq = jnp.zeros((1, 1), jnp.float32)
    for ref, keep in ((mine_ref, True), (theirs_ref, False)):
        for i in range(0, rows, TILE):
            part = pl.ds(i, TILE)
            hidden = jnp.dot(ref[part, :], root_r[...], preferred_element_type=jnp.float32)
            done = jnp.dot(hidden.astype(jnp.bfloat16), root_r[...], preferred_element_type=jnp.float32)
            product_sq += jnp.sum(done * done, keepdims=True)
            if keep:
                product[part, :] = done
    graft = jnp.sqrt((total_sq + EPS) / (product_sq + EPS)) * valid
    out_ref[...] = (product[...] * graft).astype(jnp.bfloat16)


def refresh(block, owners, counts, mine, theirs):
    rows, width = mine.shape
    vmem = pl.BlockSpec(memory_space=pltpu.VMEM)
    return pl.pallas_call(
        refresh_kernel,
        out_shape=jax.ShapeDtypeStruct((rows, width), jnp.bfloat16),
        in_specs=[pl.BlockSpec(memory_space=pltpu.SMEM), vmem, vmem, vmem, vmem],
        out_specs=vmem,
        scratch_shapes=[
            pltpu.VMEM((width, width), jnp.float32),
            pltpu.VMEM((width, width), jnp.bfloat16),
            pltpu.VMEM((rows, width), jnp.float32),
        ],
        compiler_params=pltpu.CompilerParams(vmem_limit_bytes=40 * 2**20),
        cost_estimate=pl.CostEstimate(flops=6 * width**3, bytes_accessed=6 * rows * width, transcendentals=0),
    )(block, owners, counts, mine, theirs)


def body(grads, owners, counts):
    blocks, rows_dev, width = grads.shape
    chips = lax.axis_size("yz")
    planes = lax.axis_size("x")
    half = chips // 2
    side = lax.axis_index("x") % 2
    block = side * chips + lax.axis_index("yz")

    outgoing = lax.dynamic_slice_in_dim(grads, side * chips, chips, 0)
    mine = lax.all_to_all(outgoing, "yz", split_axis=0, concat_axis=0, tiled=True)
    mine = mine.reshape(chips * rows_dev, width)
    theirs = lax.ppermute(mine, "c", [(0, 1), (1, 0)])
    done = refresh(
        block.astype(jnp.int32).reshape(1), owners.reshape(1, -1), counts.reshape(1, -1), mine, theirs
    )
    back = lax.all_to_all(
        done.reshape(chips, rows_dev, width), "yz", split_axis=0, concat_axis=0, tiled=True
    )
    up = [(i, (i + 1) % planes) for i in range(planes)]
    down = [(i, (i - 1) % planes) for i in range(planes)]
    low = lax.ppermute(back[:half], "x", up)
    high = lax.ppermute(back[half:], "x", down)
    result = jnp.zeros((blocks, rows_dev, width), jnp.bfloat16)
    result = lax.dynamic_update_slice_in_dim(result, back, side * chips, 0)
    result = lax.dynamic_update_slice_in_dim(result, low, (1 - side) * chips, 0)
    return lax.dynamic_update_slice_in_dim(result, high, (1 - side) * chips + half, 0)


def solution(mesh):
    fine = Mesh(mesh.devices.reshape(64, 2, 4), ("yz", "c", "x"))
    rows = P(None, ("yz", "c"), None)
    return jax.shard_map(body, mesh=fine, in_specs=(rows, P(), P()), out_specs=rows, check_vma=False)
```

time: 419 us -> 119 us (0.28)
  the two profiles are of different devices: /device:TPU:97 before, /device:TPU:24 now
where the time goes in v1:
time: 119 us; the launch traced here: 118 us
  blocking collectives  82.1 us (69%)
  waiting for transfers between devices  11.5 us (10%)
  Pallas kernels  9.43 us (8%)
  starting transfers between devices  8.95 us (8%)
  local copies, waits for them, and re-layouts  6.47 us (5%)
    all_to_all x1, blocking collectives, body(): lax.all_to_all(outgoing, 'yz', split_axis=0, concat_axis=0, tiled=True)  45.9 us
    all_to_all x1, blocking collectives, body(): lax.all_to_all(done.reshape(chips, rows_dev, width), 'yz', split_axis=0,...  36.2 us
    pallas_call x1, Pallas kernels, refresh(): pl.pallas_call(refresh_kernel, out_shape=jax.ShapeDtypeStruct((rows, widt...  9.43 us
    ppermute x1, waiting for transfers between devices, body(): low = lax.ppermute(back[:half], 'x', up)  7.86 us
    ppermute x1, starting transfers between devices, body(): high = lax.ppermute(back[half:], 'x', down)  3.65 us
    ppermute x1, starting transfers between devices, body(): low = lax.ppermute(back[:half], 'x', up)  3.4 us
    ppermute x1, waiting for transfers between devices, body(): theirs = lax.ppermute(mine, 'c', [(0, 1), (1, 0)])  2.75 us
  transfers between devices with their start and end apart: 3, of which 3 were waited for; matrix products, arithmetic and copies ran while one was open for 1% of the time, Pallas kernels for 0%

profile of v1, /device:TPU:24, one launch (start us, length us, event | category | flops | bytes accessed | tf_op | source)
XLA Modules:
  0.0 118.5 jit_solution(7875633872239898548)
XLA Ops:
  0.0 0.0 copy-start
  0.0 1.6 %copy-done = bf16[128,8,1024]{2,1,0:T(8,128)(2,1)S(1)} copy-done((bf16[128,8,1024]{2,1,0:T(8,128)(2,1)S(1)}, bf16[128,8,1024]{2,1,0:T(8,128)(2,1)}, u32[]{:S(2)}) %copy-start) | copy-done | bytes 2097176
  1.6 0.0 copy-start.1
  1.6 0.0 copy-start.2
  1.6 0.1 constant_dynamic-slice_fusion
  1.7 45.9 %all_to_all.10 = bf16[64,8,1024]{2,1,0:T(8,128)(2,1)S(1)} all-to-all(bf16[64,8,1024]{2,1,0:T(8,128)(2,1)S(1)} %constant_dynamic-slice_fusion), channel_id=1, replica_groups=mesh['yz'=64,'c'=2,'x'=4] {'yz'}, dimensions={0} | all-to-all | bytes 2097152 | tf_op jit(solution)/shard_map/all_to_all | solution.py:88
  47.6 1.9 %collective-permute-start = (bf16[512,1024]{1,0:T(8,128)(2,1)S(1)}, bf16[512,1024]{1,0:T(8,128)(2,1)}, u32[]{:S(2)}, u32[]{:S(2)}) collective-permute-start(bf16[512,1024]{1,0:T(8,128)(2,1)S(1)} %bitcast.5), channel_id=1, source_target_pairs={{0,4},{4,0},{1,5},{5,1},{2,6},{6,2},{3,7},{7,3},{8,12},{12,8},{9,1... | collective-permute-start | bytes 3145736 | tf_op jit(solution)/shard_map/ppermute | solution.py:90
  49.5 2.7 %collective-permute-done.theirs_ref = bf16[512,1024]{1,0:T(8,128)(2,1)} collective-permute-done((bf16[512,1024]{1,0:T(8,128)(2,1)S(1)}, bf16[512,1024]{1,0:T(8,128)(2,1)}, u32[]{:S(2)}, u32[]{:S(2)}) %collective-permute-start) | collective-permute-done | bytes 1048608 | tf_op jit(solution)/shard_map/ppermute | solution.py:90
  52.2 0.0 copy-done.1
  52.2 0.0 copy-done.2
  52.3 9.4 %shard_map.37 = bf16[512,1024]{1,0:T(8,128)(2,1)S(1)} custom-call(s32[1]{0:T(128)} %bitcast.block_ref, s32[1,128]{1,0:T(1,128)S(1)} %bitcast.8, s32[1,128]{1,0:T(1,128)S(1)} %bitcast.9, bf16[512,1024]{1,0:T(8,128)(2,1)S(1)} %bitcast.6, bf16[512,1024]{1,0:T(8,128)(2,1)} %collective-permute-done.theirs_ref), custom_call_target="tpu_custom_call" | custom-call | flops 6442450944 | bytes 3145728 | tf_op jit(solution)/shard_map/pallas_call | solution.py:64
  61.7 36.2 %all_to_all.11 = bf16[64,8,1024]{2,1,0:T(8,128)(2,1)S(1)} all-to-all(bf16[64,8,1024]{2,1,0:T(8,128)(2,1)S(1)} %bitcast.7), channel_id=1, replica_groups=mesh['yz'=64,'c'=2,'x'=4] {'yz'}, dimensions={0} | all-to-all | bytes 2097152 | tf_op jit(solution)/shard_map/all_to_all | solution.py:94
  97.9 1.0 fusion
  98.9 3.4 %collective-permute-start.1 = (bf16[32,8,1024]{2,1,0:T(8,128)(2,1)}, bf16[32,8,1024]{2,1,0:T(8,128)(2,1)}, u32[]{:S(2)}, u32[]{:S(2)}) collective-permute-start(bf16[32,8,1024]{2,1,0:T(8,128)(2,1)} %get-tuple-element.6), channel_id=1, source_target_pairs={{0,1},{1,2},{2,3},{3,0},{4,5},{5,6},{6,7},{7,4},{8,9},{9,10},{10,1... | collective-permute-start | bytes 1572872 | tf_op jit(solution)/shard_map/ppermute | solution.py:99
  102.3 3.6 %collective-permute-start.2 = (bf16[32,8,1024]{2,1,0:T(8,128)(2,1)}, bf16[32,8,1024]{2,1,0:T(8,128)(2,1)}, u32[]{:S(2)}, u32[]{:S(2)}) collective-permute-start(bf16[32,8,1024]{2,1,0:T(8,128)(2,1)} %get-tuple-element.5), channel_id=1, source_target_pairs={{0,3},{1,0},{2,1},{3,2},{4,7},{5,4},{6,5},{7,6},{8,11},{9,8},{10,9... | collective-permute-start | bytes 1572872 | tf_op jit(solution)/shard_map/ppermute | solution.py:100
  106.0 0.3 broadcast_in_dim.3
  106.2 0.1 constant_dynamic-update-slice_fusion.2
  106.3 7.9 %collective-permute-done.1 = bf16[32,8,1024]{2,1,0:T(8,128)(2,1)} collective-permute-done((bf16[32,8,1024]{2,1,0:T(8,128)(2,1)}, bf16[32,8,1024]{2,1,0:T(8,128)(2,1)}, u32[]{:S(2)}, u32[]{:S(2)}) %collective-permute-start.1) | collective-permute-done | bytes 524320 | tf_op jit(solution)/shard_map/ppermute | solution.py:99
  114.2 1.1 constant_dynamic-update-slice_fusion.1
  115.3 0.0 copy-start.3
  115.3 0.8 collective-permute-done.2
  116.1 0.5 copy-done.3
  116.6 1.9 %constant_dynamic-update-slice_fusion = bf16[128,8,1024]{2,1,0:T(8,128)(2,1)} fusion(bf16[128,8,1024]{2,1,0:T(8,128)(2,1)} %copy-done.3, bf16[32,8,1024]{2,1,0:T(8,128)(2,1)} %collective-permute-done.2, s32[]{:T(128)S(6)} %select_n.20), kind=kLoop, calls=%fused_computation | loop fusion | bytes 1048580 | tf_op jit(solution)/shard_map/dynamic_update_slice | solution.py:104
Async XLA Ops:
  0.0 1.6 %copy-start = (bf16[128,8,1024]{2,1,0:T(8,128)(2,1)S(1)}, bf16[128,8,1024]{2,1,0:T(8,128)(2,1)}, u32[]{:S(2)}) copy-start(bf16[128,8,1024]{2,1,0:T(8,128)(2,1)} %param.3) | copy-start | bytes 6291460
  1.6 50.7 %copy-start.1 = (s32[128]{0:T(128)S(1)}, s32[128]{0:T(128)}, u32[]{:S(2)}) copy-start(s32[128]{0:T(128)} %param.4) | copy-start | bytes 1540
  1.6 50.7 %copy-start.2 = (s32[128]{0:T(128)S(1)}, s32[128]{0:T(128)}, u32[]{:S(2)}) copy-start(s32[128]{0:T(128)} %param.5) | copy-start | bytes 1540
  47.6 4.7 %collective-permute-start = (bf16[512,1024]{1,0:T(8,128)(2,1)S(1)}, bf16[512,1024]{1,0:T(8,128)(2,1)}, u32[]{:S(2)}, u32[]{:S(2)}) collective-permute-start(bf16[512,1024]{1,0:T(8,128)(2,1)S(1)} %bitcast.5), channel_id=1, source_target_pairs={{0,4},{4,0},{1,5},{5,1},{2,6},{6,2},{3,7},{7,3},{8,12},{12,8},{9,1... | collective-permute-start | bytes 3145736 | tf_op jit(solution)/shard_map/ppermute | solution.py:90
  98.9 15.3 %collective-permute-start.1 = (bf16[32,8,1024]{2,1,0:T(8,128)(2,1)}, bf16[32,8,1024]{2,1,0:T(8,128)(2,1)}, u32[]{:S(2)}, u32[]{:S(2)}) collective-permute-start(bf16[32,8,1024]{2,1,0:T(8,128)(2,1)} %get-tuple-element.6), channel_id=1, source_target_pairs={{0,1},{1,2},{2,3},{3,0},{4,5},{5,6},{6,7},{7,4},{8,9},{9,10},{10,1... | collective-permute-start | bytes 1572872 | tf_op jit(solution)/shard_map/ppermute | solution.py:99
  102.3 13.8 %collective-permute-start.2 = (bf16[32,8,1024]{2,1,0:T(8,128)(2,1)}, bf16[32,8,1024]{2,1,0:T(8,128)(2,1)}, u32[]{:S(2)}, u32[]{:S(2)}) collective-permute-start(bf16[32,8,1024]{2,1,0:T(8,128)(2,1)} %get-tuple-element.5), channel_id=1, source_target_pairs={{0,3},{1,0},{2,1},{3,2},{4,7},{5,4},{6,5},{7,6},{8,11},{9,8},{10,9... | collective-permute-start | bytes 1572872 | tf_op jit(solution)/shard_map/ppermute | solution.py:100
  115.3 1.3 %copy-start.3 = (bf16[128,8,1024]{2,1,0:T(8,128)(2,1)}, bf16[128,8,1024]{2,1,0:T(8,128)(2,1)S(1)}, u32[]{:S(2)}) copy-start(bf16[128,8,1024]{2,1,0:T(8,128)(2,1)S(1)} %constant_dynamic-update-slice_fusion.1) | copy-start | bytes 6291460

commit v2 on v1

v2 whole, which is shorter than its diff:
```python
import jax
import jax.numpy as jnp
from jax import lax
from jax.experimental import pallas as pl
from jax.experimental.pallas import tpu as pltpu
from jax.sharding import Mesh
from jax.sharding import PartitionSpec as P

EPS = 1e-06
TILE = 256


def first_dims(a, b):
    return lax.dot_general(a, b, (((0,), (0,)), ((), ())), preferred_element_type=jnp.float32)


def gram_kernel(rows_ref, out_ref):
    width = rows_ref.shape[1]
    for j in range(0, width, TILE):
        out_ref[j:, j : j + TILE] = first_dims(rows_ref[:, j:], rows_ref[:, j : j + TILE])


def gram(rows):
    count, width = rows.shape
    vmem = pl.BlockSpec(memory_space=pltpu.VMEM)
    return pl.pallas_call(
        gram_kernel,
        out_shape=jax.ShapeDtypeStruct((width, width), jnp.float32),
        in_specs=[vmem],
        out_specs=vmem,
        compiler_params=pltpu.CompilerParams(vmem_limit_bytes=24 * 2**20),
        cost_estimate=pl.CostEstimate(
            flops=2 * count * width**2, bytes_accessed=2 * count * width + 4 * width**2, transcendentals=0
        ),
    )(rows)


def on_diagonal(tile):
    r = lax.broadcasted_iota(jnp.int32, tile.shape, 0)
    c = lax.broadcasted_iota(jnp.int32, tile.shape, 1)
    return r == c


def refresh_kernel(
    block_ref, owners_ref, counts_ref, mine_ref, theirs_ref, gram_ref, out_ref, right, root_r, rest, product
):
    rows, width = mine_ref.shape
    places = lax.broadcasted_iota(jnp.int32, owners_ref.shape, 1)
    block = block_ref[0]
    owners = owners_ref[...]
    owner = jnp.sum(jnp.where(places == block, owners, 0))
    slot = jnp.sum(jnp.where((owners == owner) & (places < block), 1, 0))
    have = jnp.sum(jnp.where(places == owner, counts_ref[...], 0))
    valid = (slot < have).astype(jnp.float32)

    total_sq = jnp.zeros((1, 1), jnp.float32)
    for j in range(0, width, TILE):
        tile = gram_ref[j:, j : j + TILE] + first_dims(theirs_ref[:, j:], theirs_ref[:, j : j + TILE])
        right[j:, j : j + TILE] = tile
        top = tile[:TILE, :]
        total_sq += jnp.sum(jnp.where(on_diagonal(top), top, 0.0), keepdims=True)

    scale_c = total_sq / width + EPS
    quarter = lax.rsqrt(jnp.sqrt(scale_c)) * 0.25
    slope = quarter / scale_c
    diag = 5.0 * quarter - EPS * slope
    for j in range(0, width, TILE):
        cols = slice(j, j + TILE)
        tile = -slope * right[cols, cols]
        tile = jnp.where(on_diagonal(tile), diag + tile, tile)
        kept = tile.astype(jnp.bfloat16)
        root_r[cols, cols] = kept
        off = jnp.where(on_diagonal(tile), tile - kept.astype(jnp.float32), 0.0)
        rest[:, cols] = 2.0 * jnp.sum(off, axis=0, keepdims=True)
        if j + TILE < width:
            below = (-slope * right[j + TILE :, cols]).astype(jnp.bfloat16)
            root_r[j + TILE :, cols] = below
            root_r[cols, j + TILE :] = below.T

    product_sq = jnp.zeros((1, 1), jnp.float32)
    for ref, keep in ((mine_ref, True), (theirs_ref, False)):
        for i in range(0, rows, TILE):
            hidden = jnp.dot(ref[i : i + TILE, :], root_r[...], preferred_element_type=jnp.float32)
            done = jnp.dot(hidden.astype(jnp.bfloat16), root_r[...], preferred_element_type=jnp.float32)
            done = done + hidden * rest[...]
            product_sq += jnp.sum(done * done, keepdims=True)
            if keep:
                product[i : i + TILE, :] = done
    graft = jnp.sqrt((total_sq + EPS) / (product_sq + EPS)) * valid
    out_ref[...] = (product[...] * graft).astype(jnp.bfloat16)


def refresh(block, owners, counts, mine, theirs, mine_gram):
    rows, width = mine.shape
    vmem = pl.BlockSpec(memory_space=pltpu.VMEM)
    return pl.pallas_call(
        refresh_kernel,
        out_shape=jax.ShapeDtypeStruct((rows, width), jnp.bfloat16),
        in_specs=[pl.BlockSpec(memory_space=pltpu.SMEM), vmem, vmem, vmem, vmem, vmem],
        out_specs=vmem,
        scratch_shapes=[
            pltpu.VMEM((width, width), jnp.float32),
            pltpu.VMEM((width, width), jnp.bfloat16),
            pltpu.VMEM((1, width), jnp.float32),
            pltpu.VMEM((rows, width), jnp.float32),
        ],
        compiler_params=pltpu.CompilerParams(vmem_limit_bytes=40 * 2**20),
        cost_estimate=pl.CostEstimate(flops=5 * width**3, bytes_accessed=6 * rows * width, transcendentals=0),
    )(block, owners, counts, mine, theirs, mine_gram)


def place_own_kernel(side_ref, own_ref, out_ref, sem):
    half = own_ref.shape[0]
    copy = pltpu.make_async_copy(own_ref, out_ref.at[pl.ds(side_ref[0] * half, half)], sem)
    copy.start()
    copy.wait()


def place_own(side, own, blocks):
    any_space = pl.BlockSpec(memory_space=pl.ANY)
    return pl.pallas_call(
        place_own_kernel,
        out_shape=jax.ShapeDtypeStruct((blocks,) + own.shape[1:], own.dtype),
        in_specs=[pl.BlockSpec(memory_space=pltpu.SMEM), any_space],
        out_specs=pl.BlockSpec(memory_space=pltpu.HBM),
        scratch_shapes=[pltpu.SemaphoreType.DMA],
        cost_estimate=pl.CostEstimate(flops=0, bytes_accessed=4 * own.size, transcendentals=0),
    )(side, own)


def place_others_kernel(side_ref, held_ref, low_ref, high_ref, out_ref, low_sem, high_sem):
    part = low_ref.shape[0]
    start = (1 - side_ref[0]) * (2 * part)
    low = pltpu.make_async_copy(low_ref, out_ref.at[pl.ds(start, part)], low_sem)
    high = pltpu.make_async_copy(high_ref, out_ref.at[pl.ds(start + part, part)], high_sem)
    low.start()
    high.start()
    low.wait()
    high.wait()


def place_others(side, held, low, high):
    any_space = pl.BlockSpec(memory_space=pl.ANY)
    hbm = pl.BlockSpec(memory_space=pltpu.HBM)
    return pl.pallas_call(
        place_others_kernel,
        out_shape=jax.ShapeDtypeStruct(held.shape, held.dtype),
        in_specs=[pl.BlockSpec(memory_space=pltpu.SMEM), hbm, any_space, any_space],
        out_specs=hbm,
        scratch_shapes=[pltpu.SemaphoreType.DMA, pltpu.SemaphoreType.DMA],
        input_output_aliases={1: 0},
        cost_estimate=pl.CostEstimate(flops=0, bytes_accessed=8 * low.size, transcendentals=0),
    )(side, held, low, high)


def body(grads, owners, counts):
    blocks, rows_dev, width = grads.shape
    chips = lax.axis_size("yz")
    planes = lax.axis_size("x")
    half = chips // 2
    side = (lax.axis_index("x") % 2).astype(jnp.int32)
    block = side * chips + lax.axis_index("yz").astype(jnp.int32)
    side_ref = side.reshape(1)

    outgoing = lax.dynamic_slice_in_dim(grads, side * chips, chips, 0)
    mine = lax.all_to_all(outgoing, "yz", split_axis=0, concat_axis=0, tiled=True)
    mine = mine.reshape(chips * rows_dev, width)
    theirs = lax.ppermute(mine, "c", [(0, 1), (1, 0)])
    done = refresh(
        block.reshape(1), owners.reshape(1, -1), counts.reshape(1, -1), mine, theirs, gram(mine)
    )
    back = lax.all_to_all(
        done.reshape(chips, rows_dev, width), "yz", split_axis=0, concat_axis=0, tiled=True
    )
    up = [(i, (i + 1) % planes) for i in range(planes)]
    down = [(i, (i - 1) % planes) for i in range(planes)]
    low = lax.ppermute(back[:half], "x", up)
    high = lax.ppermute(back[half:], "x", down)
    held = place_own(side_ref, back, blocks)
    return place_others(side_ref, held, low, high)


def solution(mesh):
    fine = Mesh(mesh.devices.reshape(64, 2, 4), ("yz", "c", "x"))
    rows = P(None, ("yz", "c"), None)
    return jax.shard_map(body, mesh=fine, in_specs=(rows, P(), P()), out_specs=rows, check_vma=False)
```

time: 119 us -> 171 us (1.44)
  the two profiles are of different devices: /device:TPU:24 before, /device:TPU:22 now
where the time goes in v2:
time: 171 us
  blocking collectives  82.8 us (48%)
  Pallas kernels  74.6 us (44%)
  starting transfers between devices  8.95 us (5%)
  local copies, waits for them, and re-layouts  2.8 us (2%)
  waiting for transfers between devices  1.83 us (1%)
    all_to_all x1, blocking collectives, body(): lax.all_to_all(outgoing, 'yz', split_axis=0, concat_axis=0, tiled=True)  46.8 us
    all_to_all x1, blocking collectives, body(): lax.all_to_all(done.reshape(chips, rows_dev, width), 'yz', split_axis=0,...  36 us
    pallas_call x1, Pallas kernels, place_others(): pl.pallas_call(place_others_kernel, out_shape=jax.ShapeDtypeStruct(held.s...  32.9 us
    pallas_call x1, Pallas kernels, place_own(): pl.pallas_call(place_own_kernel, out_shape=jax.ShapeDtypeStruct((blocks,)...  32.9 us
    pallas_call x1, Pallas kernels, refresh(): pl.pallas_call(refresh_kernel, out_shape=jax.ShapeDtypeStruct((rows, widt...  7.93 us
    ppermute x1, starting transfers between devices, body(): low = lax.ppermute(back[:half], 'x', up)  4.35 us
  transfers between devices with their start and end apart: 3, of which 1 were waited for; matrix products, arithmetic and copies ran while one was open for 0% of the time, Pallas kernels for 20%

profile of v2, /device:TPU:22, one launch (start us, length us, event | category | flops | bytes accessed | tf_op | source)
XLA Modules:
  0.0 171.1 jit_solution(7081869435329432497)
XLA Ops:
  0.0 0.0 copy-start
  0.0 1.6 copy-done
  1.6 0.1 constant_dynamic-slice_fusion
  1.7 46.8 %all_to_all.10 = bf16[64,8,1024]{2,1,0:T(8,128)(2,1)S(1)} all-to-all(bf16[64,8,1024]{2,1,0:T(8,128)(2,1)S(1)} %constant_dynamic-slice_fusion), channel_id=1, replica_groups=mesh['yz'=64,'c'=2,'x'=4] {'yz'}, dimensions={0} | all-to-all | bytes 2097152 | tf_op jit(solution)/shard_map/all_to_all | solution.py:166
  48.4 1.9 %collective-permute-start = (bf16[512,1024]{1,0:T(8,128)(2,1)S(1)}, bf16[512,1024]{1,0:T(8,128)(2,1)}, u32[]{:S(2)}, u32[]{:S(2)}) collective-permute-start(bf16[512,1024]{1,0:T(8,128)(2,1)S(1)} %bitcast.6), channel_id=1, source_target_pairs={{0,4},{4,0},{1,5},{5,1},{2,6},{6,2},{3,7},{7,3},{8,12},{12,8},{9,1... | collective-permute-start | bytes 3145736 | tf_op jit(solution)/shard_map/ppermute | solution.py:168
  50.4 0.0 copy-start.1
  50.4 0.0 copy-start.2
  50.4 0.9 shard_map.37.gram_ref
  51.3 1.8 %collective-permute-done.theirs_ref = bf16[512,1024]{1,0:T(8,128)(2,1)} collective-permute-done((bf16[512,1024]{1,0:T(8,128)(2,1)S(1)}, bf16[512,1024]{1,0:T(8,128)(2,1)}, u32[]{:S(2)}, u32[]{:S(2)}) %collective-permute-start) | collective-permute-done | bytes 1048608 | tf_op jit(solution)/shard_map/ppermute | solution.py:168
  53.1 0.0 copy-done.1
  53.1 0.0 copy-done.2
  53.1 7.9 %shard_map.38 = bf16[512,1024]{1,0:T(8,128)(2,1)S(1)} custom-call(s32[1]{0:T(128)} %bitcast.1.block_ref, s32[1,128]{1,0:T(1,128)S(1)} %bitcast.10, s32[1,128]{1,0:T(1,128)S(1)} %bitcast.11, bf16[512,1024]{1,0:T(8,128)(2,1)S(1)} %bitcast.8, bf16[512,1024]{1,0:T(8,128)(2,1)} %collective-permute-done.theirs_ref, f32[1024,1024]{1,0:T(8,128)S(1)} %shard_map.37.gram_ref), custom_call_target="tpu_custom_call" | custom-call | flops 5368709120 | bytes 3145728 | tf_op jit(solution)/shard_map/pallas_call | solution.py:96
  61.1 36.0 %all_to_all.11.own_ref = bf16[64,8,1024]{2,1,0:T(8,128)(2,1)S(1)} all-to-all(bf16[64,8,1024]{2,1,0:T(8,128)(2,1)S(1)} %bitcast.9), channel_id=1, replica_groups=mesh['yz'=64,'c'=2,'x'=4] {'yz'}, dimensions={0} | all-to-all | bytes 2097152 | tf_op jit(solution)/shard_map/all_to_all | solution.py:172
  97.1 0.0 copy-start.3
  97.1 1.1 fusion
  98.2 2.7 %collective-permute-start.2 = (bf16[32,8,1024]{2,1,0:T(8,128)(2,1)}, bf16[32,8,1024]{2,1,0:T(8,128)(2,1)}, u32[]{:S(2)}, u32[]{:S(2)}) collective-permute-start(bf16[32,8,1024]{2,1,0:T(8,128)(2,1)} %get-tuple-element.5), channel_id=1, source_target_pairs={{0,3},{1,0},{2,1},{3,2},{4,7},{5,4},{6,5},{7,6},{8,11},{9,8},{10,9... | collective-permute-start | bytes 1572872 | tf_op jit(solution)/shard_map/ppermute | solution.py:178
  100.9 4.3 %collective-permute-start.1 = (bf16[32,8,1024]{2,1,0:T(8,128)(2,1)}, bf16[32,8,1024]{2,1,0:T(8,128)(2,1)}, u32[]{:S(2)}, u32[]{:S(2)}) collective-permute-start(bf16[32,8,1024]{2,1,0:T(8,128)(2,1)} %get-tuple-element.6), channel_id=1, source_target_pairs={{0,1},{1,2},{2,3},{3,0},{4,5},{5,6},{6,7},{7,4},{8,9},{9,10},{10,1... | collective-permute-start | bytes 1572872 | tf_op jit(solution)/shard_map/ppermute | solution.py:177
  105.2 0.0 copy-done.3
  105.3 32.9 %shard_map.39.held_ref = bf16[128,8,1024]{2,1,0:T(8,128)(2,1)} custom-call(s32[1]{0:T(128)} %bitcast.side_ref, bf16[64,8,1024]{2,1,0:T(8,128)(2,1)} %copy-done.3), custom_call_target="tpu_custom_call" | custom-call | bytes 2097152 | tf_op jit(solution)/shard_map/pallas_call | solution.py:121
  138.1 0.0 collective-permute-done.2.high_ref
  138.2 0.0 collective-permute-done.1.low_ref
  138.2 32.9 %shard_map.40 = bf16[128,8,1024]{2,1,0:T(8,128)(2,1)} custom-call(s32[1]{0:T(128)} %bitcast.side_ref, bf16[128,8,1024]{2,1,0:T(8,128)(2,1)} %shard_map.39.held_ref, bf16[32,8,1024]{2,1,0:T(8,128)(2,1)} %collective-permute-done.1.low_ref, bf16[32,8,1024]{2,1,0:T(8,128)(2,1)} %collective-permute-done.2.high_ref), custom_call_target="tpu_custom_call", output_to_operand_aliasing={{}: (1, {})} | custom-call | bytes 2097152 | tf_op jit(solution)/shard_map/pallas_call | solution.py:145
Async XLA Ops:
  0.0 1.6 copy-start
  48.4 4.7 %collective-permute-start = (bf16[512,1024]{1,0:T(8,128)(2,1)S(1)}, bf16[512,1024]{1,0:T(8,128)(2,1)}, u32[]{:S(2)}, u32[]{:S(2)}) collective-permute-start(bf16[512,1024]{1,0:T(8,128)(2,1)S(1)} %bitcast.6), channel_id=1, source_target_pairs={{0,4},{4,0},{1,5},{5,1},{2,6},{6,2},{3,7},{7,3},{8,12},{12,8},{9,1... | collective-permute-start | bytes 3145736 | tf_op jit(solution)/shard_map/ppermute | solution.py:168
  50.4 2.8 %copy-start.1 = (s32[128]{0:T(128)S(1)}, s32[128]{0:T(128)}, u32[]{:S(2)}) copy-start(s32[128]{0:T(128)} %param.4) | copy-start | bytes 1540
  50.4 2.7 %copy-start.2 = (s32[128]{0:T(128)S(1)}, s32[128]{0:T(128)}, u32[]{:S(2)}) copy-start(s32[128]{0:T(128)} %param.5) | copy-start | bytes 1540
  97.1 8.2 %copy-start.3 = (bf16[64,8,1024]{2,1,0:T(8,128)(2,1)}, bf16[64,8,1024]{2,1,0:T(8,128)(2,1)S(1)}, u32[]{:S(2)}) copy-start(bf16[64,8,1024]{2,1,0:T(8,128)(2,1)S(1)} %all_to_all.11.own_ref) | copy-start | bytes 3145732
  98.2 40.0 %collective-permute-start.2 = (bf16[32,8,1024]{2,1,0:T(8,128)(2,1)}, bf16[32,8,1024]{2,1,0:T(8,128)(2,1)}, u32[]{:S(2)}, u32[]{:S(2)}) collective-permute-start(bf16[32,8,1024]{2,1,0:T(8,128)(2,1)} %get-tuple-element.5), channel_id=1, source_target_pairs={{0,3},{1,0},{2,1},{3,2},{4,7},{5,4},{6,5},{7,6},{8,11},{9,8},{10,9... | collective-permute-start | bytes 1572872 | tf_op jit(solution)/shard_map/ppermute | solution.py:178
  100.9 37.3 %collective-permute-start.1 = (bf16[32,8,1024]{2,1,0:T(8,128)(2,1)}, bf16[32,8,1024]{2,1,0:T(8,128)(2,1)}, u32[]{:S(2)}, u32[]{:S(2)}) collective-permute-start(bf16[32,8,1024]{2,1,0:T(8,128)(2,1)} %get-tuple-element.6), channel_id=1, source_target_pairs={{0,1},{1,2},{2,3},{3,0},{4,5},{5,6},{6,7},{7,4},{8,9},{9,10},{10,1... | collective-permute-start | bytes 1572872 | tf_op jit(solution)/shard_map/ppermute | solution.py:177

commit v3 on v2

--- a/solution.py
+++ b/solution.py
@@ -117,11 +117,11 @@
 
 
 def place_own(side, own, blocks):
-    any_space = pl.BlockSpec(memory_space=pl.ANY)
+    vmem = pl.BlockSpec(memory_space=pltpu.VMEM)
     return pl.pallas_call(
         place_own_kernel,
         out_shape=jax.ShapeDtypeStruct((blocks,) + own.shape[1:], own.dtype),
-        in_specs=[pl.BlockSpec(memory_space=pltpu.SMEM), any_space],
+        in_specs=[pl.BlockSpec(memory_space=pltpu.SMEM), vmem],
         out_specs=pl.BlockSpec(memory_space=pltpu.HBM),
         scratch_shapes=[pltpu.SemaphoreType.DMA],
         cost_estimate=pl.CostEstimate(flops=0, bytes_accessed=4 * own.size, transcendentals=0),
@@ -140,12 +140,12 @@
 
 
 def place_others(side, held, low, high):
-    any_space = pl.BlockSpec(memory_space=pl.ANY)
+    vmem = pl.BlockSpec(memory_space=pltpu.VMEM)
     hbm = pl.BlockSpec(memory_space=pltpu.HBM)
     return pl.pallas_call(
         place_others_kernel,
         out_shape=jax.ShapeDtypeStruct(held.shape, held.dtype),
-        in_specs=[pl.BlockSpec(memory_space=pltpu.SMEM), hbm, any_space, any_space],
+        in_specs=[pl.BlockSpec(memory_space=pltpu.SMEM), hbm, vmem, vmem],
         out_specs=hbm,
         scratch_shapes=[pltpu.SemaphoreType.DMA, pltpu.SemaphoreType.DMA],
         input_output_aliases={1: 0},

time: 171 us -> 120 us (0.70)
  the two profiles are of different devices: /device:TPU:22 before, /device:TPU:24 now
where the time goes in v3:
time: 120 us; the launch traced here: 119 us
  blocking collectives  82.1 us (68%)
  Pallas kernels  13.2 us (11%)
  waiting for transfers between devices  12.7 us (11%)
  starting transfers between devices  8.49 us (7%)
  local copies, waits for them, and re-layouts  2.8 us (2%)
    all_to_all x1, blocking collectives, body(): lax.all_to_all(outgoing, 'yz', split_axis=0, concat_axis=0, tiled=True)  45.9 us
    all_to_all x1, blocking collectives, body(): lax.all_to_all(done.reshape(chips, rows_dev, width), 'yz', split_axis=0,...  36.2 us
    pallas_call x1, Pallas kernels, refresh(): pl.pallas_call(refresh_kernel, out_shape=jax.ShapeDtypeStruct((rows, widt...  7.93 us
    ppermute x1, waiting for transfers between devices, body(): high = lax.ppermute(back[half:], 'x', down)  5.51 us
    ppermute x1, waiting for transfers between devices, body(): low = lax.ppermute(back[:half], 'x', up)  5.33 us
    ppermute x1, starting transfers between devices, body(): high = lax.ppermute(back[half:], 'x', down)  4.66 us
  transfers between devices with their start and end apart: 3, of which 3 were waited for; matrix products, arithmetic and copies ran while one was open for 0% of the time, Pallas kernels for 3%

profile of v3, /device:TPU:24, one launch (start us, length us, event | category | flops | bytes accessed | tf_op | source)
XLA Modules:
  0.0 119.3 jit_solution(18253286843363780162)
XLA Ops:
  0.0 0.0 copy-start
  0.0 1.6 %copy-done = bf16[128,8,1024]{2,1,0:T(8,128)(2,1)S(1)} copy-done((bf16[128,8,1024]{2,1,0:T(8,128)(2,1)S(1)}, bf16[128,8,1024]{2,1,0:T(8,128)(2,1)}, u32[]{:S(2)}) %copy-start) | copy-done | bytes 2097176
  1.6 0.1 constant_dynamic-slice_fusion
  1.7 45.9 %all_to_all.10 = bf16[64,8,1024]{2,1,0:T(8,128)(2,1)S(1)} all-to-all(bf16[64,8,1024]{2,1,0:T(8,128)(2,1)S(1)} %constant_dynamic-slice_fusion), channel_id=1, replica_groups=mesh['yz'=64,'c'=2,'x'=4] {'yz'}, dimensions={0} | all-to-all | bytes 2097152 | tf_op jit(solution)/shard_map/all_to_all | solution.py:166
  47.6 1.9 %collective-permute-start = (bf16[512,1024]{1,0:T(8,128)(2,1)S(1)}, bf16[512,1024]{1,0:T(8,128)(2,1)}, u32[]{:S(2)}, u32[]{:S(2)}) collective-permute-start(bf16[512,1024]{1,0:T(8,128)(2,1)S(1)} %bitcast.6), channel_id=1, source_target_pairs={{0,4},{4,0},{1,5},{5,1},{2,6},{6,2},{3,7},{7,3},{8,12},{12,8},{9,1... | collective-permute-start | bytes 3145736 | tf_op jit(solution)/shard_map/ppermute | solution.py:168
  49.5 0.0 copy-start.1
  49.5 0.0 copy-start.2
  49.5 0.9 shard_map.37.gram_ref
  50.4 1.8 %collective-permute-done.theirs_ref = bf16[512,1024]{1,0:T(8,128)(2,1)} collective-permute-done((bf16[512,1024]{1,0:T(8,128)(2,1)S(1)}, bf16[512,1024]{1,0:T(8,128)(2,1)}, u32[]{:S(2)}, u32[]{:S(2)}) %collective-permute-start) | collective-permute-done | bytes 1048608 | tf_op jit(solution)/shard_map/ppermute | solution.py:168
  52.2 0.0 copy-done.1
  52.2 0.0 copy-done.2
  52.2 7.9 %shard_map.38 = bf16[512,1024]{1,0:T(8,128)(2,1)S(1)} custom-call(s32[1]{0:T(128)} %bitcast.1.block_ref, s32[1,128]{1,0:T(1,128)S(1)} %bitcast.10, s32[1,128]{1,0:T(1,128)S(1)} %bitcast.11, bf16[512,1024]{1,0:T(8,128)(2,1)S(1)} %bitcast.8, bf16[512,1024]{1,0:T(8,128)(2,1)} %collective-permute-done.theirs_ref, f32[1024,1024]{1,0:T(8,128)S(1)} %shard_map.37.gram_ref), custom_call_target="tpu_custom_call" | custom-call | flops 5368709120 | bytes 3145728 | tf_op jit(solution)/shard_map/pallas_call | solution.py:96
  60.2 36.2 %all_to_all.11.own_ref = bf16[64,8,1024]{2,1,0:T(8,128)(2,1)S(1)} all-to-all(bf16[64,8,1024]{2,1,0:T(8,128)(2,1)S(1)} %bitcast.9), channel_id=1, replica_groups=mesh['yz'=64,'c'=2,'x'=4] {'yz'}, dimensions={0} | all-to-all | bytes 2097152 | tf_op jit(solution)/shard_map/all_to_all | solution.py:172
  96.4 0.0 copy-start.3
  96.4 1.1 fusion
  97.5 4.7 %collective-permute-start.2 = (bf16[32,8,1024]{2,1,0:T(8,128)(2,1)}, bf16[32,8,1024]{2,1,0:T(8,128)(2,1)}, u32[]{:S(2)}, u32[]{:S(2)}) collective-permute-start(bf16[32,8,1024]{2,1,0:T(8,128)(2,1)} %get-tuple-element.5), channel_id=1, source_target_pairs={{0,3},{1,0},{2,1},{3,2},{4,7},{5,4},{6,5},{7,6},{8,11},{9,8},{10,9... | collective-permute-start | bytes 1572872 | tf_op jit(solution)/shard_map/ppermute | solution.py:178
  102.2 1.9 %collective-permute-start.1 = (bf16[32,8,1024]{2,1,0:T(8,128)(2,1)}, bf16[32,8,1024]{2,1,0:T(8,128)(2,1)}, u32[]{:S(2)}, u32[]{:S(2)}) collective-permute-start(bf16[32,8,1024]{2,1,0:T(8,128)(2,1)} %get-tuple-element.6), channel_id=1, source_target_pairs={{0,1},{1,2},{2,3},{3,0},{4,5},{5,6},{6,7},{7,4},{8,9},{9,10},{10,1... | collective-permute-start | bytes 1572872 | tf_op jit(solution)/shard_map/ppermute | solution.py:177
  104.1 0.0 copy-done.3
  104.1 2.2 %shard_map.39.held_ref = bf16[128,8,1024]{2,1,0:T(8,128)(2,1)} custom-call(s32[1]{0:T(128)} %bitcast.side_ref, bf16[64,8,1024]{2,1,0:T(8,128)(2,1)} %copy-done.3), custom_call_target="tpu_custom_call" | custom-call | bytes 2097152 | tf_op jit(solution)/shard_map/pallas_call | solution.py:121
  106.3 5.5 %collective-permute-done.2.high_ref = bf16[32,8,1024]{2,1,0:T(8,128)(2,1)} collective-permute-done((bf16[32,8,1024]{2,1,0:T(8,128)(2,1)}, bf16[32,8,1024]{2,1,0:T(8,128)(2,1)}, u32[]{:S(2)}, u32[]{:S(2)}) %collective-permute-start.2) | collective-permute-done | bytes 524320 | tf_op jit(solution)/shard_map/ppermute | solution.py:178
  111.8 5.3 %collective-permute-done.1.low_ref = bf16[32,8,1024]{2,1,0:T(8,128)(2,1)} collective-permute-done((bf16[32,8,1024]{2,1,0:T(8,128)(2,1)}, bf16[32,8,1024]{2,1,0:T(8,128)(2,1)}, u32[]{:S(2)}, u32[]{:S(2)}) %collective-permute-start.1) | collective-permute-done | bytes 524320 | tf_op jit(solution)/shard_map/ppermute | solution.py:177
  117.1 2.2 %shard_map.40 = bf16[128,8,1024]{2,1,0:T(8,128)(2,1)} custom-call(s32[1]{0:T(128)} %bitcast.side_ref, bf16[128,8,1024]{2,1,0:T(8,128)(2,1)} %shard_map.39.held_ref, bf16[32,8,1024]{2,1,0:T(8,128)(2,1)} %collective-permute-done.1.low_ref, bf16[32,8,1024]{2,1,0:T(8,128)(2,1)} %collective-permute-done.2.high_ref), custom_call_target="tpu_custom_call", output_to_operand_aliasing={{}: (1, {})} | custom-call | bytes 2097152 | tf_op jit(solution)/shard_map/pallas_call | solution.py:145
Async XLA Ops:
  0.0 1.6 %copy-start = (bf16[128,8,1024]{2,1,0:T(8,128)(2,1)S(1)}, bf16[128,8,1024]{2,1,0:T(8,128)(2,1)}, u32[]{:S(2)}) copy-start(bf16[128,8,1024]{2,1,0:T(8,128)(2,1)} %param.3) | copy-start | bytes 6291460
  47.6 4.7 %collective-permute-start = (bf16[512,1024]{1,0:T(8,128)(2,1)S(1)}, bf16[512,1024]{1,0:T(8,128)(2,1)}, u32[]{:S(2)}, u32[]{:S(2)}) collective-permute-start(bf16[512,1024]{1,0:T(8,128)(2,1)S(1)} %bitcast.6), channel_id=1, source_target_pairs={{0,4},{4,0},{1,5},{5,1},{2,6},{6,2},{3,7},{7,3},{8,12},{12,8},{9,1... | collective-permute-start | bytes 3145736 | tf_op jit(solution)/shard_map/ppermute | solution.py:168
  49.5 2.8 %copy-start.1 = (s32[128]{0:T(128)S(1)}, s32[128]{0:T(128)}, u32[]{:S(2)}) copy-start(s32[128]{0:T(128)} %param.4) | copy-start | bytes 1540
  49.5 2.7 %copy-start.2 = (s32[128]{0:T(128)S(1)}, s32[128]{0:T(128)}, u32[]{:S(2)}) copy-start(s32[128]{0:T(128)} %param.5) | copy-start | bytes 1540
  96.4 7.7 %copy-start.3 = (bf16[64,8,1024]{2,1,0:T(8,128)(2,1)}, bf16[64,8,1024]{2,1,0:T(8,128)(2,1)S(1)}, u32[]{:S(2)}) copy-start(bf16[64,8,1024]{2,1,0:T(8,128)(2,1)S(1)} %all_to_all.11.own_ref) | copy-start | bytes 3145732
  97.5 14.3 %collective-permute-start.2 = (bf16[32,8,1024]{2,1,0:T(8,128)(2,1)}, bf16[32,8,1024]{2,1,0:T(8,128)(2,1)}, u32[]{:S(2)}, u32[]{:S(2)}) collective-permute-start(bf16[32,8,1024]{2,1,0:T(8,128)(2,1)} %get-tuple-element.5), channel_id=1, source_target_pairs={{0,3},{1,0},{2,1},{3,2},{4,7},{5,4},{6,5},{7,6},{8,11},{9,8},{10,9... | collective-permute-start | bytes 1572872 | tf_op jit(solution)/shard_map/ppermute | solution.py:178
  102.2 15.0 %collective-permute-start.1 = (bf16[32,8,1024]{2,1,0:T(8,128)(2,1)}, bf16[32,8,1024]{2,1,0:T(8,128)(2,1)}, u32[]{:S(2)}, u32[]{:S(2)}) collective-permute-start(bf16[32,8,1024]{2,1,0:T(8,128)(2,1)} %get-tuple-element.6), channel_id=1, source_target_pairs={{0,1},{1,2},{2,3},{3,0},{4,5},{5,6},{6,7},{7,4},{8,9},{9,10},{10,1... | collective-permute-start | bytes 1572872 | tf_op jit(solution)/shard_map/ppermute | solution.py:177

commit v4 on v3

v4 whole, which is shorter than its diff:
```python
import functools

import jax
import jax.numpy as jnp
from jax import lax
from jax.experimental import pallas as pl
from jax.experimental.pallas import tpu as pltpu
from jax.sharding import Mesh
from jax.sharding import PartitionSpec as P

EPS = 1e-06
TILE = 256
HANDED = (0, 4, 8, 12, 16, 24, 32)
BLOCK, RANK, TIER, PAIR, COUNT = range(5)


def down_columns(row):
    n = row.shape[1]
    return jnp.broadcast_to(row, (n, n)).T


def plan_kernel(side_ref, owners_ref, counts_ref, grads_ref, out_ref, plan_ref, rows_ref, plan_sem, sem):
    places, blocks = out_ref.shape[0], owners_ref.shape[1]
    square = (blocks, blocks)
    i = lax.broadcasted_iota(jnp.int32, square, 0)
    j = lax.broadcasted_iota(jnp.int32, square, 1)
    owners = jnp.broadcast_to(owners_ref[...], square)
    same = (down_columns(owners_ref[...]) == owners) & (i < j)
    slot = jnp.sum(jnp.where(same, 1, 0), axis=0, keepdims=True)
    have = jnp.sum(jnp.where(owners == i, down_columns(counts_ref[...]), 0), axis=0, keepdims=True)
    valid = jnp.where(slot < have, 1, 0)
    before = jnp.sum(jnp.where(i < j, down_columns(valid), 0), axis=0, keepdims=True)
    rank = jnp.where(slot < have, before, -1)
    block = jnp.sum(jnp.where(down_columns(rank) == j, i, 0), axis=0, keepdims=True)
    count = jnp.broadcast_to(jnp.sum(valid, axis=1, keepdims=True), (1, blocks))
    tier, pair = jnp.zeros_like(count), jnp.zeros_like(count)
    for smaller, k in zip(HANDED, HANDED[1:]):
        more = count > places + 2 * smaller
        tier = jnp.where(more, tier + 1, tier)
        pair = jnp.where(more, 2 * k, pair)
    for index, row in ((BLOCK, block), (RANK, rank), (TIER, tier), (PAIR, pair), (COUNT, count)):
        rows_ref[index : index + 1, :] = row
    to_scalars = pltpu.make_async_copy(rows_ref, plan_ref, plan_sem)
    to_scalars.start()
    to_scalars.wait()

    pair = plan_ref[PAIR, 0]
    first = side_ref[0] * pair

    def pick(place, carry):
        position = jnp.where(place < first, place, place + pair)
        pltpu.make_async_copy(grads_ref.at[plan_ref[BLOCK, position]], out_ref.at[place], sem).start()
        return carry

    lax.fori_loop(0, places, pick, 0, unroll=8)
    pltpu.make_async_copy(out_ref, out_ref, sem).wait()


def make_plan(side, owners, counts, grads, places):
    blocks = grads.shape[0]
    vmem = pl.BlockSpec(memory_space=pltpu.VMEM)
    smem = pl.BlockSpec(memory_space=pltpu.SMEM)
    return pl.pallas_call(
        plan_kernel,
        out_shape=(
            jax.ShapeDtypeStruct((places,) + grads.shape[1:], grads.dtype),
            jax.ShapeDtypeStruct((8, blocks), jnp.int32),
        ),
        in_specs=[smem, vmem, vmem, pl.BlockSpec(memory_space=pltpu.HBM)],
        out_specs=(vmem, smem),
        scratch_shapes=[
            pltpu.VMEM((8, blocks), jnp.int32),
            pltpu.SemaphoreType.DMA,
            pltpu.SemaphoreType.DMA,
        ],
    )(side, owners.reshape(1, -1), counts.reshape(1, -1), grads)


def first_dims(a, b):
    return lax.dot_general(a, b, (((0,), (0,)), ((), ())), preferred_element_type=jnp.float32)


def gram_kernel(rows_ref, out_ref):
    width = rows_ref.shape[1]
    for j in range(0, width, TILE):
        out_ref[j:, j : j + TILE] = first_dims(rows_ref[:, j:], rows_ref[:, j : j + TILE])


def gram(rows):
    count, width = rows.shape
    vmem = pl.BlockSpec(memory_space=pltpu.VMEM)
    return pl.pallas_call(
        gram_kernel,
        out_shape=jax.ShapeDtypeStruct((width, width), jnp.float32),
        in_specs=[vmem],
        out_specs=vmem,
        compiler_params=pltpu.CompilerParams(vmem_limit_bytes=24 * 2**20),
        cost_estimate=pl.CostEstimate(
            flops=2 * count * width**2, bytes_accessed=2 * count * width + 4 * width**2, transcendentals=0
        ),
    )(rows)


def on_diagonal(tile):
    r = lax.broadcasted_iota(jnp.int32, tile.shape, 0)
    c = lax.broadcasted_iota(jnp.int32, tile.shape, 1)
    return r == c


def refresh_kernel(mine_ref, theirs_ref, gram_ref, out_ref, right, root_r, rest, product):
    rows, width = mine_ref.shape
    total_sq = jnp.zeros((1, 1), jnp.float32)
    for j in range(0, width, TILE):
        tile = gram_ref[j:, j : j + TILE] + first_dims(theirs_ref[:, j:], theirs_ref[:, j : j + TILE])
        right[j:, j : j + TILE] = tile
        top = tile[:TILE, :]
        total_sq += jnp.sum(jnp.where(on_diagonal(top), top, 0.0), keepdims=True)

    scale_c = total_sq / width + EPS
    quarter = lax.rsqrt(jnp.sqrt(scale_c)) * 0.25
    slope = quarter / scale_c
    diag = 5.0 * quarter - EPS * slope
    for j in range(0, width, TILE):
        cols = slice(j, j + TILE)
        tile = -slope * right[cols, cols]
        tile = jnp.where(on_diagonal(tile), diag + tile, tile)
        kept = tile.astype(jnp.bfloat16)
        root_r[cols, cols] = kept
        off = jnp.where(on_diagonal(tile), tile - kept.astype(jnp.float32), 0.0)
        rest[:, cols] = 2.0 * jnp.sum(off, axis=0, keepdims=True)
        if j + TILE < width:
            below = (-slope * right[j + TILE :, cols]).astype(jnp.bfloat16)
            root_r[j + TILE :, cols] = below
            root_r[cols, j + TILE :] = below.T

    product_sq = jnp.zeros((1, 1), jnp.float32)
    for ref, keep in ((mine_ref, True), (theirs_ref, False)):
        for i in range(0, rows, TILE):
            hidden = jnp.dot(ref[i : i + TILE, :], root_r[...], preferred_element_type=jnp.float32)
            done = jnp.dot(hidden.astype(jnp.bfloat16), root_r[...], preferred_element_type=jnp.float32)
            done = done + hidden * rest[...]
            product_sq += jnp.sum(done * done, keepdims=True)
            if keep:
                product[i : i + TILE, :] = done
    graft = jnp.sqrt((total_sq + EPS) / (product_sq + EPS))
    out_ref[...] = (product[...] * graft).astype(jnp.bfloat16)


def refresh(mine, theirs, mine_gram):
    rows, width = mine.shape
    vmem = pl.BlockSpec(memory_space=pltpu.VMEM)
    return pl.pallas_call(
        refresh_kernel,
        out_shape=jax.ShapeDtypeStruct((rows, width), jnp.bfloat16),
        in_specs=[vmem, vmem, vmem],
        out_specs=vmem,
        scratch_shapes=[
            pltpu.VMEM((width, width), jnp.float32),
            pltpu.VMEM((width, width), jnp.bfloat16),
            pltpu.VMEM((1, width), jnp.float32),
            pltpu.VMEM((rows, width), jnp.float32),
        ],
        compiler_params=pltpu.CompilerParams(vmem_limit_bytes=40 * 2**20),
        cost_estimate=pl.CostEstimate(flops=5 * width**3, bytes_accessed=6 * rows * width, transcendentals=0),
    )(mine, theirs, mine_gram)


def place_own_kernel(side_ref, plan_ref, own_ref, out_ref, whole, sems):
    blocks = out_ref.shape[0]
    pieces = sems.shape[0]
    piece = blocks // pieces
    pair = plan_ref[PAIR, 0]
    first = side_ref[0] * pair
    copies = []
    for p in range(pieces):
        for block in range(p * piece, (p + 1) * piece):
            rank = plan_ref[RANK, block]
            place = jnp.where(rank < first, rank, rank - pair)
            held = (rank >= 0) & ((rank < first) | (rank >= first + pair))
            rows = own_ref[jnp.where(held, place, 0)]
            whole[block] = jnp.where(held, rows, jnp.zeros_like(rows))
        part = pl.ds(p * piece, piece)
        copies.append(pltpu.make_async_copy(whole.at[part], out_ref.at[part], sems.at[p]))
        copies[-1].start()
    for copy in copies:
        copy.wait()


def place_own(side, plan, own):
    blocks = plan.shape[1]
    shape = (blocks,) + own.shape[1:]
    smem = pl.BlockSpec(memory_space=pltpu.SMEM)
    return pl.pallas_call(
        place_own_kernel,
        out_shape=jax.ShapeDtypeStruct(shape, own.dtype),
        in_specs=[smem, smem, pl.BlockSpec(memory_space=pltpu.VMEM)],
        out_specs=pl.BlockSpec(memory_space=pltpu.HBM),
        scratch_shapes=[pltpu.VMEM(shape, own.dtype), pltpu.SemaphoreType.DMA((8,))],
        cost_estimate=pl.CostEstimate(flops=0, bytes_accessed=4 * own.size, transcendentals=0),
    )(side, plan, own)


def place_others_kernel(side_ref, plan_ref, held_ref, low_ref, high_ref, out_ref, sems):
    k = low_ref.shape[0]
    first = side_ref[0] * (2 * k)
    count = plan_ref[COUNT, 0]
    copies = []
    for q in range(2 * k):
        source = low_ref.at[q] if q < k else high_ref.at[q - k]
        copies.append(pltpu.make_async_copy(source, out_ref.at[plan_ref[BLOCK, first + q]], sems.at[q]))
    for act in ("start", "wait"):
        for q, copy in enumerate(copies):
            pl.when(first + q < count)(getattr(copy, act))


def place_others(side, plan, held, low, high):
    smem = pl.BlockSpec(memory_space=pltpu.SMEM)
    vmem = pl.BlockSpec(memory_space=pltpu.VMEM)
    hbm = pl.BlockSpec(memory_space=pltpu.HBM)
    return pl.pallas_call(
        place_others_kernel,
        out_shape=jax.ShapeDtypeStruct(held.shape, held.dtype),
        in_specs=[smem, smem, hbm, vmem, vmem],
        out_specs=hbm,
        scratch_shapes=[pltpu.SemaphoreType.DMA((2 * low.shape[0],))],
        input_output_aliases={2: 0},
        cost_estimate=pl.CostEstimate(flops=0, bytes_accessed=8 * low.size, transcendentals=0),
    )(side, plan, held, low, high)


def exchange(k, side, plan, own):
    planes = lax.axis_size("x")
    if k == 0:
        return place_own(side, plan, own)
    up = [(i, (i + 1) % planes) for i in range(planes)]
    down = [(i, (i - 1) % planes) for i in range(planes)]
    low = lax.ppermute(own[:k], "x", up)
    high = lax.ppermute(own[k : 2 * k], "x", down)
    held = place_own(side, plan, own)
    return place_others(side, plan, held, low, high)


def body(grads, owners, counts):
    blocks, rows_dev, width = grads.shape
    chips = lax.axis_size("yz")
    side = (lax.axis_index("x") % 2).astype(jnp.int32).reshape(1)

    outgoing, plan = make_plan(side, owners, counts, grads, chips)
    mine = lax.all_to_all(outgoing, "yz", split_axis=0, concat_axis=0, tiled=True)
    mine = mine.reshape(chips * rows_dev, width)
    theirs = lax.ppermute(mine, "c", [(0, 1), (1, 0)])
    done = refresh(mine, theirs, gram(mine))
    own = lax.all_to_all(
        done.reshape(chips, rows_dev, width), "yz", split_axis=0, concat_axis=0, tiled=True
    )
    branches = [functools.partial(exchange, k) for k in HANDED]
    return lax.switch(plan[TIER, 0], branches, side, plan, own)


def solution(mesh):
    fine = Mesh(mesh.devices.reshape(64, 2, 4), ("yz", "c", "x"))
    rows = P(None, ("yz", "c"), None)
    return jax.shard_map(body, mesh=fine, in_specs=(rows, P(), P()), out_specs=rows, check_vma=False)
```

time: 120 us -> 115 us (0.958)
  the two profiles are of different devices: /device:TPU:24 before, /device:TPU:22 now
where the time goes in v4:
time: 115 us; the launch traced here: 114 us
  blocking collectives  47 us (41%)
  waiting for transfers between devices  35 us (30%)
  Pallas kernels  16.5 us (14%)
  starting transfers between devices  13.3 us (12%)
  local copies, waits for them, and re-layouts  1.33 us (1%)
    all_to_all x1, blocking collectives, body(): lax.all_to_all(outgoing, 'yz', split_axis=0, concat_axis=0, tiled=True)  47 us
    all_to_all x1, waiting for transfers between devices, body(): lax.all_to_all(done.reshape(chips, rows_dev, width), 'yz', split_axis=0,...  29.3 us
    pallas_call x1, Pallas kernels, refresh(): pl.pallas_call(refresh_kernel, out_shape=jax.ShapeDtypeStruct((rows, widt...  7.66 us
    all_to_all x1, starting transfers between devices, body(): lax.all_to_all(done.reshape(chips, rows_dev, width), 'yz', split_axis=0,...  5.58 us
    pallas_call x1, Pallas kernels, make_plan(): pl.pallas_call(plan_kernel, out_shape=(jax.ShapeDtypeStruct((places,) + g...  3.78 us
    ppermute x1, waiting for transfers between devices, exchange(): high = lax.ppermute(own[k:2 * k], 'x', down)  3.62 us
    ppermute x1, starting transfers between devices, exchange(): high = lax.ppermute(own[k:2 * k], 'x', down)  3.44 us
    ppermute x1, starting transfers between devices, exchange(): low = lax.ppermute(own[:k], 'x', up)  2.4 us
  transfers between devices with their start and end apart: 4, of which 4 were waited for; matrix products, arithmetic and copies ran while one was open for 1% of the time, Pallas kernels for 3%

profile of v4, /device:TPU:22, one launch (start us, length us, event | category | flops | bytes accessed | tf_op | source)
XLA Modules:
  0.0 114.5 jit_solution(16988904669491598161)
XLA Ops:
  0.0 3.8 %shard_map.44 = (bf16[64,8,1024]{2,1,0:T(8,128)(2,1)}, s32[8,128]{1,0:T(8,128)S(1)}) custom-call(s32[1]{0:T(128)} %bitcast.side_ref, s32[1,128]{1,0:T(1,128)} %bitcast.9, s32[1,128]{1,0:T(1,128)} %bitcast.10, bf16[128,8,1024]{2,1,0:T(8,128)(2,1)} %grads_ref.1), custom_call_target="tpu_custom_call" | custom-call | tf_op jit(solution)/shard_map/pallas_call | solution.py:63
  3.8 47.0 %all_to_all.10 = bf16[64,8,1024]{2,1,0:T(8,128)(2,1)S(1)} all-to-all(bf16[64,8,1024]{2,1,0:T(8,128)(2,1)} %get-tuple-element.79), channel_id=1, replica_groups=mesh['yz'=64,'c'=2,'x'=4] {'yz'}, dimensions={0} | all-to-all | bytes 2097152 | tf_op jit(solution)/shard_map/all_to_all | solution.py:249
  50.8 1.9 %collective-permute-start.12 = (bf16[512,1024]{1,0:T(8,128)(2,1)S(1)}, bf16[512,1024]{1,0:T(8,128)(2,1)S(1)}, u32[]{:S(2)}, u32[]{:S(2)}) collective-permute-start(bf16[512,1024]{1,0:T(8,128)(2,1)S(1)} %bitcast.6), channel_id=1, source_target_pairs={{0,4},{4,0},{1,5},{5,1},{2,6},{6,2},{3,7},{7,3},{8,12},{12,8},{9,1... | collective-permute-start | bytes 3145736 | tf_op jit(solution)/shard_map/ppermute | solution.py:251
  52.7 0.9 shard_map.45.gram_ref
  53.6 1.7 %collective-permute-done.12.theirs_ref = bf16[512,1024]{1,0:T(8,128)(2,1)S(1)} collective-permute-done((bf16[512,1024]{1,0:T(8,128)(2,1)S(1)}, bf16[512,1024]{1,0:T(8,128)(2,1)S(1)}, u32[]{:S(2)}, u32[]{:S(2)}) %collective-permute-start.12) | collective-permute-done | bytes 1048608 | tf_op jit(solution)/shard_map/ppermute | solution.py:251
  55.3 7.7 %shard_map.46 = bf16[512,1024]{1,0:T(8,128)(2,1)} custom-call(bf16[512,1024]{1,0:T(8,128)(2,1)S(1)} %bitcast.8, bf16[512,1024]{1,0:T(8,128)(2,1)S(1)} %collective-permute-done.12.theirs_ref, f32[1024,1024]{1,0:T(8,128)S(1)} %shard_map.45.gram_ref), custom_call_target="tpu_custom_call" | custom-call | flops 5368709120 | bytes 3145728 | tf_op jit(solution)/shard_map/pallas_call | solution.py:152
  63.0 5.6 %all-to-all-start.1 = ((bf16[64,8,1024]{2,1,0:T(8,128)(2,1)}), bf16[64,8,1024]{2,1,0:T(8,128)(2,1)S(1)}, u32[]{:S(2)}, u32[]{:S(2)}) async-start(bf16[64,8,1024]{2,1,0:T(8,128)(2,1)} %bitcast.5), calls=%async_computation.1 | async-start | bytes 2097152 | tf_op jit(solution)/shard_map/all_to_all | solution.py:253
  68.6 0.6 slice.39
  69.9 29.3 %all-to-all-done.1 = bf16[64,8,1024]{2,1,0:T(8,128)(2,1)S(1)} async-done(((bf16[64,8,1024]{2,1,0:T(8,128)(2,1)}), bf16[64,8,1024]{2,1,0:T(8,128)(2,1)S(1)}, u32[]{:S(2)}, u32[]{:S(2)}) %all-to-all-start.1) | async-done | bytes 1048608 | tf_op jit(solution)/shard_map/all_to_all | solution.py:253
  99.1 15.1 %conditional.1 = (bf16[128,8,1024]{2,1,0:T(8,128)(2,1)}) conditional(s32[]{:T(128)} %bitcast.3, (s32[1]{0:T(128)}, s32[8,128]{1,0:T(8,128)S(1)}, bf16[64,8,1024]{2,1,0:T(8,128)(2,1)S(1)}) %tuple.26, (s32[1]{0:T(128)}, s32[8,128]{1,0:T(8,128)S(1)}, bf16[64,8,1024]{2,1,0:T(8,128)(2,1)S(1)}) %tuple.26, (s32[1]{0:T(128)}, ...), branch_computations={%region_0.1_spmd, %region_1.2_spmd, %region_2.3_spmd, %region_3.4_... | conditional | bytes 14680208 | solution.py:257
  99.2 2.4 %collective-permute-start.6 = (bf16[16,8,1024]{2,1,0:T(8,128)(2,1)S(1)}, bf16[16,8,1024]{2,1,0:T(8,128)(2,1)S(1)}, u32[]{:S(2)}, u32[]{:S(2)}) collective-permute-start(bf16[16,8,1024]{2,1,0:T(8,128)(2,1)S(1)} %get-tuple-element.88), channel_id=1, source_target_pairs={{0,1},{1,2},{2,3},{3,0},{4,5},{5,6},{6,7},{7,4},{8,9},{9,10},{10,1... | collective-permute-start | bytes 786440 | tf_op jit(solution)/shard_map/cond/branch_4_fun/ppermute | solution.py:237
  101.6 3.4 %collective-permute-start.7 = (bf16[16,8,1024]{2,1,0:T(8,128)(2,1)S(1)}, bf16[16,8,1024]{2,1,0:T(8,128)(2,1)S(1)}, u32[]{:S(2)}, u32[]{:S(2)}) collective-permute-start(bf16[16,8,1024]{2,1,0:T(8,128)(2,1)S(1)} %get-tuple-element.87), channel_id=1, source_target_pairs={{0,3},{1,0},{2,1},{3,2},{4,7},{5,4},{6,5},{7,6},{8,11},{9,8},{10,9... | collective-permute-start | bytes 786440 | tf_op jit(solution)/shard_map/cond/branch_4_fun/ppermute | solution.py:238
  105.0 2.1 %branch_4_fun.2.held_ref = bf16[128,8,1024]{2,1,0:T(8,128)(2,1)} custom-call(s32[1]{0:T(128)} %get-tuple-element.67.side_ref, s32[8,128]{1,0:T(8,128)S(1)} %get-tuple-element.68.plan_ref, bf16[64,8,1024]{2,1,0:T(8,128)(2,1)S(1)} %get-tuple-element.69.own_ref), custom_call_target="tpu_custom_call" | custom-call | bytes 2097152 | tf_op jit(solution)/shard_map/cond/branch_4_fun/pallas_call | solution.py:193
  107.1 0.3 collective-permute-done.6.low_ref
  107.5 0.0 copy-start.4
  107.5 3.6 %collective-permute-done.7.high_ref = bf16[16,8,1024]{2,1,0:T(8,128)(2,1)S(1)} collective-permute-done((bf16[16,8,1024]{2,1,0:T(8,128)(2,1)S(1)}, bf16[16,8,1024]{2,1,0:T(8,128)(2,1)S(1)}, u32[]{:S(2)}, u32[]{:S(2)}) %collective-permute-start.7) | collective-permute-done | bytes 262176 | tf_op jit(solution)/shard_map/cond/branch_4_fun/ppermute | solution.py:238
  111.1 0.0 copy-done.4
  111.1 0.0 copy-start.5
  111.1 0.7 copy-done.5
  111.8 2.1 %branch_4_fun.3 = bf16[128,8,1024]{2,1,0:T(8,128)(2,1)} custom-call(s32[1]{0:T(128)} %get-tuple-element.67.side_ref, s32[8,128]{1,0:T(8,128)S(1)} %get-tuple-element.68.plan_ref, bf16[128,8,1024]{2,1,0:T(8,128)(2,1)} %branch_4_fun.2.held_ref, bf16[16,8,1024]{2,1,0:T(8,128)(2,1)} %copy-done.4, ...), custom_call_target="tpu_custom_call", output_to_operand_aliasing={{}: (2, {})} | custom-call | bytes 1048576 | tf_op jit(solution)/shard_map/cond/branch_4_fun/pallas_call | solution.py:220
  (1 shorter events, 0.0 us)
Async XLA Ops:
  50.8 4.5 %collective-permute-start.12 = (bf16[512,1024]{1,0:T(8,128)(2,1)S(1)}, bf16[512,1024]{1,0:T(8,128)(2,1)S(1)}, u32[]{:S(2)}, u32[]{:S(2)}) collective-permute-start(bf16[512,1024]{1,0:T(8,128)(2,1)S(1)} %bitcast.6), channel_id=1, source_target_pairs={{0,4},{4,0},{1,5},{5,1},{2,6},{6,2},{3,7},{7,3},{8,12},{12,8},{9,1... | collective-permute-start | bytes 3145736 | tf_op jit(solution)/shard_map/ppermute | solution.py:251
  63.0 36.2 %all-to-all-start.1 = ((bf16[64,8,1024]{2,1,0:T(8,128)(2,1)}), bf16[64,8,1024]{2,1,0:T(8,128)(2,1)S(1)}, u32[]{:S(2)}, u32[]{:S(2)}) async-start(bf16[64,8,1024]{2,1,0:T(8,128)(2,1)} %bitcast.5), calls=%async_computation.1 | async-start | bytes 2097152 | tf_op jit(solution)/shard_map/all_to_all | solution.py:253
  99.2 8.3 %collective-permute-start.6 = (bf16[16,8,1024]{2,1,0:T(8,128)(2,1)S(1)}, bf16[16,8,1024]{2,1,0:T(8,128)(2,1)S(1)}, u32[]{:S(2)}, u32[]{:S(2)}) collective-permute-start(bf16[16,8,1024]{2,1,0:T(8,128)(2,1)S(1)} %get-tuple-element.88), channel_id=1, source_target_pairs={{0,1},{1,2},{2,3},{3,0},{4,5},{5,6},{6,7},{7,4},{8,9},{9,10},{10,1... | collective-permute-start | bytes 786440 | tf_op jit(solution)/shard_map/cond/branch_4_fun/ppermute | solution.py:237
  101.6 9.5 %collective-permute-start.7 = (bf16[16,8,1024]{2,1,0:T(8,128)(2,1)S(1)}, bf16[16,8,1024]{2,1,0:T(8,128)(2,1)S(1)}, u32[]{:S(2)}, u32[]{:S(2)}) collective-permute-start(bf16[16,8,1024]{2,1,0:T(8,128)(2,1)S(1)} %get-tuple-element.87), channel_id=1, source_target_pairs={{0,3},{1,0},{2,1},{3,2},{4,7},{5,4},{6,5},{7,6},{8,11},{9,8},{10,9... | collective-permute-start | bytes 786440 | tf_op jit(solution)/shard_map/cond/branch_4_fun/ppermute | solution.py:238
  107.5 3.6 %copy-start.4 = (bf16[16,8,1024]{2,1,0:T(8,128)(2,1)}, bf16[16,8,1024]{2,1,0:T(8,128)(2,1)S(1)}, u32[]{:S(2)}) copy-start(bf16[16,8,1024]{2,1,0:T(8,128)(2,1)S(1)} %collective-permute-done.6.low_ref) | copy-start | bytes 786436 | tf_op jit(solution)/shard_map/cond
  111.1 0.7 copy-start.5

commit v5 on v4

v5 whole, which is shorter than its diff:
```python
import functools

import jax
import jax.numpy as jnp
from jax import lax
from jax.experimental import pallas as pl
from jax.experimental.pallas import tpu as pltpu
from jax.sharding import Mesh
from jax.sharding import PartitionSpec as P

EPS = 1e-06
TILE = 256
HANDED = ((0, 0), (8, 0), (13, 3), (17, 7), (21, 11), (29, 19), (37, 27))
BLOCK, RANK, TIER, MORE, COUNT = range(5)


def down_columns(row):
    n = row.shape[1]
    return jnp.broadcast_to(row, (n, n)).T


def plan_kernel(
    side_ref, owners_ref, counts_ref, grads_ref, out_ref, plan_ref, whole, rows_ref, plan_sem, whole_sem
):
    load = pltpu.make_async_copy(grads_ref, whole, whole_sem)
    load.start()
    places, blocks = out_ref.shape[0], owners_ref.shape[1]
    square = (blocks, blocks)
    i = lax.broadcasted_iota(jnp.int32, square, 0)
    j = lax.broadcasted_iota(jnp.int32, square, 1)
    owners = jnp.broadcast_to(owners_ref[...], square)
    same = (down_columns(owners_ref[...]) == owners) & (i < j)
    slot = jnp.sum(jnp.where(same, 1, 0), axis=0, keepdims=True)
    have = jnp.sum(jnp.where(owners == i, down_columns(counts_ref[...]), 0), axis=0, keepdims=True)
    valid = jnp.where(slot < have, 1, 0)
    before = jnp.sum(jnp.where(i < j, down_columns(valid), 0), axis=0, keepdims=True)
    count = jnp.broadcast_to(jnp.sum(valid, axis=1, keepdims=True), (1, blocks))
    rank = jnp.where(slot < have, before, count + j[:1, :] - before)
    block = jnp.sum(jnp.where(down_columns(rank) == j, i, 0), axis=0, keepdims=True)
    tier, more = jnp.zeros_like(count), jnp.zeros_like(count)
    for smaller, larger in zip(HANDED, HANDED[1:]):
        above = count > places + sum(smaller)
        tier = jnp.where(above, tier + 1, tier)
        more = jnp.where(above, sum(larger), more)
    for index, row in ((BLOCK, block), (RANK, rank), (TIER, tier), (MORE, more), (COUNT, count)):
        rows_ref[index : index + 1, :] = row
    to_scalars = pltpu.make_async_copy(rows_ref, plan_ref, plan_sem)
    to_scalars.start()
    to_scalars.wait()
    load.wait()
    more = plan_ref[MORE, 0]
    first = side_ref[0] * more
    for place in range(places):
        position = jnp.where(place < first, place, place + more)
        out_ref[place] = whole[plan_ref[BLOCK, position]]


def make_plan(side, owners, counts, grads, places):
    blocks = grads.shape[0]
    vmem = pl.BlockSpec(memory_space=pltpu.VMEM)
    smem = pl.BlockSpec(memory_space=pltpu.SMEM)
    return pl.pallas_call(
        plan_kernel,
        out_shape=(
            jax.ShapeDtypeStruct((places,) + grads.shape[1:], grads.dtype),
            jax.ShapeDtypeStruct((8, blocks), jnp.int32),
        ),
        in_specs=[smem, vmem, vmem, pl.BlockSpec(memory_space=pltpu.HBM)],
        out_specs=(vmem, smem),
        scratch_shapes=[
            pltpu.VMEM(grads.shape, grads.dtype),
            pltpu.VMEM((8, blocks), jnp.int32),
            pltpu.SemaphoreType.DMA,
            pltpu.SemaphoreType.DMA,
        ],
    )(side, owners.reshape(1, -1), counts.reshape(1, -1), grads)


def first_dims(a, b):
    return lax.dot_general(a, b, (((0,), (0,)), ((), ())), preferred_element_type=jnp.float32)


def gram_kernel(rows_ref, out_ref):
    width = rows_ref.shape[1]
    for j in range(0, width, TILE):
        out_ref[j:, j : j + TILE] = first_dims(rows_ref[:, j:], rows_ref[:, j : j + TILE])


def gram(rows):
    count, width = rows.shape
    vmem = pl.BlockSpec(memory_space=pltpu.VMEM)
    return pl.pallas_call(
        gram_kernel,
        out_shape=jax.ShapeDtypeStruct((width, width), jnp.float32),
        in_specs=[vmem],
        out_specs=vmem,
        compiler_params=pltpu.CompilerParams(vmem_limit_bytes=24 * 2**20),
        cost_estimate=pl.CostEstimate(
            flops=2 * count * width**2, bytes_accessed=2 * count * width + 4 * width**2, transcendentals=0
        ),
    )(rows)


def on_diagonal(tile):
    r = lax.broadcasted_iota(jnp.int32, tile.shape, 0)
    c = lax.broadcasted_iota(jnp.int32, tile.shape, 1)
    return r == c


def folded_squares(tile):
    squares = tile * tile
    folded = jnp.sum(squares.reshape(tile.shape[0] // 8, 8, tile.shape[1]), axis=0)
    return sum(folded[:, c : c + 128] for c in range(0, tile.shape[1], 128))


def refresh_kernel(
    side_ref, plan_ref, mine_ref, theirs_ref, gram_ref, out_ref, right, root, square, rest, product
):
    rows, width = mine_ref.shape
    place, more = side_ref[1], plan_ref[MORE, 0]
    position = jnp.where(place < side_ref[0] * more, place, place + more)
    valid = jnp.where(position < plan_ref[COUNT, 0], 1.0, 0.0)

    total_sq = jnp.zeros((1, 1), jnp.float32)
    for j in range(0, width, TILE):
        tile = gram_ref[j:, j : j + TILE] + first_dims(theirs_ref[:, j:], theirs_ref[:, j : j + TILE])
        right[j:, j : j + TILE] = tile
        top = tile[:TILE, :]
        total_sq += jnp.sum(jnp.where(on_diagonal(top), top, 0.0), keepdims=True)

    scale_c = total_sq / width + EPS
    quarter = lax.rsqrt(jnp.sqrt(scale_c)) * 0.25
    slope = quarter / scale_c
    diag = 5.0 * quarter - EPS * slope
    for j in range(0, width, TILE):
        cols = slice(j, j + TILE)
        tile = -slope * right[cols, cols]
        tile = jnp.where(on_diagonal(tile), diag + tile, tile)
        kept = tile.astype(jnp.bfloat16)
        root[cols, cols] = kept
        kept = kept.astype(jnp.float32)
        off = jnp.where(on_diagonal(tile), 2.0 * (tile - kept) * kept, 0.0)
        rest[:, cols] = jnp.sum(off, axis=0, keepdims=True)
        if j + TILE < width:
            below = (-slope * right[j + TILE :, cols]).astype(jnp.bfloat16)
            root[j + TILE :, cols] = below
            root[cols, j + TILE :] = below.T

    for j in range(0, width, TILE):
        cols = slice(j, j + TILE)
        tile = jnp.dot(root[j:, :], root[:, cols], preferred_element_type=jnp.float32)
        top = tile[:TILE]
        kept = top.astype(jnp.bfloat16)
        square[cols, cols] = kept
        off = jnp.where(on_diagonal(top), top - kept.astype(jnp.float32), 0.0)
        rest[:, cols] += jnp.sum(off, axis=0, keepdims=True)
        if j + TILE < width:
            below = tile[TILE:].astype(jnp.bfloat16)
            square[j + TILE :, cols] = below
            square[cols, j + TILE :] = below.T

    squares = jnp.zeros((8, 128), jnp.float32)
    for ref, keep in ((mine_ref, True), (theirs_ref, False)):
        for j in range(0, width, TILE):
            cols = slice(j, j + TILE)
            done = jnp.dot(ref[...], square[:, cols], preferred_element_type=jnp.float32)
            done = done + ref[:, cols].astype(jnp.float32) * rest[:, cols]
            squares += folded_squares(done)
            if keep:
                product[:, cols] = done
    product_sq = jnp.sum(squares, keepdims=True)
    graft = jnp.sqrt((total_sq + EPS) / (product_sq + EPS)) * valid
    out_ref[...] = (product[...] * graft).astype(jnp.bfloat16)


def refresh(side, plan, mine, theirs, mine_gram):
    rows, width = mine.shape
    vmem = pl.BlockSpec(memory_space=pltpu.VMEM)
    smem = pl.BlockSpec(memory_space=pltpu.SMEM)
    return pl.pallas_call(
        refresh_kernel,
        out_shape=jax.ShapeDtypeStruct((rows, width), jnp.bfloat16),
        in_specs=[smem, smem, vmem, vmem, vmem],
        out_specs=vmem,
        scratch_shapes=[
            pltpu.VMEM((width, width), jnp.float32),
            pltpu.VMEM((width, width), jnp.bfloat16),
            pltpu.VMEM((width, width), jnp.bfloat16),
            pltpu.VMEM((1, width), jnp.float32),
            pltpu.VMEM((rows, width), jnp.float32),
        ],
        compiler_params=pltpu.CompilerParams(vmem_limit_bytes=44 * 2**20),
        cost_estimate=pl.CostEstimate(flops=4 * width**3, bytes_accessed=6 * rows * width, transcendentals=0),
    )(side, plan, mine, theirs, mine_gram)


def place_own_kernel(side_ref, plan_ref, own_ref, out_ref, whole, sems):
    blocks = out_ref.shape[0]
    pieces = sems.shape[0]
    piece = blocks // pieces
    more, count = plan_ref[MORE, 0], plan_ref[COUNT, 0]
    first = side_ref[0] * more
    copies = []
    for p in range(pieces):
        for block in range(p * piece, (p + 1) * piece):
            rank = plan_ref[RANK, block]
            place = jnp.where(rank < first, rank, rank - more)
            held = (rank < count) & ((rank < first) | (rank >= first + more))
            rows = own_ref[jnp.where(held, place, 0)]
            whole[block] = jnp.where(held, rows, jnp.zeros_like(rows))
        part = pl.ds(p * piece, piece)
        copies.append(pltpu.make_async_copy(whole.at[part], out_ref.at[part], sems.at[p]))
        copies[-1].start()
    for copy in copies:
        copy.wait()


def place_own(side, plan, own):
    blocks = plan.shape[1]
    shape = (blocks,) + own.shape[1:]
    smem = pl.BlockSpec(memory_space=pltpu.SMEM)
    return pl.pallas_call(
        place_own_kernel,
        out_shape=jax.ShapeDtypeStruct(shape, own.dtype),
        in_specs=[smem, smem, pl.BlockSpec(memory_space=pltpu.VMEM)],
        out_specs=pl.BlockSpec(memory_space=pltpu.HBM),
        scratch_shapes=[pltpu.VMEM(shape, own.dtype), pltpu.SemaphoreType.DMA((8,))],
        cost_estimate=pl.CostEstimate(flops=0, bytes_accessed=4 * own.size, transcendentals=0),
    )(side, plan, own)


def place_others_kernel(side_ref, plan_ref, held_ref, *refs):
    parts, out_ref, sems = refs[:-2], refs[-2], refs[-1]
    position = side_ref[0] * sum(part.shape[0] for part in parts)
    for index, part in enumerate(parts):
        for q in range(part.shape[0]):
            target = out_ref.at[plan_ref[BLOCK, position + q]]
            pltpu.make_async_copy(part.at[q], target, sems.at[index]).start()
        position += part.shape[0]
    for index, part in enumerate(parts):
        pltpu.make_async_copy(part, part, sems.at[index]).wait()


def place_others(side, plan, held, parts):
    smem = pl.BlockSpec(memory_space=pltpu.SMEM)
    vmem = pl.BlockSpec(memory_space=pltpu.VMEM)
    hbm = pl.BlockSpec(memory_space=pltpu.HBM)
    size = sum(part.size for part in parts)
    return pl.pallas_call(
        place_others_kernel,
        out_shape=jax.ShapeDtypeStruct(held.shape, held.dtype),
        in_specs=[smem, smem, hbm] + [vmem] * len(parts),
        out_specs=hbm,
        scratch_shapes=[pltpu.SemaphoreType.DMA((len(parts),))],
        input_output_aliases={2: 0},
        cost_estimate=pl.CostEstimate(flops=0, bytes_accessed=4 * size, transcendentals=0),
    )(side, plan, held, *parts)


def exchange(handed, side, plan, own):
    planes = lax.axis_size("x")
    start, parts = 0, []
    for size, step in zip(handed, (1, -1)):
        if size:
            pairs = [(i, (i + step) % planes) for i in range(planes)]
            parts.append(lax.ppermute(own[start : start + size], "x", pairs))
            start += size
    held = place_own(side, plan, own)
    return place_others(side, plan, held, parts) if parts else held


def body(grads, owners, counts):
    blocks, rows_dev, width = grads.shape
    chips = lax.axis_size("yz")
    side = jnp.stack([lax.axis_index("x") % 2, lax.axis_index("yz")]).astype(jnp.int32)

    outgoing, plan = make_plan(side, owners, counts, grads, chips)
    mine = lax.all_to_all(outgoing, "yz", split_axis=0, concat_axis=0, tiled=True)
    mine = mine.reshape(chips * rows_dev, width)
    theirs = lax.ppermute(mine, "c", [(0, 1), (1, 0)])
    done = refresh(side, plan, mine, theirs, gram(mine))
    own = lax.all_to_all(
        done.reshape(chips, rows_dev, width), "yz", split_axis=0, concat_axis=0, tiled=True
    )
    branches = [functools.partial(exchange, handed) for handed in HANDED]
    return lax.switch(plan[TIER, 0], branches, side, plan, own)


def solution(mesh):
    fine = Mesh(mesh.devices.reshape(64, 2, 4), ("yz", "c", "x"))
    rows = P(None, ("yz", "c"), None)
    return jax.shard_map(body, mesh=fine, in_specs=(rows, P(), P()), out_specs=rows, check_vma=False)
```

time: 115 us -> 111 us (0.965)
  waiting for transfers between devices: 35 us -> 32.8 us
  Pallas kernels: 16.5 us -> 15.2 us
    ppermute x2, waiting for transfers between devices: 3.96 us -> 1.66 us  [exchange(): parts.append(lax.ppermute(own[start:start + size], 'x', pairs))]
  transfers between devices with their start and end apart: 4 -> 4, of which waited for: 4 -> 3; matrix products, arithmetic and copies ran while one was open for 1% -> 1% of each run, Pallas kernels for 3% -> 3%
where the time goes in v5:
time: 111 us
  blocking collectives  47 us (42%)
  waiting for transfers between devices  32.8 us (30%)
  Pallas kernels  15.2 us (14%)
  starting transfers between devices  13.3 us (12%)
  local copies, waits for them, and re-layouts  1.9 us (2%)
    all_to_all x1, blocking collectives, body(): lax.all_to_all(outgoing, 'yz', split_axis=0, concat_axis=0, tiled=True)  47 us
    all_to_all x1, waiting for transfers between devices, body(): lax.all_to_all(done.reshape(chips, rows_dev, width), 'yz', split_axis=0,...  29.4 us
    pallas_call x1, Pallas kernels, refresh(): pl.pallas_call(refresh_kernel, out_shape=jax.ShapeDtypeStruct((rows, widt...  7.2 us
    ppermute x2, starting transfers between devices, exchange(): parts.append(lax.ppermute(own[start:start + size], 'x', pairs))  5.84 us
    all_to_all x1, starting transfers between devices, body(): lax.all_to_all(done.reshape(chips, rows_dev, width), 'yz', split_axis=0,...  5.57 us
    pallas_call x1, Pallas kernels, make_plan(): pl.pallas_call(plan_kernel, out_shape=(jax.ShapeDtypeStruct((places,) + g...  3.36 us
  transfers between devices with their start and end apart: 4, of which 3 were waited for; matrix products, arithmetic and copies ran while one was open for 1% of the time, Pallas kernels for 3%

profile of v5, /device:TPU:22, one launch (start us, length us, event | category | flops | bytes accessed | tf_op | source)
XLA Modules:
  0.0 111.0 jit_solution(6296375586572363790)
XLA Ops:
  0.0 0.1 pad_add_fusion.side_ref
  0.1 3.4 %shard_map.44 = (bf16[64,8,1024]{2,1,0:T(8,128)(2,1)}, s32[8,128]{1,0:T(8,128)S(1)}) custom-call(s32[2]{0:T(128)S(1)} %pad_add_fusion.side_ref, s32[1,128]{1,0:T(1,128)} %bitcast.10, s32[1,128]{1,0:T(1,128)} %bitcast.11, bf16[128,8,1024]{2,1,0:T(8,128)(2,1)} %grads_ref.1), custom_call_target="tpu_custom_call" | custom-call | tf_op jit(solution)/shard_map/pallas_call | solution.py:62
  3.4 47.0 %all_to_all.10 = bf16[64,8,1024]{2,1,0:T(8,128)(2,1)S(1)} all-to-all(bf16[64,8,1024]{2,1,0:T(8,128)(2,1)} %get-tuple-element.79), channel_id=1, replica_groups=mesh['yz'=64,'c'=2,'x'=4] {'yz'}, dimensions={0} | all-to-all | bytes 2097152 | tf_op jit(solution)/shard_map/all_to_all | solution.py:278
  50.4 1.9 %collective-permute-start.11 = (bf16[512,1024]{1,0:T(8,128)(2,1)S(1)}, bf16[512,1024]{1,0:T(8,128)(2,1)S(1)}, u32[]{:S(2)}, u32[]{:S(2)}) collective-permute-start(bf16[512,1024]{1,0:T(8,128)(2,1)S(1)} %bitcast.7), channel_id=1, source_target_pairs={{0,4},{4,0},{1,5},{5,1},{2,6},{6,2},{3,7},{7,3},{8,12},{12,8},{9,1... | collective-permute-start | bytes 3145736 | tf_op jit(solution)/shard_map/ppermute | solution.py:280
  52.3 0.9 shard_map.45.gram_ref
  53.2 1.7 %collective-permute-done.11.theirs_ref = bf16[512,1024]{1,0:T(8,128)(2,1)S(1)} collective-permute-done((bf16[512,1024]{1,0:T(8,128)(2,1)S(1)}, bf16[512,1024]{1,0:T(8,128)(2,1)S(1)}, u32[]{:S(2)}, u32[]{:S(2)}) %collective-permute-start.11) | collective-permute-done | bytes 1048608 | tf_op jit(solution)/shard_map/ppermute | solution.py:280
  55.0 7.2 %shard_map.46 = bf16[512,1024]{1,0:T(8,128)(2,1)} custom-call(s32[2]{0:T(128)S(1)} %pad_add_fusion.side_ref, s32[8,128]{1,0:T(8,128)S(1)} %get-tuple-element.78.plan_ref, bf16[512,1024]{1,0:T(8,128)(2,1)S(1)} %bitcast.9, bf16[512,1024]{1,0:T(8,128)(2,1)S(1)} %collective-permute-done.11.theirs_ref, f32[1024,1024]{1,0:T(8,128)S(1)} %shard_map.45.gram_ref), custom_call_target="tpu_custom_call" | custom-call | flops 4294967296 | bytes 3145728 | tf_op jit(solution)/shard_map/pallas_call | solution.py:180
  62.2 5.6 %all-to-all-start.1 = ((bf16[64,8,1024]{2,1,0:T(8,128)(2,1)}), bf16[64,8,1024]{2,1,0:T(8,128)(2,1)S(1)}, u32[]{:S(2)}, u32[]{:S(2)}) async-start(bf16[64,8,1024]{2,1,0:T(8,128)(2,1)} %bitcast.6), calls=%async_computation.1 | async-start | bytes 2097152 | tf_op jit(solution)/shard_map/all_to_all | solution.py:282
  67.8 0.6 slice.36
  69.0 29.4 %all-to-all-done.1 = bf16[64,8,1024]{2,1,0:T(8,128)(2,1)S(1)} async-done(((bf16[64,8,1024]{2,1,0:T(8,128)(2,1)}), bf16[64,8,1024]{2,1,0:T(8,128)(2,1)S(1)}, u32[]{:S(2)}, u32[]{:S(2)}) %all-to-all-start.1) | async-done | bytes 1048608 | tf_op jit(solution)/shard_map/all_to_all | solution.py:282
  98.4 12.6 %conditional.1 = (bf16[128,8,1024]{2,1,0:T(8,128)(2,1)}) conditional(s32[]{:T(128)} %bitcast.4, (s32[2]{0:T(128)S(1)}, s32[8,128]{1,0:T(8,128)S(1)}, bf16[64,8,1024]{2,1,0:T(8,128)(2,1)S(1)}) %tuple.26, (s32[2]{0:T(128)S(1)}, s32[8,128]{1,0:T(8,128)S(1)}, bf16[64,8,1024]{2,1,0:T(8,128)(2,1)S(1)}) %tuple.26, ...), branch_computations={%region_0.1_spmd, %region_1.2_spmd, %region_2.3_spmd, %region_3.4_... | conditional | bytes 14680208 | solution.py:286
  98.4 2.4 %collective-permute-start.1 = (bf16[13,8,1024]{2,1,0:T(8,128)(2,1)S(1)}, bf16[13,8,1024]{2,1,0:T(8,128)(2,1)S(1)}, u32[]{:S(2)}, u32[]{:S(2)}) collective-permute-start(bf16[13,8,1024]{2,1,0:T(8,128)(2,1)S(1)} %slice.25), channel_id=1, source_target_pairs={{0,1},{1,2},{2,3},{3,0},{4,5},{5,6},{6,7},{7,4},{8,9},{9,10},{10,1... | collective-permute-start | bytes 638984 | tf_op jit(solution)/shard_map/cond/branch_2_fun/ppermute | solution.py:266
  100.8 3.5 %collective-permute-start.2 = (bf16[3,8,1024]{2,1,0:T(8,128)(2,1)S(1)}, bf16[3,8,1024]{2,1,0:T(8,128)(2,1)S(1)}, u32[]{:S(2)}, u32[]{:S(2)}) collective-permute-start(bf16[3,8,1024]{2,1,0:T(8,128)(2,1)S(1)} %slice.26), channel_id=1, source_target_pairs={{0,3},{1,0},{2,1},{3,2},{4,7},{5,4},{6,5},{7,6},{8,11},{9,8},{10,9... | collective-permute-start | bytes 147464 | tf_op jit(solution)/shard_map/cond/branch_2_fun/ppermute | solution.py:266
  104.3 2.1 %branch_2_fun.2.held_ref = bf16[128,8,1024]{2,1,0:T(8,128)(2,1)} custom-call(s32[2]{0:T(128)S(1)} %get-tuple-element.61.side_ref, s32[8,128]{1,0:T(8,128)S(1)} %get-tuple-element.62.plan_ref, bf16[64,8,1024]{2,1,0:T(8,128)(2,1)S(1)} %get-tuple-element.63.own_ref), custom_call_target="tpu_custom_call" | custom-call | bytes 2097152 | tf_op jit(solution)/shard_map/cond/branch_2_fun/pallas_call | solution.py:222
  106.3 1.7 %collective-permute-done.2.refs_1_ = bf16[3,8,1024]{2,1,0:T(8,128)(2,1)S(1)} collective-permute-done((bf16[3,8,1024]{2,1,0:T(8,128)(2,1)S(1)}, bf16[3,8,1024]{2,1,0:T(8,128)(2,1)S(1)}, u32[]{:S(2)}, u32[]{:S(2)}) %collective-permute-start.2) | collective-permute-done | bytes 49184 | tf_op jit(solution)/shard_map/cond/branch_2_fun/ppermute | solution.py:266
  108.0 0.0 copy-start.10
  108.0 0.0 collective-permute-done.1.refs_0_
  108.0 0.6 copy-done.10
  108.6 0.0 copy-start.6
  108.6 0.7 copy-done.6
  109.3 1.7 %branch_2_fun.3 = bf16[128,8,1024]{2,1,0:T(8,128)(2,1)} custom-call(s32[2]{0:T(128)S(1)} %get-tuple-element.61.side_ref, s32[8,128]{1,0:T(8,128)S(1)} %get-tuple-element.62.plan_ref, bf16[128,8,1024]{2,1,0:T(8,128)(2,1)} %branch_2_fun.2.held_ref, bf16[13,8,1024]{2,1,0:T(8,128)(2,1)} %copy-done.6, ...), custom_call_target="tpu_custom_call", output_to_operand_aliasing={{}: (2, {})} | custom-call | bytes 524288 | tf_op jit(solution)/shard_map/cond/branch_2_fun/pallas_call | solution.py:249
  (2 shorter events, 0.0 us)
Async XLA Ops:
  50.4 4.5 %collective-permute-start.11 = (bf16[512,1024]{1,0:T(8,128)(2,1)S(1)}, bf16[512,1024]{1,0:T(8,128)(2,1)S(1)}, u32[]{:S(2)}, u32[]{:S(2)}) collective-permute-start(bf16[512,1024]{1,0:T(8,128)(2,1)S(1)} %bitcast.7), channel_id=1, source_target_pairs={{0,4},{4,0},{1,5},{5,1},{2,6},{6,2},{3,7},{7,3},{8,12},{12,8},{9,1... | collective-permute-start | bytes 3145736 | tf_op jit(solution)/shard_map/ppermute | solution.py:280
  62.2 36.2 %all-to-all-start.1 = ((bf16[64,8,1024]{2,1,0:T(8,128)(2,1)}), bf16[64,8,1024]{2,1,0:T(8,128)(2,1)S(1)}, u32[]{:S(2)}, u32[]{:S(2)}) async-start(bf16[64,8,1024]{2,1,0:T(8,128)(2,1)} %bitcast.6), calls=%async_computation.1 | async-start | bytes 2097152 | tf_op jit(solution)/shard_map/all_to_all | solution.py:282
  98.4 9.6 %collective-permute-start.1 = (bf16[13,8,1024]{2,1,0:T(8,128)(2,1)S(1)}, bf16[13,8,1024]{2,1,0:T(8,128)(2,1)S(1)}, u32[]{:S(2)}, u32[]{:S(2)}) collective-permute-start(bf16[13,8,1024]{2,1,0:T(8,128)(2,1)S(1)} %slice.25), channel_id=1, source_target_pairs={{0,1},{1,2},{2,3},{3,0},{4,5},{5,6},{6,7},{7,4},{8,9},{9,10},{10,1... | collective-permute-start | bytes 638984 | tf_op jit(solution)/shard_map/cond/branch_2_fun/ppermute | solution.py:266
  100.8 7.2 %collective-permute-start.2 = (bf16[3,8,1024]{2,1,0:T(8,128)(2,1)S(1)}, bf16[3,8,1024]{2,1,0:T(8,128)(2,1)S(1)}, u32[]{:S(2)}, u32[]{:S(2)}) collective-permute-start(bf16[3,8,1024]{2,1,0:T(8,128)(2,1)S(1)} %slice.26), channel_id=1, source_target_pairs={{0,3},{1,0},{2,1},{3,2},{4,7},{5,4},{6,5},{7,6},{8,11},{9,8},{10,9... | collective-permute-start | bytes 147464 | tf_op jit(solution)/shard_map/cond/branch_2_fun/ppermute | solution.py:266
  108.0 0.6 copy-start.10
  108.6 0.7 copy-start.6

commit v6 on v5

--- a/solution.py
+++ b/solution.py
@@ -20,10 +20,14 @@
 
 
 def plan_kernel(
-    side_ref, owners_ref, counts_ref, grads_ref, out_ref, plan_ref, whole, rows_ref, plan_sem, whole_sem
+    side_ref, owners_ref, counts_ref, grads_ref, out_ref, plan_ref, whole, rows_ref, plan_sem, whole_sems
 ):
-    load = pltpu.make_async_copy(grads_ref, whole, whole_sem)
-    load.start()
+    piece = whole.shape[0] // whole_sems.shape[0]
+    loads = []
+    for p in range(whole_sems.shape[0]):
+        part = pl.ds(p * piece, piece)
+        loads.append(pltpu.make_async_copy(grads_ref.at[part], whole.at[part], whole_sems.at[p]))
+        loads[-1].start()
     places, blocks = out_ref.shape[0], owners_ref.shape[1]
     square = (blocks, blocks)
     i = lax.broadcasted_iota(jnp.int32, square, 0)
@@ -47,7 +51,8 @@
     to_scalars = pltpu.make_async_copy(rows_ref, plan_ref, plan_sem)
     to_scalars.start()
     to_scalars.wait()
-    load.wait()
+    for load in loads:
+        load.wait()
     more = plan_ref[MORE, 0]
     first = side_ref[0] * more
     for place in range(places):
@@ -71,8 +76,9 @@
             pltpu.VMEM(grads.shape, grads.dtype),
             pltpu.VMEM((8, blocks), jnp.int32),
             pltpu.SemaphoreType.DMA,
-            pltpu.SemaphoreType.DMA,
+            pltpu.SemaphoreType.DMA((8,)),
         ],
+        compiler_params=pltpu.CompilerParams(vmem_limit_bytes=8 * 2**20),
     )(side, owners.reshape(1, -1), counts.reshape(1, -1), grads)
 
 
@@ -94,7 +100,7 @@
         out_shape=jax.ShapeDtypeStruct((width, width), jnp.float32),
         in_specs=[vmem],
         out_specs=vmem,
-        compiler_params=pltpu.CompilerParams(vmem_limit_bytes=24 * 2**20),
+        compiler_params=pltpu.CompilerParams(vmem_limit_bytes=12 * 2**20),
         cost_estimate=pl.CostEstimate(
             flops=2 * count * width**2, bytes_accessed=2 * count * width + 4 * width**2, transcendentals=0
         ),
@@ -189,7 +195,7 @@
             pltpu.VMEM((1, width), jnp.float32),
             pltpu.VMEM((rows, width), jnp.float32),
         ],
-        compiler_params=pltpu.CompilerParams(vmem_limit_bytes=44 * 2**20),
+        compiler_params=pltpu.CompilerParams(vmem_limit_bytes=24 * 2**20),
         cost_estimate=pl.CostEstimate(flops=4 * width**3, bytes_accessed=6 * rows * width, transcendentals=0),
     )(side, plan, mine, theirs, mine_gram)
 
@@ -225,6 +231,7 @@
         in_specs=[smem, smem, pl.BlockSpec(memory_space=pltpu.VMEM)],
         out_specs=pl.BlockSpec(memory_space=pltpu.HBM),
         scratch_shapes=[pltpu.VMEM(shape, own.dtype), pltpu.SemaphoreType.DMA((8,))],
+        compiler_params=pltpu.CompilerParams(vmem_limit_bytes=8 * 2**20),
         cost_estimate=pl.CostEstimate(flops=0, bytes_accessed=4 * own.size, transcendentals=0),
     )(side, plan, own)
 
@@ -253,6 +260,7 @@
         out_specs=hbm,
         scratch_shapes=[pltpu.SemaphoreType.DMA((len(parts),))],
         input_output_aliases={2: 0},
+        compiler_params=pltpu.CompilerParams(vmem_limit_bytes=6 * 2**20),
         cost_estimate=pl.CostEstimate(flops=0, bytes_accessed=4 * size, transcendentals=0),
     )(side, plan, held, *parts)
 

time: 111 us -> 113 us (1.018)
  local copies, waits for them, and re-layouts: 1.9 us -> 3.53 us
  waiting for transfers between devices: 32.8 us -> 34.1 us
  Pallas kernels: 15.2 us -> 14 us
    unnamed x0 -> x6, local copies, waits for them, and re-layouts: none -> 2.9 us
    ppermute x2, waiting for transfers between devices: 1.66 us -> 3.06 us  [exchange(): parts.append(lax.ppermute(own[start:start + size], 'x', pairs))]
    cond x4 -> x0, local copies, waits for them, and re-layouts: 1.3 us -> none
where the time goes in v6:
time: 113 us
  blocking collectives  46.8 us (41%)
  waiting for transfers between devices  34.1 us (30%)
  Pallas kernels  14 us (12%)
  starting transfers between devices  13.3 us (12%)
  local copies, waits for them, and re-layouts  3.53 us (3%)
    all_to_all x1, blocking collectives, body(): lax.all_to_all(outgoing, 'yz', split_axis=0, concat_axis=0, tiled=True)  46.8 us
    all_to_all x1, waiting for transfers between devices, body(): lax.all_to_all(done.reshape(chips, rows_dev, width), 'yz', split_axis=0,...  29.3 us
    pallas_call x1, Pallas kernels, refresh(): pl.pallas_call(refresh_kernel, out_shape=jax.ShapeDtypeStruct((rows, widt...  7.21 us
    ppermute x2, starting transfers between devices, exchange(): parts.append(lax.ppermute(own[start:start + size], 'x', pairs))  5.84 us
    all_to_all x1, starting transfers between devices, body(): lax.all_to_all(done.reshape(chips, rows_dev, width), 'yz', split_axis=0,...  5.57 us
    ppermute x2, waiting for transfers between devices, exchange(): parts.append(lax.ppermute(own[start:start + size], 'x', pairs))  3.06 us
    unnamed x6, local copies, waits for them, and re-layouts  2.9 us
    pallas_call x1, Pallas kernels, make_plan(): pl.pallas_call(plan_kernel, out_shape=(jax.ShapeDtypeStruct((places,) + g...  2.46 us
  transfers between devices with their start and end apart: 4, of which 3 were waited for; matrix products, arithmetic and copies ran while one was open for 1% of the time, Pallas kernels for 3%

profile of v6, /device:TPU:22, one launch (start us, length us, event | category | flops | bytes accessed | tf_op | source)
XLA Modules:
  0.0 112.6 jit_solution(15417994779190902370)
XLA Ops:
  0.0 0.1 pad_add_fusion.side_ref
  0.1 0.0 copy-start
  0.1 1.6 %copy-done = bf16[128,8,1024]{2,1,0:T(8,128)(2,1)S(1)} copy-done((bf16[128,8,1024]{2,1,0:T(8,128)(2,1)S(1)}, bf16[128,8,1024]{2,1,0:T(8,128)(2,1)}, u32[]{:S(2)}) %copy-start) | copy-done | bytes 2097176
  1.7 0.0 copy-start.1
  1.7 0.7 copy-done.1
  2.3 0.0 copy-start.2
  2.3 0.7 copy-done.2
  3.0 2.5 %shard_map.44 = (bf16[64,8,1024]{2,1,0:T(8,128)(2,1)S(1)}, s32[8,128]{1,0:T(8,128)S(1)}) custom-call(s32[2]{0:T(128)S(1)} %pad_add_fusion.side_ref, s32[1,128]{1,0:T(1,128)S(1)} %bitcast.10, s32[1,128]{1,0:T(1,128)S(1)} %bitcast.11, bf16[128,8,1024]{2,1,0:T(8,128)(2,1)S(1)} %copy-done), custom_call_target="tpu_custom_call" | custom-call | tf_op jit(solution)/shard_map/pallas_call | solution.py:67
  5.4 46.8 %all_to_all.10 = bf16[64,8,1024]{2,1,0:T(8,128)(2,1)S(1)} all-to-all(bf16[64,8,1024]{2,1,0:T(8,128)(2,1)S(1)} %get-tuple-element.79), channel_id=1, replica_groups=mesh['yz'=64,'c'=2,'x'=4] {'yz'}, dimensions={0} | all-to-all | bytes 2097152 | tf_op jit(solution)/shard_map/all_to_all | solution.py:286
  52.2 1.9 %collective-permute-start.11 = (bf16[512,1024]{1,0:T(8,128)(2,1)S(1)}, bf16[512,1024]{1,0:T(8,128)(2,1)S(1)}, u32[]{:S(2)}, u32[]{:S(2)}) collective-permute-start(bf16[512,1024]{1,0:T(8,128)(2,1)S(1)} %bitcast.7), channel_id=1, source_target_pairs={{0,4},{4,0},{1,5},{5,1},{2,6},{6,2},{3,7},{7,3},{8,12},{12,8},{9,1... | collective-permute-start | bytes 3145736 | tf_op jit(solution)/shard_map/ppermute | solution.py:288
  54.1 0.9 shard_map.45.gram_ref
  55.0 1.7 %collective-permute-done.11.theirs_ref = bf16[512,1024]{1,0:T(8,128)(2,1)S(1)} collective-permute-done((bf16[512,1024]{1,0:T(8,128)(2,1)S(1)}, bf16[512,1024]{1,0:T(8,128)(2,1)S(1)}, u32[]{:S(2)}, u32[]{:S(2)}) %collective-permute-start.11) | collective-permute-done | bytes 1048608 | tf_op jit(solution)/shard_map/ppermute | solution.py:288
  56.8 7.2 %shard_map.46 = bf16[512,1024]{1,0:T(8,128)(2,1)} custom-call(s32[2]{0:T(128)S(1)} %pad_add_fusion.side_ref, s32[8,128]{1,0:T(8,128)S(1)} %get-tuple-element.78.plan_ref, bf16[512,1024]{1,0:T(8,128)(2,1)S(1)} %bitcast.9, bf16[512,1024]{1,0:T(8,128)(2,1)S(1)} %collective-permute-done.11.theirs_ref, f32[1024,1024]{1,0:T(8,128)S(1)} %shard_map.45.gram_ref), custom_call_target="tpu_custom_call" | custom-call | flops 4294967296 | bytes 3145728 | tf_op jit(solution)/shard_map/pallas_call | solution.py:186
  64.0 5.6 %all-to-all-start.1 = ((bf16[64,8,1024]{2,1,0:T(8,128)(2,1)}), bf16[64,8,1024]{2,1,0:T(8,128)(2,1)S(1)}, u32[]{:S(2)}, u32[]{:S(2)}) async-start(bf16[64,8,1024]{2,1,0:T(8,128)(2,1)} %bitcast.6), calls=%async_computation.1 | async-start | bytes 2097152 | tf_op jit(solution)/shard_map/all_to_all | solution.py:290
  69.5 0.6 slice.36
  70.8 29.3 %all-to-all-done.1 = bf16[64,8,1024]{2,1,0:T(8,128)(2,1)S(1)} async-done(((bf16[64,8,1024]{2,1,0:T(8,128)(2,1)}), bf16[64,8,1024]{2,1,0:T(8,128)(2,1)S(1)}, u32[]{:S(2)}, u32[]{:S(2)}) %all-to-all-start.1) | async-done | bytes 1048608 | tf_op jit(solution)/shard_map/all_to_all | solution.py:290
  100.2 12.4 %conditional.1 = (bf16[128,8,1024]{2,1,0:T(8,128)(2,1)}) conditional(s32[]{:T(128)} %bitcast.4, (s32[2]{0:T(128)S(1)}, s32[8,128]{1,0:T(8,128)S(1)}, bf16[64,8,1024]{2,1,0:T(8,128)(2,1)S(1)}) %tuple.26, (s32[2]{0:T(128)S(1)}, s32[8,128]{1,0:T(8,128)S(1)}, bf16[64,8,1024]{2,1,0:T(8,128)(2,1)S(1)}) %tuple.26, ...), branch_computations={%region_0.1_spmd, %region_1.2_spmd, %region_2.3_spmd, %region_3.4_... | conditional | bytes 10485848 | solution.py:294
  100.2 2.4 %collective-permute-start.5 = (bf16[21,8,1024]{2,1,0:T(8,128)(2,1)S(1)}, bf16[21,8,1024]{2,1,0:T(8,128)(2,1)S(1)}, u32[]{:S(2)}, u32[]{:S(2)}) collective-permute-start(bf16[21,8,1024]{2,1,0:T(8,128)(2,1)S(1)} %slice.29), channel_id=1, source_target_pairs={{0,1},{1,2},{2,3},{3,0},{4,5},{5,6},{6,7},{7,4},{8,9},{9,10},{10,1... | collective-permute-start | bytes 1032200 | tf_op jit(solution)/shard_map/cond/branch_4_fun/ppermute | solution.py:274
  102.6 3.5 %collective-permute-start.6 = (bf16[11,8,1024]{2,1,0:T(8,128)(2,1)S(1)}, bf16[11,8,1024]{2,1,0:T(8,128)(2,1)S(1)}, u32[]{:S(2)}, u32[]{:S(2)}) collective-permute-start(bf16[11,8,1024]{2,1,0:T(8,128)(2,1)S(1)} %slice.30), channel_id=1, source_target_pairs={{0,3},{1,0},{2,1},{3,2},{4,7},{5,4},{6,5},{7,6},{8,11},{9,8},{10,9... | collective-permute-start | bytes 540680 | tf_op jit(solution)/shard_map/cond/branch_4_fun/ppermute | solution.py:274
  106.1 2.1 %branch_4_fun.2.held_ref = bf16[128,8,1024]{2,1,0:T(8,128)(2,1)} custom-call(s32[2]{0:T(128)S(1)} %get-tuple-element.67.side_ref, s32[8,128]{1,0:T(8,128)S(1)} %get-tuple-element.68.plan_ref, bf16[64,8,1024]{2,1,0:T(8,128)(2,1)S(1)} %get-tuple-element.69.own_ref), custom_call_target="tpu_custom_call" | custom-call | bytes 2097152 | tf_op jit(solution)/shard_map/cond/branch_4_fun/pallas_call | solution.py:228
  108.1 3.1 %collective-permute-done.6.refs_1_ = bf16[11,8,1024]{2,1,0:T(8,128)(2,1)S(1)} collective-permute-done((bf16[11,8,1024]{2,1,0:T(8,128)(2,1)S(1)}, bf16[11,8,1024]{2,1,0:T(8,128)(2,1)S(1)}, u32[]{:S(2)}, u32[]{:S(2)}) %collective-permute-start.6) | collective-permute-done | bytes 180256 | tf_op jit(solution)/shard_map/cond/branch_4_fun/ppermute | solution.py:274
  111.2 0.0 collective-permute-done.5.refs_0_
  111.2 1.4 %branch_4_fun.3 = bf16[128,8,1024]{2,1,0:T(8,128)(2,1)} custom-call(s32[2]{0:T(128)S(1)} %get-tuple-element.67.side_ref, s32[8,128]{1,0:T(8,128)S(1)} %get-tuple-element.68.plan_ref, bf16[128,8,1024]{2,1,0:T(8,128)(2,1)} %branch_4_fun.2.held_ref, bf16[21,8,1024]{2,1,0:T(8,128)(2,1)S(1)} %collective-permute-done.5.refs_0_, ...), custom_call_target="tpu_custom_call", output_to_operand_aliasing={{}: (2, {})} | custom-call | bytes 1048576 | tf_op jit(solution)/shard_map/cond/branch_4_fun/pallas_call | solution.py:256
  (2 shorter events, 0.0 us)
Async XLA Ops:
  0.1 1.6 %copy-start = (bf16[128,8,1024]{2,1,0:T(8,128)(2,1)S(1)}, bf16[128,8,1024]{2,1,0:T(8,128)(2,1)}, u32[]{:S(2)}) copy-start(bf16[128,8,1024]{2,1,0:T(8,128)(2,1)} %grads_ref.1) | copy-start | bytes 6291460
  1.7 0.7 copy-start.1
  2.3 0.7 copy-start.2
  52.2 4.5 %collective-permute-start.11 = (bf16[512,1024]{1,0:T(8,128)(2,1)S(1)}, bf16[512,1024]{1,0:T(8,128)(2,1)S(1)}, u32[]{:S(2)}, u32[]{:S(2)}) collective-permute-start(bf16[512,1024]{1,0:T(8,128)(2,1)S(1)} %bitcast.7), channel_id=1, source_target_pairs={{0,4},{4,0},{1,5},{5,1},{2,6},{6,2},{3,7},{7,3},{8,12},{12,8},{9,1... | collective-permute-start | bytes 3145736 | tf_op jit(solution)/shard_map/ppermute | solution.py:288
  64.0 36.2 %all-to-all-start.1 = ((bf16[64,8,1024]{2,1,0:T(8,128)(2,1)}), bf16[64,8,1024]{2,1,0:T(8,128)(2,1)S(1)}, u32[]{:S(2)}, u32[]{:S(2)}) async-start(bf16[64,8,1024]{2,1,0:T(8,128)(2,1)} %bitcast.6), calls=%async_computation.1 | async-start | bytes 2097152 | tf_op jit(solution)/shard_map/all_to_all | solution.py:290
  100.2 11.0 %collective-permute-start.5 = (bf16[21,8,1024]{2,1,0:T(8,128)(2,1)S(1)}, bf16[21,8,1024]{2,1,0:T(8,128)(2,1)S(1)}, u32[]{:S(2)}, u32[]{:S(2)}) collective-permute-start(bf16[21,8,1024]{2,1,0:T(8,128)(2,1)S(1)} %slice.29), channel_id=1, source_target_pairs={{0,1},{1,2},{2,3},{3,0},{4,5},{5,6},{6,7},{7,4},{8,9},{9,10},{10,1... | collective-permute-start | bytes 1032200 | tf_op jit(solution)/shard_map/cond/branch_4_fun/ppermute | solution.py:274
  102.6 8.6 %collective-permute-start.6 = (bf16[11,8,1024]{2,1,0:T(8,128)(2,1)S(1)}, bf16[11,8,1024]{2,1,0:T(8,128)(2,1)S(1)}, u32[]{:S(2)}, u32[]{:S(2)}) collective-permute-start(bf16[11,8,1024]{2,1,0:T(8,128)(2,1)S(1)} %slice.30), channel_id=1, source_target_pairs={{0,3},{1,0},{2,1},{3,2},{4,7},{5,4},{6,5},{7,6},{8,11},{9,8},{10,9... | collective-permute-start | bytes 540680 | tf_op jit(solution)/shard_map/cond/branch_4_fun/ppermute | solution.py:274

commit v7 on v6

--- a/solution.py
+++ b/solution.py
@@ -10,7 +10,10 @@
 
 EPS = 1e-06
 TILE = 256
-HANDED = ((0, 0), (8, 0), (13, 3), (17, 7), (21, 11), (29, 19), (37, 27))
+HANDED = (
+    *((0, 0), (4, 0), (8, 0), (12, 0), (16, 0), (15, 5)),
+    *((17, 7), (19, 9), (21, 11), (25, 15), (29, 19), (37, 27)),
+)
 BLOCK, RANK, TIER, MORE, COUNT = range(5)
 
 
@@ -20,7 +23,7 @@
 
 
 def plan_kernel(
-    side_ref, owners_ref, counts_ref, grads_ref, out_ref, plan_ref, whole, rows_ref, plan_sem, whole_sems
+    side_ref, owners_ref, counts_ref, grads_ref, out_ref, plan_ref, tier_ref, whole, rows_ref, plan_sem, whole_sems
 ):
     piece = whole.shape[0] // whole_sems.shape[0]
     loads = []
@@ -53,6 +56,7 @@
     to_scalars.wait()
     for load in loads:
         load.wait()
+    tier_ref[0] = plan_ref[TIER, 0]
     more = plan_ref[MORE, 0]
     first = side_ref[0] * more
     for place in range(places):
@@ -67,11 +71,12 @@
     return pl.pallas_call(
         plan_kernel,
         out_shape=(
-            jax.ShapeDtypeStruct((places,) + grads.shape[1:], grads.dtype),
+            pltpu.VMEM((places,) + grads.shape[1:], grads.dtype),
             jax.ShapeDtypeStruct((8, blocks), jnp.int32),
+            jax.ShapeDtypeStruct((1,), jnp.int32),
         ),
         in_specs=[smem, vmem, vmem, pl.BlockSpec(memory_space=pltpu.HBM)],
-        out_specs=(vmem, smem),
+        out_specs=(vmem, smem, smem),
         scratch_shapes=[
             pltpu.VMEM(grads.shape, grads.dtype),
             pltpu.VMEM((8, blocks), jnp.int32),
@@ -79,7 +84,13 @@
             pltpu.SemaphoreType.DMA((8,)),
         ],
         compiler_params=pltpu.CompilerParams(vmem_limit_bytes=8 * 2**20),
-    )(side, owners.reshape(1, -1), counts.reshape(1, -1), grads)
+    )(
+        side,
+        *(
+            pltpu.with_memory_space_constraint(array, pltpu.HBM)
+            for array in (owners.reshape(1, -1), counts.reshape(1, -1), grads)
+        ),
+    )
 
 
 def first_dims(a, b):
@@ -282,7 +293,7 @@
     chips = lax.axis_size("yz")
     side = jnp.stack([lax.axis_index("x") % 2, lax.axis_index("yz")]).astype(jnp.int32)
 
-    outgoing, plan = make_plan(side, owners, counts, grads, chips)
+    outgoing, plan, tier = make_plan(side, owners, counts, grads, chips)
     mine = lax.all_to_all(outgoing, "yz", split_axis=0, concat_axis=0, tiled=True)
     mine = mine.reshape(chips * rows_dev, width)
     theirs = lax.ppermute(mine, "c", [(0, 1), (1, 0)])
@@ -291,7 +302,7 @@
         done.reshape(chips, rows_dev, width), "yz", split_axis=0, concat_axis=0, tiled=True
     )
     branches = [functools.partial(exchange, handed) for handed in HANDED]
-    return lax.switch(plan[TIER, 0], branches, side, plan, own)
+    return lax.switch(tier[0], branches, side, plan, own)
 
 
 def solution(mesh):

time: 113 us -> 110 us (0.973)
  local copies, waits for them, and re-layouts: 3.53 us -> 0.03 us
    unnamed x6 -> x0, local copies, waits for them, and re-layouts: 2.9 us -> none
  transfers between devices with their start and end apart: 4 -> 4, of which waited for: 3 -> 3; matrix products, arithmetic and copies ran while one was open for 1% -> 0% of each run, Pallas kernels for 3% -> 3%
where the time goes in v7:
time: 110 us
  blocking collectives  46.8 us (43%)
  waiting for transfers between devices  34.1 us (31%)
  Pallas kernels  14.5 us (13%)
  starting transfers between devices  13.3 us (12%)
    all_to_all x1, blocking collectives, body(): lax.all_to_all(outgoing, 'yz', split_axis=0, concat_axis=0, tiled=True)  46.8 us
    all_to_all x1, waiting for transfers between devices, body(): lax.all_to_all(done.reshape(chips, rows_dev, width), 'yz', split_axis=0,...  30 us
    pallas_call x1, Pallas kernels, refresh(): pl.pallas_call(refresh_kernel, out_shape=jax.ShapeDtypeStruct((rows, widt...  7.2 us
    ppermute x2, starting transfers between devices, exchange(): parts.append(lax.ppermute(own[start:start + size], 'x', pairs))  5.84 us
    all_to_all x1, starting transfers between devices, body(): lax.all_to_all(done.reshape(chips, rows_dev, width), 'yz', split_axis=0,...  5.58 us
    pallas_call x1, Pallas kernels, make_plan(): pl.pallas_call(plan_kernel, out_shape=(pltpu.VMEM((places,) + grads.shape...  3 us
    ppermute x2, waiting for transfers between devices, exchange(): parts.append(lax.ppermute(own[start:start + size], 'x', pairs))  2.39 us
  transfers between devices with their start and end apart: 4, of which 3 were waited for; matrix products, arithmetic and copies ran while one was open for 0% of the time, Pallas kernels for 3%

profile of v7, /device:TPU:22, one launch (start us, length us, event | category | flops | bytes accessed | tf_op | source)
XLA Modules:
  0.0 109.7 jit_solution(13067712892121616301)
XLA Ops:
  0.0 0.1 pad_add_fusion.side_ref
  0.1 3.0 %shard_map.49 = (bf16[64,8,1024]{2,1,0:T(8,128)(2,1)S(1)}, s32[8,128]{1,0:T(8,128)S(1)}, s32[1]{0:T(128)}) custom-call(s32[2]{0:T(128)S(1)} %pad_add_fusion.side_ref, s32[1,128]{1,0:T(1,128)} %bitcast.10, s32[1,128]{1,0:T(1,128)} %bitcast.11, bf16[128,8,1024]{2,1,0:T(8,128)(2,1)} %grads_ref.1), custom_call_target="tpu_custom_call" | custom-call | tf_op jit(solution)/shard_map/pallas_call | solution.py:71
  3.1 46.8 %all_to_all.10 = bf16[64,8,1024]{2,1,0:T(8,128)(2,1)S(1)} all-to-all(bf16[64,8,1024]{2,1,0:T(8,128)(2,1)S(1)} %get-tuple-element.131), channel_id=1, replica_groups=mesh['yz'=64,'c'=2,'x'=4] {'yz'}, dimensions={0} | all-to-all | bytes 2097152 | tf_op jit(solution)/shard_map/all_to_all | solution.py:297
  49.9 1.9 %collective-permute-start.18 = (bf16[512,1024]{1,0:T(8,128)(2,1)S(1)}, bf16[512,1024]{1,0:T(8,128)(2,1)S(1)}, u32[]{:S(2)}, u32[]{:S(2)}) collective-permute-start(bf16[512,1024]{1,0:T(8,128)(2,1)S(1)} %bitcast.7), channel_id=1, source_target_pairs={{0,4},{4,0},{1,5},{5,1},{2,6},{6,2},{3,7},{7,3},{8,12},{12,8},{9,1... | collective-permute-start | bytes 3145736 | tf_op jit(solution)/shard_map/ppermute | solution.py:299
  51.8 0.9 shard_map.50.gram_ref
  52.7 1.7 %collective-permute-done.18.theirs_ref = bf16[512,1024]{1,0:T(8,128)(2,1)S(1)} collective-permute-done((bf16[512,1024]{1,0:T(8,128)(2,1)S(1)}, bf16[512,1024]{1,0:T(8,128)(2,1)S(1)}, u32[]{:S(2)}, u32[]{:S(2)}) %collective-permute-start.18) | collective-permute-done | bytes 1048608 | tf_op jit(solution)/shard_map/ppermute | solution.py:299
  54.4 7.2 %shard_map.51 = bf16[512,1024]{1,0:T(8,128)(2,1)} custom-call(s32[2]{0:T(128)S(1)} %pad_add_fusion.side_ref, s32[8,128]{1,0:T(8,128)S(1)} %get-tuple-element.130.plan_ref, bf16[512,1024]{1,0:T(8,128)(2,1)S(1)} %bitcast.9, bf16[512,1024]{1,0:T(8,128)(2,1)S(1)} %collective-permute-done.18.theirs_ref, f32[1024,1024]{1,0:T(8,128)S(1)} %shard_map.50.gram_ref), custom_call_target="tpu_custom_call" | custom-call | flops 4294967296 | bytes 3145728 | tf_op jit(solution)/shard_map/pallas_call | solution.py:197
  61.6 5.6 %all-to-all-start.1 = ((bf16[64,8,1024]{2,1,0:T(8,128)(2,1)}), bf16[64,8,1024]{2,1,0:T(8,128)(2,1)S(1)}, u32[]{:S(2)}, u32[]{:S(2)}) async-start(bf16[64,8,1024]{2,1,0:T(8,128)(2,1)} %bitcast.6), calls=%async_computation.1 | async-start | bytes 2097152 | tf_op jit(solution)/shard_map/all_to_all | solution.py:301
  67.8 30.0 %all-to-all-done.1 = bf16[64,8,1024]{2,1,0:T(8,128)(2,1)S(1)} async-done(((bf16[64,8,1024]{2,1,0:T(8,128)(2,1)}), bf16[64,8,1024]{2,1,0:T(8,128)(2,1)S(1)}, u32[]{:S(2)}, u32[]{:S(2)}) %all-to-all-start.1) | async-done | bytes 1048608 | tf_op jit(solution)/shard_map/all_to_all | solution.py:301
  97.8 11.7 %conditional.1 = (bf16[128,8,1024]{2,1,0:T(8,128)(2,1)}) conditional(s32[]{:T(128)} %bitcast.4, (s32[2]{0:T(128)S(1)}, s32[8,128]{1,0:T(8,128)S(1)}, bf16[64,8,1024]{2,1,0:T(8,128)(2,1)S(1)}) %tuple.41, (s32[2]{0:T(128)S(1)}, s32[8,128]{1,0:T(8,128)S(1)}, bf16[64,8,1024]{2,1,0:T(8,128)(2,1)S(1)}) %tuple.41, ...), branch_computations={%region_0.1_spmd, %region_1.2_spmd, %region_2.3_spmd, %region_3.4_... | conditional | bytes 10485848 | solution.py:305
  97.8 2.4 %collective-permute-start.6 = (bf16[17,8,1024]{2,1,0:T(8,128)(2,1)S(1)}, bf16[17,8,1024]{2,1,0:T(8,128)(2,1)S(1)}, u32[]{:S(2)}, u32[]{:S(2)}) collective-permute-start(bf16[17,8,1024]{2,1,0:T(8,128)(2,1)S(1)} %slice.42), channel_id=1, source_target_pairs={{0,1},{1,2},{2,3},{3,0},{4,5},{5,6},{6,7},{7,4},{8,9},{9,10},{10,1... | collective-permute-start | bytes 835592 | tf_op jit(solution)/shard_map/cond/branch_6_fun/ppermute | solution.py:285
  100.2 3.4 %collective-permute-start.7 = (bf16[7,8,1024]{2,1,0:T(8,128)(2,1)S(1)}, bf16[7,8,1024]{2,1,0:T(8,128)(2,1)S(1)}, u32[]{:S(2)}, u32[]{:S(2)}) collective-permute-start(bf16[7,8,1024]{2,1,0:T(8,128)(2,1)S(1)} %slice.43), channel_id=1, source_target_pairs={{0,3},{1,0},{2,1},{3,2},{4,7},{5,4},{6,5},{7,6},{8,11},{9,8},{10,9... | collective-permute-start | bytes 344072 | tf_op jit(solution)/shard_map/cond/branch_6_fun/ppermute | solution.py:285
  103.7 2.1 %branch_6_fun.2.held_ref = bf16[128,8,1024]{2,1,0:T(8,128)(2,1)} custom-call(s32[2]{0:T(128)S(1)} %get-tuple-element.108.side_ref, s32[8,128]{1,0:T(8,128)S(1)} %get-tuple-element.109.plan_ref, bf16[64,8,1024]{2,1,0:T(8,128)(2,1)S(1)} %get-tuple-element.110.own_ref), custom_call_target="tpu_custom_call" | custom-call | bytes 2097152 | tf_op jit(solution)/shard_map/cond/branch_6_fun/pallas_call | solution.py:239
  105.7 2.4 %collective-permute-done.7.refs_1_ = bf16[7,8,1024]{2,1,0:T(8,128)(2,1)S(1)} collective-permute-done((bf16[7,8,1024]{2,1,0:T(8,128)(2,1)S(1)}, bf16[7,8,1024]{2,1,0:T(8,128)(2,1)S(1)}, u32[]{:S(2)}, u32[]{:S(2)}) %collective-permute-start.7) | collective-permute-done | bytes 114720 | tf_op jit(solution)/shard_map/cond/branch_6_fun/ppermute | solution.py:285
  108.1 0.0 collective-permute-done.6.refs_0_
  108.1 1.4 %branch_6_fun.3 = bf16[128,8,1024]{2,1,0:T(8,128)(2,1)} custom-call(s32[2]{0:T(128)S(1)} %get-tuple-element.108.side_ref, s32[8,128]{1,0:T(8,128)S(1)} %get-tuple-element.109.plan_ref, bf16[128,8,1024]{2,1,0:T(8,128)(2,1)} %branch_6_fun.2.held_ref, bf16[17,8,1024]{2,1,0:T(8,128)(2,1)S(1)} %collective-permute-done.6.refs_0_, ...), custom_call_target="tpu_custom_call", output_to_operand_aliasing={{}: (2, {})} | custom-call | bytes 786432 | tf_op jit(solution)/shard_map/cond/branch_6_fun/pallas_call | solution.py:267
  (2 shorter events, 0.0 us)
Async XLA Ops:
  49.9 4.5 %collective-permute-start.18 = (bf16[512,1024]{1,0:T(8,128)(2,1)S(1)}, bf16[512,1024]{1,0:T(8,128)(2,1)S(1)}, u32[]{:S(2)}, u32[]{:S(2)}) collective-permute-start(bf16[512,1024]{1,0:T(8,128)(2,1)S(1)} %bitcast.7), channel_id=1, source_target_pairs={{0,4},{4,0},{1,5},{5,1},{2,6},{6,2},{3,7},{7,3},{8,12},{12,8},{9,1... | collective-permute-start | bytes 3145736 | tf_op jit(solution)/shard_map/ppermute | solution.py:299
  61.6 36.2 %all-to-all-start.1 = ((bf16[64,8,1024]{2,1,0:T(8,128)(2,1)}), bf16[64,8,1024]{2,1,0:T(8,128)(2,1)S(1)}, u32[]{:S(2)}, u32[]{:S(2)}) async-start(bf16[64,8,1024]{2,1,0:T(8,128)(2,1)} %bitcast.6), calls=%async_computation.1 | async-start | bytes 2097152 | tf_op jit(solution)/shard_map/all_to_all | solution.py:301
  97.8 10.3 %collective-permute-start.6 = (bf16[17,8,1024]{2,1,0:T(8,128)(2,1)S(1)}, bf16[17,8,1024]{2,1,0:T(8,128)(2,1)S(1)}, u32[]{:S(2)}, u32[]{:S(2)}) collective-permute-start(bf16[17,8,1024]{2,1,0:T(8,128)(2,1)S(1)} %slice.42), channel_id=1, source_target_pairs={{0,1},{1,2},{2,3},{3,0},{4,5},{5,6},{6,7},{7,4},{8,9},{9,10},{10,1... | collective-permute-start | bytes 835592 | tf_op jit(solution)/shard_map/cond/branch_6_fun/ppermute | solution.py:285
  100.2 7.9 %collective-permute-start.7 = (bf16[7,8,1024]{2,1,0:T(8,128)(2,1)S(1)}, bf16[7,8,1024]{2,1,0:T(8,128)(2,1)S(1)}, u32[]{:S(2)}, u32[]{:S(2)}) collective-permute-start(bf16[7,8,1024]{2,1,0:T(8,128)(2,1)S(1)} %slice.43), channel_id=1, source_target_pairs={{0,3},{1,0},{2,1},{3,2},{4,7},{5,4},{6,5},{7,6},{8,11},{9,8},{10,9... | collective-permute-start | bytes 344072 | tf_op jit(solution)/shard_map/cond/branch_6_fun/ppermute | solution.py:285

commit v8 on v7

--- a/solution.py
+++ b/solution.py
@@ -97,10 +97,17 @@
     return lax.dot_general(a, b, (((0,), (0,)), ((), ())), preferred_element_type=jnp.float32)
 
 
-def gram_kernel(rows_ref, out_ref):
+def folded_squares(tile):
+    squares = tile * tile
+    folded = jnp.sum(squares.reshape(tile.shape[0] // 8, 8, tile.shape[1]), axis=0)
+    return sum(folded[:, c : c + 128] for c in range(0, tile.shape[1], 128))
+
+
+def gram_kernel(rows_ref, out_ref, squares_ref):
     width = rows_ref.shape[1]
     for j in range(0, width, TILE):
         out_ref[j:, j : j + TILE] = first_dims(rows_ref[:, j:], rows_ref[:, j : j + TILE])
+    squares_ref[...] = folded_squares(rows_ref[...].astype(jnp.float32))
 
 
 def gram(rows):
@@ -108,9 +115,12 @@
     vmem = pl.BlockSpec(memory_space=pltpu.VMEM)
     return pl.pallas_call(
         gram_kernel,
-        out_shape=jax.ShapeDtypeStruct((width, width), jnp.float32),
+        out_shape=(
+            jax.ShapeDtypeStruct((width, width), jnp.float32),
+            jax.ShapeDtypeStruct((8, 128), jnp.float32),
+        ),
         in_specs=[vmem],
-        out_specs=vmem,
+        out_specs=(vmem, vmem),
         compiler_params=pltpu.CompilerParams(vmem_limit_bytes=12 * 2**20),
         cost_estimate=pl.CostEstimate(
             flops=2 * count * width**2, bytes_accessed=2 * count * width + 4 * width**2, transcendentals=0
@@ -124,42 +134,34 @@
     return r == c
 
 
-def folded_squares(tile):
-    squares = tile * tile
-    folded = jnp.sum(squares.reshape(tile.shape[0] // 8, 8, tile.shape[1]), axis=0)
-    return sum(folded[:, c : c + 128] for c in range(0, tile.shape[1], 128))
-
-
-def refresh_kernel(
-    side_ref, plan_ref, mine_ref, theirs_ref, gram_ref, out_ref, right, root, square, rest, product
-):
+def refresh_kernel(side_ref, plan_ref, tier_ref, mine_ref, theirs_ref, gram_ref, squares_ref, out_ref, *scratch):
+    del tier_ref
+    root, square, rest, product = scratch
     rows, width = mine_ref.shape
     place, more = side_ref[1], plan_ref[MORE, 0]
     position = jnp.where(place < side_ref[0] * more, place, place + more)
     valid = jnp.where(position < plan_ref[COUNT, 0], 1.0, 0.0)
 
-    total_sq = jnp.zeros((1, 1), jnp.float32)
-    for j in range(0, width, TILE):
-        tile = gram_ref[j:, j : j + TILE] + first_dims(theirs_ref[:, j:], theirs_ref[:, j : j + TILE])
-        right[j:, j : j + TILE] = tile
-        top = tile[:TILE, :]
-        total_sq += jnp.sum(jnp.where(on_diagonal(top), top, 0.0), keepdims=True)
-
+    total_sq = squares_ref[...] + folded_squares(theirs_ref[...].astype(jnp.float32))
+    total_sq = jnp.sum(total_sq, keepdims=True)
     scale_c = total_sq / width + EPS
     quarter = lax.rsqrt(jnp.sqrt(scale_c)) * 0.25
     slope = quarter / scale_c
     diag = 5.0 * quarter - EPS * slope
+
     for j in range(0, width, TILE):
         cols = slice(j, j + TILE)
-        tile = -slope * right[cols, cols]
-        tile = jnp.where(on_diagonal(tile), diag + tile, tile)
-        kept = tile.astype(jnp.bfloat16)
+        tile = gram_ref[j:, cols] + first_dims(theirs_ref[:, j:], theirs_ref[:, cols])
+        tile = -slope * tile
+        top = tile[:TILE]
+        top = jnp.where(on_diagonal(top), diag + top, top)
+        kept = top.astype(jnp.bfloat16)
         root[cols, cols] = kept
         kept = kept.astype(jnp.float32)
-        off = jnp.where(on_diagonal(tile), 2.0 * (tile - kept) * kept, 0.0)
+        off = jnp.where(on_diagonal(top), 2.0 * (top - kept) * kept, 0.0)
         rest[:, cols] = jnp.sum(off, axis=0, keepdims=True)
         if j + TILE < width:
-            below = (-slope * right[j + TILE :, cols]).astype(jnp.bfloat16)
+            below = tile[TILE:].astype(jnp.bfloat16)
             root[j + TILE :, cols] = below
             root[cols, j + TILE :] = below.T
 
@@ -177,38 +179,37 @@
             square[cols, j + TILE :] = below.T
 
     squares = jnp.zeros((8, 128), jnp.float32)
-    for ref, keep in ((mine_ref, True), (theirs_ref, False)):
-        for j in range(0, width, TILE):
-            cols = slice(j, j + TILE)
+    for j in range(0, width, TILE):
+        cols = slice(j, j + TILE)
+        for ref in (mine_ref, theirs_ref):
             done = jnp.dot(ref[...], square[:, cols], preferred_element_type=jnp.float32)
             done = done + ref[:, cols].astype(jnp.float32) * rest[:, cols]
             squares += folded_squares(done)
-            if keep:
+            if ref is mine_ref:
                 product[:, cols] = done
     product_sq = jnp.sum(squares, keepdims=True)
     graft = jnp.sqrt((total_sq + EPS) / (product_sq + EPS)) * valid
     out_ref[...] = (product[...] * graft).astype(jnp.bfloat16)
 
 
-def refresh(side, plan, mine, theirs, mine_gram):
+def refresh(side, plan, tier, mine, theirs, mine_gram, mine_squares):
     rows, width = mine.shape
     vmem = pl.BlockSpec(memory_space=pltpu.VMEM)
     smem = pl.BlockSpec(memory_space=pltpu.SMEM)
     return pl.pallas_call(
         refresh_kernel,
         out_shape=jax.ShapeDtypeStruct((rows, width), jnp.bfloat16),
-        in_specs=[smem, smem, vmem, vmem, vmem],
+        in_specs=[smem, smem, smem, vmem, vmem, vmem, vmem],
         out_specs=vmem,
         scratch_shapes=[
-            pltpu.VMEM((width, width), jnp.float32),
             pltpu.VMEM((width, width), jnp.bfloat16),
             pltpu.VMEM((width, width), jnp.bfloat16),
             pltpu.VMEM((1, width), jnp.float32),
             pltpu.VMEM((rows, width), jnp.float32),
         ],
-        compiler_params=pltpu.CompilerParams(vmem_limit_bytes=24 * 2**20),
+        compiler_params=pltpu.CompilerParams(vmem_limit_bytes=14 * 2**20),
         cost_estimate=pl.CostEstimate(flops=4 * width**3, bytes_accessed=6 * rows * width, transcendentals=0),
-    )(side, plan, mine, theirs, mine_gram)
+    )(side, plan, tier, mine, theirs, mine_gram, mine_squares)
 
 
 def place_own_kernel(side_ref, plan_ref, own_ref, out_ref, whole, sems):
@@ -297,12 +298,13 @@
     mine = lax.all_to_all(outgoing, "yz", split_axis=0, concat_axis=0, tiled=True)
     mine = mine.reshape(chips * rows_dev, width)
     theirs = lax.ppermute(mine, "c", [(0, 1), (1, 0)])
-    done = refresh(side, plan, mine, theirs, gram(mine))
+    tier = lax.clamp(0, tier[0], len(HANDED) - 1)
+    done = refresh(side, plan, tier.reshape(1), mine, theirs, *gram(mine))
     own = lax.all_to_all(
         done.reshape(chips, rows_dev, width), "yz", split_axis=0, concat_axis=0, tiled=True
     )
     branches = [functools.partial(exchange, handed) for handed in HANDED]
-    return lax.switch(tier[0], branches, side, plan, own)
+    return lax.switch(tier, branches, side, plan, own)
 
 
 def solution(mesh):

time: 110 us -> 107 us (0.973)
  the two profiles are of different devices: /device:TPU:22 before, /device:TPU:16 now
where the time goes in v8:
time: 107 us
  blocking collectives  82.8 us (77%)
  Pallas kernels  13.3 us (12%)
  starting transfers between devices  5.31 us (5%)
  waiting for transfers between devices  4.37 us (4%)
    all_to_all x1, blocking collectives, body(): lax.all_to_all(outgoing, 'yz', split_axis=0, concat_axis=0, tiled=True)  46.8 us
    all_to_all x1, blocking collectives, body(): lax.all_to_all(done.reshape(chips, rows_dev, width), 'yz', split_axis=0,...  36 us
    pallas_call x1, Pallas kernels, refresh(): pl.pallas_call(refresh_kernel, out_shape=jax.ShapeDtypeStruct((rows, widt...  6.1 us
    ppermute x1, starting transfers between devices, exchange(): parts.append(lax.ppermute(own[start:start + size], 'x', pairs))  3.4 us
    ppermute x1, waiting for transfers between devices, exchange(): parts.append(lax.ppermute(own[start:start + size], 'x', pairs))  3.31 us
    pallas_call x1, Pallas kernels, make_plan(): pl.pallas_call(plan_kernel, out_shape=(pltpu.VMEM((places,) + grads.shape...  3 us
  transfers between devices with their start and end apart: 2, of which 2 were waited for; matrix products, arithmetic and copies ran while one was open for 0% of the time, Pallas kernels for 3%

profile of v8, /device:TPU:16, one launch (start us, length us, event | category | flops | bytes accessed | tf_op | source)
XLA Modules:
  0.0 106.9 jit_solution(17381819694979047809)
XLA Ops:
  0.0 0.1 pad_add_fusion.side_ref
  0.1 3.0 %shard_map.49 = (bf16[64,8,1024]{2,1,0:T(8,128)(2,1)S(1)}, s32[8,128]{1,0:T(8,128)S(1)}, s32[1]{0:T(128)}) custom-call(s32[2]{0:T(128)S(1)} %pad_add_fusion.side_ref, s32[1,128]{1,0:T(1,128)} %bitcast.11, s32[1,128]{1,0:T(1,128)} %bitcast.12, bf16[128,8,1024]{2,1,0:T(8,128)(2,1)} %grads_ref.1), custom_call_target="tpu_custom_call" | custom-call | tf_op jit(solution)/shard_map/pallas_call | solution.py:71
  3.1 46.8 %all_to_all.10 = bf16[64,8,1024]{2,1,0:T(8,128)(2,1)S(1)} all-to-all(bf16[64,8,1024]{2,1,0:T(8,128)(2,1)S(1)} %get-tuple-element.133), channel_id=1, replica_groups=mesh['yz'=64,'c'=2,'x'=4] {'yz'}, dimensions={0} | all-to-all | bytes 2097152 | tf_op jit(solution)/shard_map/all_to_all | solution.py:298
  49.9 1.9 %collective-permute-start.18 = (bf16[512,1024]{1,0:T(8,128)(2,1)S(1)}, bf16[512,1024]{1,0:T(8,128)(2,1)S(1)}, u32[]{:S(2)}, u32[]{:S(2)}) collective-permute-start(bf16[512,1024]{1,0:T(8,128)(2,1)S(1)} %bitcast.7), channel_id=1, source_target_pairs={{0,4},{4,0},{1,5},{5,1},{2,6},{6,2},{3,7},{7,3},{8,12},{12,8},{9,1... | collective-permute-start | bytes 3145736 | tf_op jit(solution)/shard_map/ppermute | solution.py:300
  52.4 0.9 shard_map.50
  53.3 1.1 collective-permute-done.18.theirs_ref
  54.4 6.1 %shard_map.51 = bf16[512,1024]{1,0:T(8,128)(2,1)S(1)} custom-call(s32[2]{0:T(128)S(1)} %pad_add_fusion.side_ref, s32[8,128]{1,0:T(8,128)S(1)} %get-tuple-element.132.plan_ref, s32[1]{0:T(128)} %clamp.7.tier_ref, bf16[512,1024]{1,0:T(8,128)(2,1)S(1)} %bitcast.9, bf16[512,1024]{1,0:T(8,128)(2,1)S(1)} %collective-permute-done.18.theirs_ref, ...), custom_call_target="tpu_custom_call" | custom-call | flops 4294967296 | bytes 3145728 | tf_op jit(solution)/shard_map/pallas_call | solution.py:199
  60.5 36.0 %all_to_all.11 = bf16[64,8,1024]{2,1,0:T(8,128)(2,1)S(1)} all-to-all(bf16[64,8,1024]{2,1,0:T(8,128)(2,1)S(1)} %bitcast.10), channel_id=1, replica_groups=mesh['yz'=64,'c'=2,'x'=4] {'yz'}, dimensions={0} | all-to-all | bytes 2097152 | tf_op jit(solution)/shard_map/all_to_all | solution.py:303
  96.5 10.3 %conditional.1 = (bf16[128,8,1024]{2,1,0:T(8,128)(2,1)}) conditional(s32[]{:T(128)} %bitcast.4, (s32[2]{0:T(128)S(1)}, s32[8,128]{1,0:T(8,128)S(1)}, bf16[64,8,1024]{2,1,0:T(8,128)(2,1)S(1)}) %tuple.41, (s32[2]{0:T(128)S(1)}, s32[8,128]{1,0:T(8,128)S(1)}, bf16[64,8,1024]{2,1,0:T(8,128)(2,1)S(1)}) %tuple.41, ...), branch_computations={%region_0.1_spmd, %region_1.2_spmd, %region_2.3_spmd, %region_3.4_... | conditional | bytes 10485848 | solution.py:307
  96.5 3.4 %collective-permute-start.2 = (bf16[12,8,1024]{2,1,0:T(8,128)(2,1)S(1)}, bf16[12,8,1024]{2,1,0:T(8,128)(2,1)S(1)}, u32[]{:S(2)}, u32[]{:S(2)}) collective-permute-start(bf16[12,8,1024]{2,1,0:T(8,128)(2,1)S(1)} %slice.38), channel_id=1, source_target_pairs={{0,1},{1,2},{2,3},{3,0},{4,5},{5,6},{6,7},{7,4},{8,9},{9,10},{10,1... | collective-permute-start | bytes 589832 | tf_op jit(solution)/shard_map/cond/branch_3_fun/ppermute | solution.py:286
  99.9 2.1 %branch_3_fun.2.held_ref = bf16[128,8,1024]{2,1,0:T(8,128)(2,1)} custom-call(s32[2]{0:T(128)S(1)} %get-tuple-element.98.side_ref, s32[8,128]{1,0:T(8,128)S(1)} %get-tuple-element.100.plan_ref, bf16[64,8,1024]{2,1,0:T(8,128)(2,1)S(1)} %get-tuple-element.101.own_ref), custom_call_target="tpu_custom_call" | custom-call | bytes 2097152 | tf_op jit(solution)/shard_map/cond/branch_3_fun/pallas_call | solution.py:240
  102.0 3.3 %collective-permute-done.2.refs_0_ = bf16[12,8,1024]{2,1,0:T(8,128)(2,1)S(1)} collective-permute-done((bf16[12,8,1024]{2,1,0:T(8,128)(2,1)S(1)}, bf16[12,8,1024]{2,1,0:T(8,128)(2,1)S(1)}, u32[]{:S(2)}, u32[]{:S(2)}) %collective-permute-start.2) | collective-permute-done | bytes 196640 | tf_op jit(solution)/shard_map/cond/branch_3_fun/ppermute | solution.py:286
  105.3 1.3 %branch_3_fun.3 = bf16[128,8,1024]{2,1,0:T(8,128)(2,1)} custom-call(s32[2]{0:T(128)S(1)} %get-tuple-element.98.side_ref, s32[8,128]{1,0:T(8,128)S(1)} %get-tuple-element.100.plan_ref, bf16[128,8,1024]{2,1,0:T(8,128)(2,1)} %branch_3_fun.2.held_ref, bf16[12,8,1024]{2,1,0:T(8,128)(2,1)S(1)} %collective-permute-done.2.refs_0_), custom_call_target="tpu_custom_call", output_to_operand_aliasing={{}: (2, {})} | custom-call | bytes 393216 | tf_op jit(solution)/shard_map/cond/branch_3_fun/pallas_call | solution.py:268
  (1 shorter events, 0.0 us)
Async XLA Ops:
  49.9 4.5 %collective-permute-start.18 = (bf16[512,1024]{1,0:T(8,128)(2,1)S(1)}, bf16[512,1024]{1,0:T(8,128)(2,1)S(1)}, u32[]{:S(2)}, u32[]{:S(2)}) collective-permute-start(bf16[512,1024]{1,0:T(8,128)(2,1)S(1)} %bitcast.7), channel_id=1, source_target_pairs={{0,4},{4,0},{1,5},{5,1},{2,6},{6,2},{3,7},{7,3},{8,12},{12,8},{9,1... | collective-permute-start | bytes 3145736 | tf_op jit(solution)/shard_map/ppermute | solution.py:300
  96.5 8.8 %collective-permute-start.2 = (bf16[12,8,1024]{2,1,0:T(8,128)(2,1)S(1)}, bf16[12,8,1024]{2,1,0:T(8,128)(2,1)S(1)}, u32[]{:S(2)}, u32[]{:S(2)}) collective-permute-start(bf16[12,8,1024]{2,1,0:T(8,128)(2,1)S(1)} %slice.38), channel_id=1, source_target_pairs={{0,1},{1,2},{2,3},{3,0},{4,5},{5,6},{6,7},{7,4},{8,9},{9,10},{10,1... | collective-permute-start | bytes 589832 | tf_op jit(solution)/shard_map/cond/branch_3_fun/ppermute | solution.py:286

commit v9 on v8

--- a/solution.py
+++ b/solution.py
@@ -10,10 +10,7 @@
 
 EPS = 1e-06
 TILE = 256
-HANDED = (
-    *((0, 0), (4, 0), (8, 0), (12, 0), (16, 0), (15, 5)),
-    *((17, 7), (19, 9), (21, 11), (25, 15), (29, 19), (37, 27)),
-)
+HANDED = (0, 4, 8, 12, 16, 20, 24, 28, 32, 40, 48, 64)
 BLOCK, RANK, TIER, MORE, COUNT = range(5)
 
 
@@ -46,9 +43,9 @@
     block = jnp.sum(jnp.where(down_columns(rank) == j, i, 0), axis=0, keepdims=True)
     tier, more = jnp.zeros_like(count), jnp.zeros_like(count)
     for smaller, larger in zip(HANDED, HANDED[1:]):
-        above = count > places + sum(smaller)
+        above = count > places + smaller
         tier = jnp.where(above, tier + 1, tier)
-        more = jnp.where(above, sum(larger), more)
+        more = jnp.where(above, larger, more)
     for index, row in ((BLOCK, block), (RANK, rank), (TIER, tier), (MORE, more), (COUNT, count)):
         rows_ref[index : index + 1, :] = row
     to_scalars = pltpu.make_async_copy(rows_ref, plan_ref, plan_sem)
@@ -248,45 +245,43 @@
     )(side, plan, own)
 
 
-def place_others_kernel(side_ref, plan_ref, held_ref, *refs):
-    parts, out_ref, sems = refs[:-2], refs[-2], refs[-1]
-    position = side_ref[0] * sum(part.shape[0] for part in parts)
-    for index, part in enumerate(parts):
-        for q in range(part.shape[0]):
-            target = out_ref.at[plan_ref[BLOCK, position + q]]
-            pltpu.make_async_copy(part.at[q], target, sems.at[index]).start()
-        position += part.shape[0]
-    for index, part in enumerate(parts):
-        pltpu.make_async_copy(part, part, sems.at[index]).wait()
-
-
-def place_others(side, plan, held, parts):
+def place_others_kernel(side_ref, plan_ref, held_ref, got_ref, out_ref, sem):
+    size = got_ref.shape[0]
+    first = side_ref[0] * size
+    for q in range(size):
+        target = out_ref.at[plan_ref[BLOCK, first + q]]
+        pltpu.make_async_copy(got_ref.at[q], target, sem).start()
+    pltpu.make_async_copy(got_ref, got_ref, sem).wait()
+
+
+def place_others(side, plan, held, got):
     smem = pl.BlockSpec(memory_space=pltpu.SMEM)
     vmem = pl.BlockSpec(memory_space=pltpu.VMEM)
     hbm = pl.BlockSpec(memory_space=pltpu.HBM)
-    size = sum(part.size for part in parts)
     return pl.pallas_call(
         place_others_kernel,
         out_shape=jax.ShapeDtypeStruct(held.shape, held.dtype),
-        in_specs=[smem, smem, hbm] + [vmem] * len(parts),
+        in_specs=[smem, smem, hbm, vmem],
         out_specs=hbm,
-        scratch_shapes=[pltpu.SemaphoreType.DMA((len(parts),))],
+        scratch_shapes=[pltpu.SemaphoreType.DMA],
         input_output_aliases={2: 0},
         compiler_params=pltpu.CompilerParams(vmem_limit_bytes=6 * 2**20),
-        cost_estimate=pl.CostEstimate(flops=0, bytes_accessed=4 * size, transcendentals=0),
-    )(side, plan, held, *parts)
+        cost_estimate=pl.CostEstimate(flops=0, bytes_accessed=4 * got.size, transcendentals=0),
+    )(side, plan, held, got)
 
 
 def exchange(handed, side, plan, own):
-    planes = lax.axis_size("x")
-    start, parts = 0, []
-    for size, step in zip(handed, (1, -1)):
-        if size:
-            pairs = [(i, (i + step) % planes) for i in range(planes)]
-            parts.append(lax.ppermute(own[start : start + size], "x", pairs))
-            start += size
+    if handed == 0:
+        return place_own(side, plan, own)
+    planes, cores = lax.axis_size("x"), lax.axis_size("c")
+    pairs = [
+        (core * planes + x, core * planes + (x + 1 - 2 * core) % planes)
+        for core in range(cores)
+        for x in range(planes)
+    ]
+    got = lax.ppermute(own[:handed], ("c", "x"), pairs)
     held = place_own(side, plan, own)
-    return place_others(side, plan, held, parts) if parts else held
+    return place_others(side, plan, held, got)
 
 
 def body(grads, owners, counts):

time: 107 us -> 108 us (level)
  no operation moved by 1% of the time
where the time goes in v9:
time: 108 us
  blocking collectives  82.8 us (77%)
  Pallas kernels  13.4 us (12%)
  starting transfers between devices  5.31 us (5%)
  waiting for transfers between devices  5.07 us (5%)
    all_to_all x1, blocking collectives, body(): lax.all_to_all(outgoing, 'yz', split_axis=0, concat_axis=0, tiled=True)  46.8 us
    all_to_all x1, blocking collectives, body(): lax.all_to_all(done.reshape(chips, rows_dev, width), 'yz', split_axis=0,...  36 us
    pallas_call x1, Pallas kernels, refresh(): pl.pallas_call(refresh_kernel, out_shape=jax.ShapeDtypeStruct((rows, widt...  6.1 us
    ppermute x1, waiting for transfers between devices, exchange(): got = lax.ppermute(own[:handed], ('c', 'x'), pairs)  4.01 us
    ppermute x1, starting transfers between devices, exchange(): got = lax.ppermute(own[:handed], ('c', 'x'), pairs)  3.4 us
    pallas_call x1, Pallas kernels, make_plan(): pl.pallas_call(plan_kernel, out_shape=(pltpu.VMEM((places,) + grads.shape...  3 us
  transfers between devices with their start and end apart: 2, of which 2 were waited for; matrix products, arithmetic and copies ran while one was open for 0% of the time, Pallas kernels for 3%

profile of v9, /device:TPU:16, one launch (start us, length us, event | category | flops | bytes accessed | tf_op | source)
XLA Modules:
  0.0 107.7 jit_solution(13140232772549931620)
XLA Ops:
  0.0 0.1 pad_add_fusion.side_ref
  0.1 3.0 %shard_map.49 = (bf16[64,8,1024]{2,1,0:T(8,128)(2,1)S(1)}, s32[8,128]{1,0:T(8,128)S(1)}, s32[1]{0:T(128)}) custom-call(s32[2]{0:T(128)S(1)} %pad_add_fusion.side_ref, s32[1,128]{1,0:T(1,128)} %bitcast.11, s32[1,128]{1,0:T(1,128)} %bitcast.12, bf16[128,8,1024]{2,1,0:T(8,128)(2,1)} %grads_ref.1), custom_call_target="tpu_custom_call" | custom-call | tf_op jit(solution)/shard_map/pallas_call | solution.py:68
  3.1 46.8 %all_to_all.10 = bf16[64,8,1024]{2,1,0:T(8,128)(2,1)S(1)} all-to-all(bf16[64,8,1024]{2,1,0:T(8,128)(2,1)S(1)} %get-tuple-element.133), channel_id=1, replica_groups=mesh['yz'=64,'c'=2,'x'=4] {'yz'}, dimensions={0} | all-to-all | bytes 2097152 | tf_op jit(solution)/shard_map/all_to_all | solution.py:293
  49.9 1.9 %collective-permute-start.11 = (bf16[512,1024]{1,0:T(8,128)(2,1)S(1)}, bf16[512,1024]{1,0:T(8,128)(2,1)S(1)}, u32[]{:S(2)}, u32[]{:S(2)}) collective-permute-start(bf16[512,1024]{1,0:T(8,128)(2,1)S(1)} %bitcast.7), channel_id=1, source_target_pairs={{0,4},{4,0},{1,5},{5,1},{2,6},{6,2},{3,7},{7,3},{8,12},{12,8},{9,1... | collective-permute-start | bytes 3145736 | tf_op jit(solution)/shard_map/ppermute | solution.py:295
  52.4 0.9 shard_map.50
  53.3 1.1 collective-permute-done.11.theirs_ref
  54.4 6.1 %shard_map.51 = bf16[512,1024]{1,0:T(8,128)(2,1)S(1)} custom-call(s32[2]{0:T(128)S(1)} %pad_add_fusion.side_ref, s32[8,128]{1,0:T(8,128)S(1)} %get-tuple-element.132.plan_ref, s32[1]{0:T(128)} %clamp.7.tier_ref, bf16[512,1024]{1,0:T(8,128)(2,1)S(1)} %bitcast.9, bf16[512,1024]{1,0:T(8,128)(2,1)S(1)} %collective-permute-done.11.theirs_ref, ...), custom_call_target="tpu_custom_call" | custom-call | flops 4294967296 | bytes 3145728 | tf_op jit(solution)/shard_map/pallas_call | solution.py:196
  60.5 36.0 %all_to_all.11 = bf16[64,8,1024]{2,1,0:T(8,128)(2,1)S(1)} all-to-all(bf16[64,8,1024]{2,1,0:T(8,128)(2,1)S(1)} %bitcast.10), channel_id=1, replica_groups=mesh['yz'=64,'c'=2,'x'=4] {'yz'}, dimensions={0} | all-to-all | bytes 2097152 | tf_op jit(solution)/shard_map/all_to_all | solution.py:298
  96.5 11.0 %conditional.1 = (bf16[128,8,1024]{2,1,0:T(8,128)(2,1)}) conditional(s32[]{:T(128)} %bitcast.4, (s32[2]{0:T(128)S(1)}, s32[8,128]{1,0:T(8,128)S(1)}, bf16[64,8,1024]{2,1,0:T(8,128)(2,1)S(1)}) %tuple.41, (s32[2]{0:T(128)S(1)}, s32[8,128]{1,0:T(8,128)S(1)}, bf16[64,8,1024]{2,1,0:T(8,128)(2,1)S(1)}) %tuple.41, ...), branch_computations={%region_0.1_spmd, %region_1.2_spmd, %region_2.3_spmd, %region_3.4_... | conditional | bytes 8388656 | solution.py:302
  96.5 3.4 %collective-permute-start.3 = (bf16[16,8,1024]{2,1,0:T(8,128)(2,1)S(1)}, bf16[16,8,1024]{2,1,0:T(8,128)(2,1)S(1)}, u32[]{:S(2)}, u32[]{:S(2)}) collective-permute-start(bf16[16,8,1024]{2,1,0:T(8,128)(2,1)S(1)} %slice.23), channel_id=1, source_target_pairs={{0,1},{1,2},{2,3},{3,0},{4,7},{5,4},{6,5},{7,6},{8,9},{9,10},{10,1... | collective-permute-start | bytes 786440 | tf_op jit(solution)/shard_map/cond/branch_4_fun/ppermute | solution.py:282
  99.9 2.1 %branch_4_fun.2.held_ref = bf16[128,8,1024]{2,1,0:T(8,128)(2,1)} custom-call(s32[2]{0:T(128)S(1)} %get-tuple-element.102.side_ref, s32[8,128]{1,0:T(8,128)S(1)} %get-tuple-element.103.plan_ref, bf16[64,8,1024]{2,1,0:T(8,128)(2,1)S(1)} %get-tuple-element.104.own_ref), custom_call_target="tpu_custom_call" | custom-call | bytes 2097152 | tf_op jit(solution)/shard_map/cond/branch_4_fun/pallas_call | solution.py:237
  102.0 4.0 %collective-permute-done.3.got_ref = bf16[16,8,1024]{2,1,0:T(8,128)(2,1)S(1)} collective-permute-done((bf16[16,8,1024]{2,1,0:T(8,128)(2,1)S(1)}, bf16[16,8,1024]{2,1,0:T(8,128)(2,1)S(1)}, u32[]{:S(2)}, u32[]{:S(2)}) %collective-permute-start.3) | collective-permute-done | bytes 262176 | tf_op jit(solution)/shard_map/cond/branch_4_fun/ppermute | solution.py:282
  106.0 1.3 %branch_4_fun.3 = bf16[128,8,1024]{2,1,0:T(8,128)(2,1)} custom-call(s32[2]{0:T(128)S(1)} %get-tuple-element.102.side_ref, s32[8,128]{1,0:T(8,128)S(1)} %get-tuple-element.103.plan_ref, bf16[128,8,1024]{2,1,0:T(8,128)(2,1)} %branch_4_fun.2.held_ref, bf16[16,8,1024]{2,1,0:T(8,128)(2,1)S(1)} %collective-permute-done.3.got_ref), custom_call_target="tpu_custom_call", output_to_operand_aliasing={{}: (2, {})} | custom-call | bytes 524288 | tf_op jit(solution)/shard_map/cond/branch_4_fun/pallas_call | solution.py:261
  (1 shorter events, 0.0 us)
Async XLA Ops:
  49.9 4.5 %collective-permute-start.11 = (bf16[512,1024]{1,0:T(8,128)(2,1)S(1)}, bf16[512,1024]{1,0:T(8,128)(2,1)S(1)}, u32[]{:S(2)}, u32[]{:S(2)}) collective-permute-start(bf16[512,1024]{1,0:T(8,128)(2,1)S(1)} %bitcast.7), channel_id=1, source_target_pairs={{0,4},{4,0},{1,5},{5,1},{2,6},{6,2},{3,7},{7,3},{8,12},{12,8},{9,1... | collective-permute-start | bytes 3145736 | tf_op jit(solution)/shard_map/ppermute | solution.py:295
  96.5 9.5 %collective-permute-start.3 = (bf16[16,8,1024]{2,1,0:T(8,128)(2,1)S(1)}, bf16[16,8,1024]{2,1,0:T(8,128)(2,1)S(1)}, u32[]{:S(2)}, u32[]{:S(2)}) collective-permute-start(bf16[16,8,1024]{2,1,0:T(8,128)(2,1)S(1)} %slice.23), channel_id=1, source_target_pairs={{0,1},{1,2},{2,3},{3,0},{4,7},{5,4},{6,5},{7,6},{8,9},{9,10},{10,1... | collective-permute-start | bytes 786440 | tf_op jit(solution)/shard_map/cond/branch_4_fun/ppermute | solution.py:282

commit v10 on v8

--- a/solution.py
+++ b/solution.py
@@ -11,8 +11,8 @@
 EPS = 1e-06
 TILE = 256
 HANDED = (
-    *((0, 0), (4, 0), (8, 0), (12, 0), (16, 0), (15, 5)),
-    *((17, 7), (19, 9), (21, 11), (25, 15), (29, 19), (37, 27)),
+    *((0, 0), (4, 0), (8, 0), (12, 0), (16, 0), (20, 0)),
+    *((18, 6), (20, 8), (22, 10), (26, 14), (30, 18), (38, 26)),
 )
 BLOCK, RANK, TIER, MORE, COUNT = range(5)
 
@@ -278,12 +278,16 @@
 
 
 def exchange(handed, side, plan, own):
-    planes = lax.axis_size("x")
+    planes, cores = lax.axis_size("x"), lax.axis_size("c")
     start, parts = 0, []
-    for size, step in zip(handed, (1, -1)):
+    for size, steps in zip(handed, ((1, -1), (-1, 1))):
         if size:
-            pairs = [(i, (i + step) % planes) for i in range(planes)]
-            parts.append(lax.ppermute(own[start : start + size], "x", pairs))
+            pairs = [
+                (core * planes + x, core * planes + (x + steps[core]) % planes)
+                for core in range(cores)
+                for x in range(planes)
+            ]
+            parts.append(lax.ppermute(own[start : start + size], ("c", "x"), pairs))
             start += size
     held = place_own(side, plan, own)
     return place_others(side, plan, held, parts) if parts else held

time: 107 us -> 108 us (level)
  no operation moved by 1% of the time
where the time goes in v10:
time: 108 us
  blocking collectives  82.8 us (77%)
  Pallas kernels  13.4 us (12%)
  starting transfers between devices  5.31 us (5%)
  waiting for transfers between devices  5.07 us (5%)
    all_to_all x1, blocking collectives, body(): lax.all_to_all(outgoing, 'yz', split_axis=0, concat_axis=0, tiled=True)  46.8 us
    all_to_all x1, blocking collectives, body(): lax.all_to_all(done.reshape(chips, rows_dev, width), 'yz', split_axis=0,...  36 us
    pallas_call x1, Pallas kernels, refresh(): pl.pallas_call(refresh_kernel, out_shape=jax.ShapeDtypeStruct((rows, widt...  6.1 us
    ppermute x1, waiting for transfers between devices, exchange(): parts.append(lax.ppermute(own[start:start + size], ('c', 'x'), pairs))  4.01 us
    ppermute x1, starting transfers between devices, exchange(): parts.append(lax.ppermute(own[start:start + size], ('c', 'x'), pairs))  3.4 us
    pallas_call x1, Pallas kernels, make_plan(): pl.pallas_call(plan_kernel, out_shape=(pltpu.VMEM((places,) + grads.shape...  3 us
  transfers between devices with their start and end apart: 2, of which 2 were waited for; matrix products, arithmetic and copies ran while one was open for 0% of the time, Pallas kernels for 3%

profile of v10, /device:TPU:16, one launch (start us, length us, event | category | flops | bytes accessed | tf_op | source)
XLA Modules:
  0.0 107.7 jit_solution(253684941786174578)
XLA Ops:
  0.0 0.1 pad_add_fusion.side_ref
  0.1 3.0 %shard_map.49 = (bf16[64,8,1024]{2,1,0:T(8,128)(2,1)S(1)}, s32[8,128]{1,0:T(8,128)S(1)}, s32[1]{0:T(128)}) custom-call(s32[2]{0:T(128)S(1)} %pad_add_fusion.side_ref, s32[1,128]{1,0:T(1,128)} %bitcast.11, s32[1,128]{1,0:T(1,128)} %bitcast.12, bf16[128,8,1024]{2,1,0:T(8,128)(2,1)} %grads_ref.1), custom_call_target="tpu_custom_call" | custom-call | tf_op jit(solution)/shard_map/pallas_call | solution.py:71
  3.1 46.8 %all_to_all.10 = bf16[64,8,1024]{2,1,0:T(8,128)(2,1)S(1)} all-to-all(bf16[64,8,1024]{2,1,0:T(8,128)(2,1)S(1)} %get-tuple-element.133), channel_id=1, replica_groups=mesh['yz'=64,'c'=2,'x'=4] {'yz'}, dimensions={0} | all-to-all | bytes 2097152 | tf_op jit(solution)/shard_map/all_to_all | solution.py:302
  49.9 1.9 %collective-permute-start.17 = (bf16[512,1024]{1,0:T(8,128)(2,1)S(1)}, bf16[512,1024]{1,0:T(8,128)(2,1)S(1)}, u32[]{:S(2)}, u32[]{:S(2)}) collective-permute-start(bf16[512,1024]{1,0:T(8,128)(2,1)S(1)} %bitcast.7), channel_id=1, source_target_pairs={{0,4},{4,0},{1,5},{5,1},{2,6},{6,2},{3,7},{7,3},{8,12},{12,8},{9,1... | collective-permute-start | bytes 3145736 | tf_op jit(solution)/shard_map/ppermute | solution.py:304
  52.4 0.9 shard_map.50
  53.3 1.1 collective-permute-done.17.theirs_ref
  54.4 6.1 %shard_map.51 = bf16[512,1024]{1,0:T(8,128)(2,1)S(1)} custom-call(s32[2]{0:T(128)S(1)} %pad_add_fusion.side_ref, s32[8,128]{1,0:T(8,128)S(1)} %get-tuple-element.132.plan_ref, s32[1]{0:T(128)} %clamp.7.tier_ref, bf16[512,1024]{1,0:T(8,128)(2,1)S(1)} %bitcast.9, bf16[512,1024]{1,0:T(8,128)(2,1)S(1)} %collective-permute-done.17.theirs_ref, ...), custom_call_target="tpu_custom_call" | custom-call | flops 4294967296 | bytes 3145728 | tf_op jit(solution)/shard_map/pallas_call | solution.py:199
  60.5 36.0 %all_to_all.11 = bf16[64,8,1024]{2,1,0:T(8,128)(2,1)S(1)} all-to-all(bf16[64,8,1024]{2,1,0:T(8,128)(2,1)S(1)} %bitcast.10), channel_id=1, replica_groups=mesh['yz'=64,'c'=2,'x'=4] {'yz'}, dimensions={0} | all-to-all | bytes 2097152 | tf_op jit(solution)/shard_map/all_to_all | solution.py:307
  96.5 11.0 %conditional.1 = (bf16[128,8,1024]{2,1,0:T(8,128)(2,1)}) conditional(s32[]{:T(128)} %bitcast.4, (s32[2]{0:T(128)S(1)}, s32[8,128]{1,0:T(8,128)S(1)}, bf16[64,8,1024]{2,1,0:T(8,128)(2,1)S(1)}) %tuple.41, (s32[2]{0:T(128)S(1)}, s32[8,128]{1,0:T(8,128)S(1)}, bf16[64,8,1024]{2,1,0:T(8,128)(2,1)S(1)}) %tuple.41, ...), branch_computations={%region_0.1_spmd, %region_1.2_spmd, %region_2.3_spmd, %region_3.4_... | conditional | bytes 10485848 | solution.py:311
  96.5 3.4 %collective-permute-start.3 = (bf16[16,8,1024]{2,1,0:T(8,128)(2,1)S(1)}, bf16[16,8,1024]{2,1,0:T(8,128)(2,1)S(1)}, u32[]{:S(2)}, u32[]{:S(2)}) collective-permute-start(bf16[16,8,1024]{2,1,0:T(8,128)(2,1)S(1)} %slice.37), channel_id=1, source_target_pairs={{0,1},{1,2},{2,3},{3,0},{4,7},{5,4},{6,5},{7,6},{8,9},{9,10},{10,1... | collective-permute-start | bytes 786440 | tf_op jit(solution)/shard_map/cond/branch_4_fun/ppermute | solution.py:290
  99.9 2.1 %branch_4_fun.2.held_ref = bf16[128,8,1024]{2,1,0:T(8,128)(2,1)} custom-call(s32[2]{0:T(128)S(1)} %get-tuple-element.102.side_ref, s32[8,128]{1,0:T(8,128)S(1)} %get-tuple-element.103.plan_ref, bf16[64,8,1024]{2,1,0:T(8,128)(2,1)S(1)} %get-tuple-element.104.own_ref), custom_call_target="tpu_custom_call" | custom-call | bytes 2097152 | tf_op jit(solution)/shard_map/cond/branch_4_fun/pallas_call | solution.py:240
  102.0 4.0 %collective-permute-done.3.refs_0_ = bf16[16,8,1024]{2,1,0:T(8,128)(2,1)S(1)} collective-permute-done((bf16[16,8,1024]{2,1,0:T(8,128)(2,1)S(1)}, bf16[16,8,1024]{2,1,0:T(8,128)(2,1)S(1)}, u32[]{:S(2)}, u32[]{:S(2)}) %collective-permute-start.3) | collective-permute-done | bytes 262176 | tf_op jit(solution)/shard_map/cond/branch_4_fun/ppermute | solution.py:290
  106.0 1.3 %branch_4_fun.3 = bf16[128,8,1024]{2,1,0:T(8,128)(2,1)} custom-call(s32[2]{0:T(128)S(1)} %get-tuple-element.102.side_ref, s32[8,128]{1,0:T(8,128)S(1)} %get-tuple-element.103.plan_ref, bf16[128,8,1024]{2,1,0:T(8,128)(2,1)} %branch_4_fun.2.held_ref, bf16[16,8,1024]{2,1,0:T(8,128)(2,1)S(1)} %collective-permute-done.3.refs_0_), custom_call_target="tpu_custom_call", output_to_operand_aliasing={{}: (2, {})} | custom-call | bytes 524288 | tf_op jit(solution)/shard_map/cond/branch_4_fun/pallas_call | solution.py:268
  (1 shorter events, 0.0 us)
Async XLA Ops:
  49.9 4.5 %collective-permute-start.17 = (bf16[512,1024]{1,0:T(8,128)(2,1)S(1)}, bf16[512,1024]{1,0:T(8,128)(2,1)S(1)}, u32[]{:S(2)}, u32[]{:S(2)}) collective-permute-start(bf16[512,1024]{1,0:T(8,128)(2,1)S(1)} %bitcast.7), channel_id=1, source_target_pairs={{0,4},{4,0},{1,5},{5,1},{2,6},{6,2},{3,7},{7,3},{8,12},{12,8},{9,1... | collective-permute-start | bytes 3145736 | tf_op jit(solution)/shard_map/ppermute | solution.py:304
  96.5 9.5 %collective-permute-start.3 = (bf16[16,8,1024]{2,1,0:T(8,128)(2,1)S(1)}, bf16[16,8,1024]{2,1,0:T(8,128)(2,1)S(1)}, u32[]{:S(2)}, u32[]{:S(2)}) collective-permute-start(bf16[16,8,1024]{2,1,0:T(8,128)(2,1)S(1)} %slice.37), channel_id=1, source_target_pairs={{0,1},{1,2},{2,3},{3,0},{4,7},{5,4},{6,5},{7,6},{8,9},{9,10},{10,1... | collective-permute-start | bytes 786440 | tf_op jit(solution)/shard_map/cond/branch_4_fun/ppermute | solution.py:290

commit v11 on v10

--- a/solution.py
+++ b/solution.py
@@ -11,8 +11,8 @@
 EPS = 1e-06
 TILE = 256
 HANDED = (
-    *((0, 0), (4, 0), (8, 0), (12, 0), (16, 0), (20, 0)),
-    *((18, 6), (20, 8), (22, 10), (26, 14), (30, 18), (38, 26)),
+    *((size, 0) for size in (0, 4, 8, 10, 12, 14, 16, 18, 20, 22, 24)),
+    *((19, 9), (21, 11), (25, 15), (29, 19), (37, 27)),
 )
 BLOCK, RANK, TIER, MORE, COUNT = range(5)
 
@@ -279,11 +279,12 @@
 
 def exchange(handed, side, plan, own):
     planes, cores = lax.axis_size("x"), lax.axis_size("c")
+    steps = ((1, 1), (-1, -1)) if handed[1] else ((1, -1), (0, 0))
     start, parts = 0, []
-    for size, steps in zip(handed, ((1, -1), (-1, 1))):
+    for size, step in zip(handed, steps):
         if size:
             pairs = [
-                (core * planes + x, core * planes + (x + steps[core]) % planes)
+                (core * planes + x, core * planes + (x + step[core]) % planes)
                 for core in range(cores)
                 for x in range(planes)
             ]

time: 108 us -> 109 us (level)
  the two profiles are of different devices: /device:TPU:16 before, /device:TPU:22 now
where the time goes in v11:
time: 109 us
  blocking collectives  82.7 us (76%)
  Pallas kernels  13.4 us (12%)
  starting transfers between devices  7.75 us (7%)
  waiting for transfers between devices  3.8 us (3%)
    all_to_all x1, blocking collectives, body(): lax.all_to_all(outgoing, 'yz', split_axis=0, concat_axis=0, tiled=True)  46.8 us
    all_to_all x1, blocking collectives, body(): lax.all_to_all(done.reshape(chips, rows_dev, width), 'yz', split_axis=0,...  36 us
    pallas_call x1, Pallas kernels, refresh(): pl.pallas_call(refresh_kernel, out_shape=jax.ShapeDtypeStruct((rows, widt...  6.1 us
    ppermute x2, starting transfers between devices, exchange(): parts.append(lax.ppermute(own[start:start + size], ('c', 'x'), pairs))  5.84 us
    pallas_call x1, Pallas kernels, make_plan(): pl.pallas_call(plan_kernel, out_shape=(pltpu.VMEM((places,) + grads.shape...  3 us
    ppermute x2, waiting for transfers between devices, exchange(): parts.append(lax.ppermute(own[start:start + size], ('c', 'x'), pairs))  2.74 us
  transfers between devices with their start and end apart: 3, of which 2 were waited for; matrix products, arithmetic and copies ran while one was open for 0% of the time, Pallas kernels for 3%

profile of v11, /device:TPU:22, one launch (start us, length us, event | category | flops | bytes accessed | tf_op | source)
XLA Modules:
  0.0 108.7 jit_solution(5810091889115592612)
XLA Ops:
  0.0 0.1 pad_add_fusion.side_ref
  0.1 3.0 %shard_map.53 = (bf16[64,8,1024]{2,1,0:T(8,128)(2,1)S(1)}, s32[8,128]{1,0:T(8,128)S(1)}, s32[1]{0:T(128)}) custom-call(s32[2]{0:T(128)S(1)} %pad_add_fusion.side_ref, s32[1,128]{1,0:T(1,128)} %bitcast.11, s32[1,128]{1,0:T(1,128)} %bitcast.12, bf16[128,8,1024]{2,1,0:T(8,128)(2,1)} %grads_ref.1), custom_call_target="tpu_custom_call" | custom-call | tf_op jit(solution)/shard_map/pallas_call | solution.py:71
  3.1 46.8 %all_to_all.10 = bf16[64,8,1024]{2,1,0:T(8,128)(2,1)S(1)} all-to-all(bf16[64,8,1024]{2,1,0:T(8,128)(2,1)S(1)} %get-tuple-element.173), channel_id=1, replica_groups=mesh['yz'=64,'c'=2,'x'=4] {'yz'}, dimensions={0} | all-to-all | bytes 2097152 | tf_op jit(solution)/shard_map/all_to_all | solution.py:303
  49.9 1.9 %collective-permute-start.20 = (bf16[512,1024]{1,0:T(8,128)(2,1)S(1)}, bf16[512,1024]{1,0:T(8,128)(2,1)S(1)}, u32[]{:S(2)}, u32[]{:S(2)}) collective-permute-start(bf16[512,1024]{1,0:T(8,128)(2,1)S(1)} %bitcast.7), channel_id=1, source_target_pairs={{0,4},{4,0},{1,5},{5,1},{2,6},{6,2},{3,7},{7,3},{8,12},{12,8},{9,1... | collective-permute-start | bytes 3145736 | tf_op jit(solution)/shard_map/ppermute | solution.py:305
  52.4 0.9 shard_map.54
  53.3 1.1 collective-permute-done.20.theirs_ref
  54.4 6.1 %shard_map.55 = bf16[512,1024]{1,0:T(8,128)(2,1)S(1)} custom-call(s32[2]{0:T(128)S(1)} %pad_add_fusion.side_ref, s32[8,128]{1,0:T(8,128)S(1)} %get-tuple-element.172.plan_ref, s32[1]{0:T(128)} %clamp.7.tier_ref, bf16[512,1024]{1,0:T(8,128)(2,1)S(1)} %bitcast.9, bf16[512,1024]{1,0:T(8,128)(2,1)S(1)} %collective-permute-done.20.theirs_ref, ...), custom_call_target="tpu_custom_call" | custom-call | flops 4294967296 | bytes 3145728 | tf_op jit(solution)/shard_map/pallas_call | solution.py:199
  60.5 36.0 %all_to_all.11 = bf16[64,8,1024]{2,1,0:T(8,128)(2,1)S(1)} all-to-all(bf16[64,8,1024]{2,1,0:T(8,128)(2,1)S(1)} %bitcast.10), channel_id=1, replica_groups=mesh['yz'=64,'c'=2,'x'=4] {'yz'}, dimensions={0} | all-to-all | bytes 2097152 | tf_op jit(solution)/shard_map/all_to_all | solution.py:308
  96.5 12.1 %conditional.1 = (bf16[128,8,1024]{2,1,0:T(8,128)(2,1)}) conditional(s32[]{:T(128)} %bitcast.4, (s32[2]{0:T(128)S(1)}, s32[8,128]{1,0:T(8,128)S(1)}, bf16[64,8,1024]{2,1,0:T(8,128)(2,1)S(1)}) %tuple.53, (s32[2]{0:T(128)S(1)}, s32[8,128]{1,0:T(8,128)S(1)}, bf16[64,8,1024]{2,1,0:T(8,128)(2,1)S(1)}) %tuple.53, ...), branch_computations={%region_0.1_spmd, %region_1.2_spmd, %region_2.3_spmd, %region_3.4_... | conditional | bytes 10485848 | solution.py:312
  96.5 2.4 %collective-permute-start.10 = (bf16[19,8,1024]{2,1,0:T(8,128)(2,1)S(1)}, bf16[19,8,1024]{2,1,0:T(8,128)(2,1)S(1)}, u32[]{:S(2)}, u32[]{:S(2)}) collective-permute-start(bf16[19,8,1024]{2,1,0:T(8,128)(2,1)S(1)} %slice.50), channel_id=1, source_target_pairs={{0,1},{1,2},{2,3},{3,0},{4,5},{5,6},{6,7},{7,4},{8,9},{9,10},{10,1... | collective-permute-start | bytes 933896 | tf_op jit(solution)/shard_map/cond/branch_11_fun/ppermute | solution.py:291
  98.9 3.4 %collective-permute-start.11 = (bf16[9,8,1024]{2,1,0:T(8,128)(2,1)S(1)}, bf16[9,8,1024]{2,1,0:T(8,128)(2,1)S(1)}, u32[]{:S(2)}, u32[]{:S(2)}) collective-permute-start(bf16[9,8,1024]{2,1,0:T(8,128)(2,1)S(1)} %slice.51), channel_id=1, source_target_pairs={{0,3},{1,0},{2,1},{3,2},{4,7},{5,4},{6,5},{7,6},{8,11},{9,8},{10,9... | collective-permute-start | bytes 442376 | tf_op jit(solution)/shard_map/cond/branch_11_fun/ppermute | solution.py:291
  102.4 2.1 %branch_11_fun.2.held_ref = bf16[128,8,1024]{2,1,0:T(8,128)(2,1)} custom-call(s32[2]{0:T(128)S(1)} %get-tuple-element.151.side_ref, s32[8,128]{1,0:T(8,128)S(1)} %get-tuple-element.152.plan_ref, bf16[64,8,1024]{2,1,0:T(8,128)(2,1)S(1)} %get-tuple-element.153.own_ref), custom_call_target="tpu_custom_call" | custom-call | bytes 2097152 | tf_op jit(solution)/shard_map/cond/branch_11_fun/pallas_call | solution.py:240
  104.5 2.7 %collective-permute-done.11.refs_1_ = bf16[9,8,1024]{2,1,0:T(8,128)(2,1)S(1)} collective-permute-done((bf16[9,8,1024]{2,1,0:T(8,128)(2,1)S(1)}, bf16[9,8,1024]{2,1,0:T(8,128)(2,1)S(1)}, u32[]{:S(2)}, u32[]{:S(2)}) %collective-permute-start.11) | collective-permute-done | bytes 147488 | tf_op jit(solution)/shard_map/cond/branch_11_fun/ppermute | solution.py:291
  107.2 0.0 collective-permute-done.10.refs_0_
  107.2 1.4 %branch_11_fun.3 = bf16[128,8,1024]{2,1,0:T(8,128)(2,1)} custom-call(s32[2]{0:T(128)S(1)} %get-tuple-element.151.side_ref, s32[8,128]{1,0:T(8,128)S(1)} %get-tuple-element.152.plan_ref, bf16[128,8,1024]{2,1,0:T(8,128)(2,1)} %branch_11_fun.2.held_ref, bf16[19,8,1024]{2,1,0:T(8,128)(2,1)S(1)} %collective-permute-done.10.refs_0_, ...), custom_call_target="tpu_custom_call", output_to_operand_aliasing={{}: (2, {})} | custom-call | bytes 917504 | tf_op jit(solution)/shard_map/cond/branch_11_fun/pallas_call | solution.py:268
  (2 shorter events, 0.0 us)
Async XLA Ops:
  49.9 4.5 %collective-permute-start.20 = (bf16[512,1024]{1,0:T(8,128)(2,1)S(1)}, bf16[512,1024]{1,0:T(8,128)(2,1)S(1)}, u32[]{:S(2)}, u32[]{:S(2)}) collective-permute-start(bf16[512,1024]{1,0:T(8,128)(2,1)S(1)} %bitcast.7), channel_id=1, source_target_pairs={{0,4},{4,0},{1,5},{5,1},{2,6},{6,2},{3,7},{7,3},{8,12},{12,8},{9,1... | collective-permute-start | bytes 3145736 | tf_op jit(solution)/shard_map/ppermute | solution.py:305
  96.5 10.7 %collective-permute-start.10 = (bf16[19,8,1024]{2,1,0:T(8,128)(2,1)S(1)}, bf16[19,8,1024]{2,1,0:T(8,128)(2,1)S(1)}, u32[]{:S(2)}, u32[]{:S(2)}) collective-permute-start(bf16[19,8,1024]{2,1,0:T(8,128)(2,1)S(1)} %slice.50), channel_id=1, source_target_pairs={{0,1},{1,2},{2,3},{3,0},{4,5},{5,6},{6,7},{7,4},{8,9},{9,10},{10,1... | collective-permute-start | bytes 933896 | tf_op jit(solution)/shard_map/cond/branch_11_fun/ppermute | solution.py:291
  98.9 8.2 %collective-permute-start.11 = (bf16[9,8,1024]{2,1,0:T(8,128)(2,1)S(1)}, bf16[9,8,1024]{2,1,0:T(8,128)(2,1)S(1)}, u32[]{:S(2)}, u32[]{:S(2)}) collective-permute-start(bf16[9,8,1024]{2,1,0:T(8,128)(2,1)S(1)} %slice.51), channel_id=1, source_target_pairs={{0,3},{1,0},{2,1},{3,2},{4,7},{5,4},{6,5},{7,6},{8,11},{9,8},{10,9... | collective-permute-start | bytes 442376 | tf_op jit(solution)/shard_map/cond/branch_11_fun/ppermute | solution.py:291

commit v12 on v11

--- a/solution.py
+++ b/solution.py
@@ -11,8 +11,8 @@
 EPS = 1e-06
 TILE = 256
 HANDED = (
-    *((size, 0) for size in (0, 4, 8, 10, 12, 14, 16, 18, 20, 22, 24)),
-    *((19, 9), (21, 11), (25, 15), (29, 19), (37, 27)),
+    *((size, 0) for size in (0, 4, 8, 10, 12, 14, 16, 18, 20)),
+    *((16, 6), (17, 7), (19, 9), (21, 11), (25, 15), (29, 19), (37, 27)),
 )
 BLOCK, RANK, TIER, MORE, COUNT = range(5)
 

time: 109 us -> 109 us (level)
  no operation moved by 1% of the time
where the time goes in v12:
time: 109 us
  blocking collectives  82.7 us (76%)
  Pallas kernels  13.4 us (12%)
  starting transfers between devices  7.75 us (7%)
  waiting for transfers between devices  3.8 us (3%)
    all_to_all x1, blocking collectives, body(): lax.all_to_all(outgoing, 'yz', split_axis=0, concat_axis=0, tiled=True)  46.8 us
    all_to_all x1, blocking collectives, body(): lax.all_to_all(done.reshape(chips, rows_dev, width), 'yz', split_axis=0,...  36 us
    pallas_call x1, Pallas kernels, refresh(): pl.pallas_call(refresh_kernel, out_shape=jax.ShapeDtypeStruct((rows, widt...  6.1 us
    ppermute x2, starting transfers between devices, exchange(): parts.append(lax.ppermute(own[start:start + size], ('c', 'x'), pairs))  5.84 us
    pallas_call x1, Pallas kernels, make_plan(): pl.pallas_call(plan_kernel, out_shape=(pltpu.VMEM((places,) + grads.shape...  3 us
    ppermute x2, waiting for transfers between devices, exchange(): parts.append(lax.ppermute(own[start:start + size], ('c', 'x'), pairs))  2.74 us
  transfers between devices with their start and end apart: 3, of which 2 were waited for; matrix products, arithmetic and copies ran while one was open for 0% of the time, Pallas kernels for 3%

profile of v12, /device:TPU:22, one launch (start us, length us, event | category | flops | bytes accessed | tf_op | source)
XLA Modules:
  0.0 108.7 jit_solution(3949784379106514911)
XLA Ops:
  0.0 0.1 pad_add_fusion.side_ref
  0.1 3.0 %shard_map.53 = (bf16[64,8,1024]{2,1,0:T(8,128)(2,1)S(1)}, s32[8,128]{1,0:T(8,128)S(1)}, s32[1]{0:T(128)}) custom-call(s32[2]{0:T(128)S(1)} %pad_add_fusion.side_ref, s32[1,128]{1,0:T(1,128)} %bitcast.11, s32[1,128]{1,0:T(1,128)} %bitcast.12, bf16[128,8,1024]{2,1,0:T(8,128)(2,1)} %grads_ref.1), custom_call_target="tpu_custom_call" | custom-call | tf_op jit(solution)/shard_map/pallas_call | solution.py:71
  3.1 46.8 %all_to_all.10 = bf16[64,8,1024]{2,1,0:T(8,128)(2,1)S(1)} all-to-all(bf16[64,8,1024]{2,1,0:T(8,128)(2,1)S(1)} %get-tuple-element.173), channel_id=1, replica_groups=mesh['yz'=64,'c'=2,'x'=4] {'yz'}, dimensions={0} | all-to-all | bytes 2097152 | tf_op jit(solution)/shard_map/all_to_all | solution.py:303
  49.9 1.9 %collective-permute-start.22 = (bf16[512,1024]{1,0:T(8,128)(2,1)S(1)}, bf16[512,1024]{1,0:T(8,128)(2,1)S(1)}, u32[]{:S(2)}, u32[]{:S(2)}) collective-permute-start(bf16[512,1024]{1,0:T(8,128)(2,1)S(1)} %bitcast.7), channel_id=1, source_target_pairs={{0,4},{4,0},{1,5},{5,1},{2,6},{6,2},{3,7},{7,3},{8,12},{12,8},{9,1... | collective-permute-start | bytes 3145736 | tf_op jit(solution)/shard_map/ppermute | solution.py:305
  52.4 0.9 shard_map.54
  53.3 1.1 collective-permute-done.22.theirs_ref
  54.4 6.1 %shard_map.55 = bf16[512,1024]{1,0:T(8,128)(2,1)S(1)} custom-call(s32[2]{0:T(128)S(1)} %pad_add_fusion.side_ref, s32[8,128]{1,0:T(8,128)S(1)} %get-tuple-element.172.plan_ref, s32[1]{0:T(128)} %clamp.7.tier_ref, bf16[512,1024]{1,0:T(8,128)(2,1)S(1)} %bitcast.9, bf16[512,1024]{1,0:T(8,128)(2,1)S(1)} %collective-permute-done.22.theirs_ref, ...), custom_call_target="tpu_custom_call" | custom-call | flops 4294967296 | bytes 3145728 | tf_op jit(solution)/shard_map/pallas_call | solution.py:199
  60.5 36.0 %all_to_all.11 = bf16[64,8,1024]{2,1,0:T(8,128)(2,1)S(1)} all-to-all(bf16[64,8,1024]{2,1,0:T(8,128)(2,1)S(1)} %bitcast.10), channel_id=1, replica_groups=mesh['yz'=64,'c'=2,'x'=4] {'yz'}, dimensions={0} | all-to-all | bytes 2097152 | tf_op jit(solution)/shard_map/all_to_all | solution.py:308
  96.5 12.1 %conditional.1 = (bf16[128,8,1024]{2,1,0:T(8,128)(2,1)}) conditional(s32[]{:T(128)} %bitcast.4, (s32[2]{0:T(128)S(1)}, s32[8,128]{1,0:T(8,128)S(1)}, bf16[64,8,1024]{2,1,0:T(8,128)(2,1)S(1)}) %tuple.53, (s32[2]{0:T(128)S(1)}, s32[8,128]{1,0:T(8,128)S(1)}, bf16[64,8,1024]{2,1,0:T(8,128)(2,1)S(1)}) %tuple.53, ...), branch_computations={%region_0.1_spmd, %region_1.2_spmd, %region_2.3_spmd, %region_3.4_... | conditional | bytes 10485848 | solution.py:312
  96.5 2.4 %collective-permute-start.12 = (bf16[19,8,1024]{2,1,0:T(8,128)(2,1)S(1)}, bf16[19,8,1024]{2,1,0:T(8,128)(2,1)S(1)}, u32[]{:S(2)}, u32[]{:S(2)}) collective-permute-start(bf16[19,8,1024]{2,1,0:T(8,128)(2,1)S(1)} %slice.56), channel_id=1, source_target_pairs={{0,1},{1,2},{2,3},{3,0},{4,5},{5,6},{6,7},{7,4},{8,9},{9,10},{10,1... | collective-permute-start | bytes 933896 | tf_op jit(solution)/shard_map/cond/branch_11_fun/ppermute | solution.py:291
  98.9 3.4 %collective-permute-start.13 = (bf16[9,8,1024]{2,1,0:T(8,128)(2,1)S(1)}, bf16[9,8,1024]{2,1,0:T(8,128)(2,1)S(1)}, u32[]{:S(2)}, u32[]{:S(2)}) collective-permute-start(bf16[9,8,1024]{2,1,0:T(8,128)(2,1)S(1)} %slice.57), channel_id=1, source_target_pairs={{0,3},{1,0},{2,1},{3,2},{4,7},{5,4},{6,5},{7,6},{8,11},{9,8},{10,9... | collective-permute-start | bytes 442376 | tf_op jit(solution)/shard_map/cond/branch_11_fun/ppermute | solution.py:291
  102.4 2.1 %branch_11_fun.2.held_ref = bf16[128,8,1024]{2,1,0:T(8,128)(2,1)} custom-call(s32[2]{0:T(128)S(1)} %get-tuple-element.151.side_ref, s32[8,128]{1,0:T(8,128)S(1)} %get-tuple-element.152.plan_ref, bf16[64,8,1024]{2,1,0:T(8,128)(2,1)S(1)} %get-tuple-element.153.own_ref), custom_call_target="tpu_custom_call" | custom-call | bytes 2097152 | tf_op jit(solution)/shard_map/cond/branch_11_fun/pallas_call | solution.py:240
  104.5 2.7 %collective-permute-done.13.refs_1_ = bf16[9,8,1024]{2,1,0:T(8,128)(2,1)S(1)} collective-permute-done((bf16[9,8,1024]{2,1,0:T(8,128)(2,1)S(1)}, bf16[9,8,1024]{2,1,0:T(8,128)(2,1)S(1)}, u32[]{:S(2)}, u32[]{:S(2)}) %collective-permute-start.13) | collective-permute-done | bytes 147488 | tf_op jit(solution)/shard_map/cond/branch_11_fun/ppermute | solution.py:291
  107.2 0.0 collective-permute-done.12.refs_0_
  107.2 1.4 %branch_11_fun.3 = bf16[128,8,1024]{2,1,0:T(8,128)(2,1)} custom-call(s32[2]{0:T(128)S(1)} %get-tuple-element.151.side_ref, s32[8,128]{1,0:T(8,128)S(1)} %get-tuple-element.152.plan_ref, bf16[128,8,1024]{2,1,0:T(8,128)(2,1)} %branch_11_fun.2.held_ref, bf16[19,8,1024]{2,1,0:T(8,128)(2,1)S(1)} %collective-permute-done.12.refs_0_, ...), custom_call_target="tpu_custom_call", output_to_operand_aliasing={{}: (2, {})} | custom-call | bytes 917504 | tf_op jit(solution)/shard_map/cond/branch_11_fun/pallas_call | solution.py:268
  (2 shorter events, 0.0 us)
Async XLA Ops:
  49.9 4.5 %collective-permute-start.22 = (bf16[512,1024]{1,0:T(8,128)(2,1)S(1)}, bf16[512,1024]{1,0:T(8,128)(2,1)S(1)}, u32[]{:S(2)}, u32[]{:S(2)}) collective-permute-start(bf16[512,1024]{1,0:T(8,128)(2,1)S(1)} %bitcast.7), channel_id=1, source_target_pairs={{0,4},{4,0},{1,5},{5,1},{2,6},{6,2},{3,7},{7,3},{8,12},{12,8},{9,1... | collective-permute-start | bytes 3145736 | tf_op jit(solution)/shard_map/ppermute | solution.py:305
  96.5 10.7 %collective-permute-start.12 = (bf16[19,8,1024]{2,1,0:T(8,128)(2,1)S(1)}, bf16[19,8,1024]{2,1,0:T(8,128)(2,1)S(1)}, u32[]{:S(2)}, u32[]{:S(2)}) collective-permute-start(bf16[19,8,1024]{2,1,0:T(8,128)(2,1)S(1)} %slice.56), channel_id=1, source_target_pairs={{0,1},{1,2},{2,3},{3,0},{4,5},{5,6},{6,7},{7,4},{8,9},{9,10},{10,1... | collective-permute-start | bytes 933896 | tf_op jit(solution)/shard_map/cond/branch_11_fun/ppermute | solution.py:291
  98.9 8.2 %collective-permute-start.13 = (bf16[9,8,1024]{2,1,0:T(8,128)(2,1)S(1)}, bf16[9,8,1024]{2,1,0:T(8,128)(2,1)S(1)}, u32[]{:S(2)}, u32[]{:S(2)}) collective-permute-start(bf16[9,8,1024]{2,1,0:T(8,128)(2,1)S(1)} %slice.57), channel_id=1, source_target_pairs={{0,3},{1,0},{2,1},{3,2},{4,7},{5,4},{6,5},{7,6},{8,11},{9,8},{10,9... | collective-permute-start | bytes 442376 | tf_op jit(solution)/shard_map/cond/branch_11_fun/ppermute | solution.py:291

commit v13 on v12

--- a/solution.py
+++ b/solution.py
@@ -136,7 +136,7 @@
 
 def refresh_kernel(side_ref, plan_ref, tier_ref, mine_ref, theirs_ref, gram_ref, squares_ref, out_ref, *scratch):
     del tier_ref
-    root, square, rest, product = scratch
+    root, square, rest, product, turned = scratch
     rows, width = mine_ref.shape
     place, more = side_ref[1], plan_ref[MORE, 0]
     position = jnp.where(place < side_ref[0] * more, place, place + more)
@@ -149,9 +149,10 @@
     slope = quarter / scale_c
     diag = 5.0 * quarter - EPS * slope
 
+    turned[...] = theirs_ref[...].T
     for j in range(0, width, TILE):
         cols = slice(j, j + TILE)
-        tile = gram_ref[j:, cols] + first_dims(theirs_ref[:, j:], theirs_ref[:, cols])
+        tile = gram_ref[j:, cols] + jnp.dot(turned[j:, :], theirs_ref[:, cols], preferred_element_type=jnp.float32)
         tile = -slope * tile
         top = tile[:TILE]
         top = jnp.where(on_diagonal(top), diag + top, top)
@@ -206,6 +207,7 @@
             pltpu.VMEM((width, width), jnp.bfloat16),
             pltpu.VMEM((1, width), jnp.float32),
             pltpu.VMEM((rows, width), jnp.float32),
+            pltpu.VMEM((width, rows), jnp.bfloat16),
         ],
         compiler_params=pltpu.CompilerParams(vmem_limit_bytes=14 * 2**20),
         cost_estimate=pl.CostEstimate(flops=4 * width**3, bytes_accessed=6 * rows * width, transcendentals=0),

time: 109 us -> 108 us (level)
  the two profiles are of different devices: /device:TPU:22 before, /device:TPU:16 now
where the time goes in v13:
time: 108 us
  blocking collectives  82.8 us (77%)
  Pallas kernels  13 us (12%)
  waiting for transfers between devices  5.77 us (5%)
  starting transfers between devices  5.31 us (5%)
    all_to_all x1, blocking collectives, body(): lax.all_to_all(outgoing, 'yz', split_axis=0, concat_axis=0, tiled=True)  46.8 us
    all_to_all x1, blocking collectives, body(): lax.all_to_all(done.reshape(chips, rows_dev, width), 'yz', split_axis=0,...  36 us
    pallas_call x1, Pallas kernels, refresh(): pl.pallas_call(refresh_kernel, out_shape=jax.ShapeDtypeStruct((rows, widt...  5.7 us
    ppermute x1, waiting for transfers between devices, exchange(): parts.append(lax.ppermute(own[start:start + size], ('c', 'x'), pairs))  4.71 us
    ppermute x1, starting transfers between devices, exchange(): parts.append(lax.ppermute(own[start:start + size], ('c', 'x'), pairs))  3.4 us
    pallas_call x1, Pallas kernels, make_plan(): pl.pallas_call(plan_kernel, out_shape=(pltpu.VMEM((places,) + grads.shape...  3 us
  transfers between devices with their start and end apart: 2, of which 2 were waited for; matrix products, arithmetic and copies ran while one was open for 0% of the time, Pallas kernels for 3%

profile of v13, /device:TPU:16, one launch (start us, length us, event | category | flops | bytes accessed | tf_op | source)
XLA Modules:
  0.0 107.8 jit_solution(13002722070483323590)
XLA Ops:
  0.0 0.1 pad_add_fusion.side_ref
  0.1 3.0 %shard_map.53 = (bf16[64,8,1024]{2,1,0:T(8,128)(2,1)S(1)}, s32[8,128]{1,0:T(8,128)S(1)}, s32[1]{0:T(128)}) custom-call(s32[2]{0:T(128)S(1)} %pad_add_fusion.side_ref, s32[1,128]{1,0:T(1,128)} %bitcast.11, s32[1,128]{1,0:T(1,128)} %bitcast.12, bf16[128,8,1024]{2,1,0:T(8,128)(2,1)} %grads_ref.1), custom_call_target="tpu_custom_call" | custom-call | tf_op jit(solution)/shard_map/pallas_call | solution.py:71
  3.1 46.8 %all_to_all.10 = bf16[64,8,1024]{2,1,0:T(8,128)(2,1)S(1)} all-to-all(bf16[64,8,1024]{2,1,0:T(8,128)(2,1)S(1)} %get-tuple-element.173), channel_id=1, replica_groups=mesh['yz'=64,'c'=2,'x'=4] {'yz'}, dimensions={0} | all-to-all | bytes 2097152 | tf_op jit(solution)/shard_map/all_to_all | solution.py:305
  49.9 1.9 %collective-permute-start.22 = (bf16[512,1024]{1,0:T(8,128)(2,1)S(1)}, bf16[512,1024]{1,0:T(8,128)(2,1)S(1)}, u32[]{:S(2)}, u32[]{:S(2)}) collective-permute-start(bf16[512,1024]{1,0:T(8,128)(2,1)S(1)} %bitcast.7), channel_id=1, source_target_pairs={{0,4},{4,0},{1,5},{5,1},{2,6},{6,2},{3,7},{7,3},{8,12},{12,8},{9,1... | collective-permute-start | bytes 3145736 | tf_op jit(solution)/shard_map/ppermute | solution.py:307
  52.4 0.9 shard_map.54
  53.3 1.1 collective-permute-done.22.theirs_ref
  54.4 5.7 %shard_map.55 = bf16[512,1024]{1,0:T(8,128)(2,1)S(1)} custom-call(s32[2]{0:T(128)S(1)} %pad_add_fusion.side_ref, s32[8,128]{1,0:T(8,128)S(1)} %get-tuple-element.172.plan_ref, s32[1]{0:T(128)} %clamp.7.tier_ref, bf16[512,1024]{1,0:T(8,128)(2,1)S(1)} %bitcast.9, bf16[512,1024]{1,0:T(8,128)(2,1)S(1)} %collective-permute-done.22.theirs_ref, ...), custom_call_target="tpu_custom_call" | custom-call | flops 4294967296 | bytes 3145728 | tf_op jit(solution)/shard_map/pallas_call | solution.py:200
  60.1 36.0 %all_to_all.11 = bf16[64,8,1024]{2,1,0:T(8,128)(2,1)S(1)} all-to-all(bf16[64,8,1024]{2,1,0:T(8,128)(2,1)S(1)} %bitcast.10), channel_id=1, replica_groups=mesh['yz'=64,'c'=2,'x'=4] {'yz'}, dimensions={0} | all-to-all | bytes 2097152 | tf_op jit(solution)/shard_map/all_to_all | solution.py:310
  96.1 11.6 %conditional.1 = (bf16[128,8,1024]{2,1,0:T(8,128)(2,1)}) conditional(s32[]{:T(128)} %bitcast.4, (s32[2]{0:T(128)S(1)}, s32[8,128]{1,0:T(8,128)S(1)}, bf16[64,8,1024]{2,1,0:T(8,128)(2,1)S(1)}) %tuple.53, (s32[2]{0:T(128)S(1)}, s32[8,128]{1,0:T(8,128)S(1)}, bf16[64,8,1024]{2,1,0:T(8,128)(2,1)S(1)}) %tuple.53, ...), branch_computations={%region_0.1_spmd, %region_1.2_spmd, %region_2.3_spmd, %region_3.4_... | conditional | bytes 10485848 | solution.py:314
  96.1 3.4 %collective-permute-start.7 = (bf16[20,8,1024]{2,1,0:T(8,128)(2,1)S(1)}, bf16[20,8,1024]{2,1,0:T(8,128)(2,1)S(1)}, u32[]{:S(2)}, u32[]{:S(2)}) collective-permute-start(bf16[20,8,1024]{2,1,0:T(8,128)(2,1)S(1)} %slice.51), channel_id=1, source_target_pairs={{0,1},{1,2},{2,3},{3,0},{4,7},{5,4},{6,5},{7,6},{8,9},{9,10},{10,1... | collective-permute-start | bytes 983048 | tf_op jit(solution)/shard_map/cond/branch_8_fun/ppermute | solution.py:293
  99.5 2.1 %branch_8_fun.2.held_ref = bf16[128,8,1024]{2,1,0:T(8,128)(2,1)} custom-call(s32[2]{0:T(128)S(1)} %get-tuple-element.142.side_ref, s32[8,128]{1,0:T(8,128)S(1)} %get-tuple-element.143.plan_ref, bf16[64,8,1024]{2,1,0:T(8,128)(2,1)S(1)} %get-tuple-element.144.own_ref), custom_call_target="tpu_custom_call" | custom-call | bytes 2097152 | tf_op jit(solution)/shard_map/cond/branch_8_fun/pallas_call | solution.py:242
  101.6 4.7 %collective-permute-done.7.refs_0_ = bf16[20,8,1024]{2,1,0:T(8,128)(2,1)S(1)} collective-permute-done((bf16[20,8,1024]{2,1,0:T(8,128)(2,1)S(1)}, bf16[20,8,1024]{2,1,0:T(8,128)(2,1)S(1)}, u32[]{:S(2)}, u32[]{:S(2)}) %collective-permute-start.7) | collective-permute-done | bytes 327712 | tf_op jit(solution)/shard_map/cond/branch_8_fun/ppermute | solution.py:293
  106.3 1.3 %branch_8_fun.3 = bf16[128,8,1024]{2,1,0:T(8,128)(2,1)} custom-call(s32[2]{0:T(128)S(1)} %get-tuple-element.142.side_ref, s32[8,128]{1,0:T(8,128)S(1)} %get-tuple-element.143.plan_ref, bf16[128,8,1024]{2,1,0:T(8,128)(2,1)} %branch_8_fun.2.held_ref, bf16[20,8,1024]{2,1,0:T(8,128)(2,1)S(1)} %collective-permute-done.7.refs_0_), custom_call_target="tpu_custom_call", output_to_operand_aliasing={{}: (2, {})} | custom-call | bytes 655360 | tf_op jit(solution)/shard_map/cond/branch_8_fun/pallas_call | solution.py:270
  (1 shorter events, 0.0 us)
Async XLA Ops:
  49.9 4.5 %collective-permute-start.22 = (bf16[512,1024]{1,0:T(8,128)(2,1)S(1)}, bf16[512,1024]{1,0:T(8,128)(2,1)S(1)}, u32[]{:S(2)}, u32[]{:S(2)}) collective-permute-start(bf16[512,1024]{1,0:T(8,128)(2,1)S(1)} %bitcast.7), channel_id=1, source_target_pairs={{0,4},{4,0},{1,5},{5,1},{2,6},{6,2},{3,7},{7,3},{8,12},{12,8},{9,1... | collective-permute-start | bytes 3145736 | tf_op jit(solution)/shard_map/ppermute | solution.py:307
  96.1 10.2 %collective-permute-start.7 = (bf16[20,8,1024]{2,1,0:T(8,128)(2,1)S(1)}, bf16[20,8,1024]{2,1,0:T(8,128)(2,1)S(1)}, u32[]{:S(2)}, u32[]{:S(2)}) collective-permute-start(bf16[20,8,1024]{2,1,0:T(8,128)(2,1)S(1)} %slice.51), channel_id=1, source_target_pairs={{0,1},{1,2},{2,3},{3,0},{4,7},{5,4},{6,5},{7,6},{8,9},{9,10},{10,1... | collective-permute-start | bytes 983048 | tf_op jit(solution)/shard_map/cond/branch_8_fun/ppermute | solution.py:293
